TPU v7x, 32 devices: a whole 2x2x4 slice. The times are simulated.
32 devices in a mesh: groups: 2 (over x), seq: 16 (over z, y, core).
Axes of the slice: x: 2, y: 2, z: 4, core: 2. Of those that a mesh axis runs over, the one named last changes fastest.
Arguments:
- queries: bfloat16 [6, 16, 16, 2560], P('groups', 'seq'), parts along dimension 0, may hold values from -6 to 6
- keys: bfloat16 [6, 16, 16, 2560], P('groups', 'seq'), parts along dimension 0, may hold values from -6 to 6
- values: bfloat16 [6, 16, 16, 2560], P('groups', 'seq'), parts along dimension 0, may hold values from -6 to 6
- stream: bfloat16 [6, 16, 16, 2560], P('groups', 'seq'), parts along dimension 0, may hold values from -3 to 3
- head_weight: bfloat16 [2560, 64], replicated, may hold values from -0.125 to 0.125
- conv_in_weight: bfloat16 [3, 3, 3, 16, 384], replicated, may hold values from -0.3125 to 0.3125
- norm_gain: float32 [384], replicated, may hold values from 0.5 to 1.5
- norm_shift: float32 [384], replicated, may hold values from -3 to 3
- conv_mid_weight: bfloat16 [3, 3, 3, 384, 384], replicated, may hold values from -0.0625 to 0.0625
Outputs:
- decoded: bfloat16 [6, 32, 32, 384], P('groups', 'seq'), parts along dimension 0
There are 2 independent parts, one for each index of `groups`. A program takes and returns all parts, laid end to end along the dimension named above; an argument that names none is the same for every part. Nothing has to cross between parts.
All inputs are finite; a program needn't handle non-finite values.
Results may differ from a plain program's by a relative error of at most 0.01.
Values may be sent and summed in bfloat16 or wider, within the bound.
No kernel may reach another device: no remote copies, remote signals or barrier semaphores. Data moves between devices by JAX's collectives and lax.ppermute only.
A program may use at most 128 MiB of HBM per device.

v0:
```python
import jax
import jax.numpy as jnp
from jax import lax
from jax.sharding import PartitionSpec as P

HEADS = 20
GROUPS = 32


def swapped(value, axis, distance):
    mask = 2**distance
    pairs = [(source, source ^ mask) for source in range(lax.axis_size(axis))]
    return lax.ppermute(value, axis, pairs)


def from_behind(value, axis, steps):
    count = lax.axis_size(axis)
    pairs = [(source, (source + steps) % count) for source in range(count)]
    return lax.ppermute(value, axis, pairs)


def with_halo(cells, sides, width):
    for axis, dim in sides:
        count = lax.axis_size(axis)
        ends = count - 1
        head = lax.slice_in_dim(cells, 0, width, axis=dim)
        tail = lax.slice_in_dim(cells, cells.shape[dim] - width, cells.shape[dim], axis=dim)
        cells = jnp.concatenate(
            [
                lax.ppermute(tail, axis, [(i, (i + 1) % count) for i in range(ends)]),
                cells,
                lax.ppermute(head, axis, [((i + 1) % count, i) for i in range(ends)]),
            ],
            axis=dim,
        )
    return cells


def conv_taps(padded, weight, frames, rows, cols):
    inner = padded.shape[-1]
    total = jnp.zeros((frames * rows * cols, weight.shape[-1]), jnp.float32)
    for step_t in range(3):
        for step_h in range(3):
            for step_w in range(3):
                piece = padded[
                    step_t : step_t + frames, step_h : step_h + rows, step_w : step_w + cols, :
                ].reshape(-1, inner)
                total = total + jnp.dot(
                    piece, weight[step_t, step_h, step_w], preferred_element_type=jnp.float32
                )
    return total.reshape(frames, rows, cols, -1)


def pad_local(field):
    return jnp.pad(field, ((2, 0), (0, 0), (1, 1), (0, 0)))


def group_stats(first):
    grouped = first.reshape(first.shape[0], first.shape[1], first.shape[2], GROUPS, -1)
    counted = grouped.size // GROUPS * lax.axis_size("seq")
    sums = lax.psum(jnp.sum(grouped, axis=(0, 1, 2, 4)), "seq")
    mean = sums / counted
    centered = grouped - mean[:, None]
    spread = lax.psum(jnp.sum(centered * centered, axis=(0, 1, 2, 4)), "seq")
    variance = spread / counted
    return (mean, variance)


def normalize(field, mean, variance, norm_gain, norm_shift):
    grouped = field.reshape(field.shape[0], field.shape[1], field.shape[2], GROUPS, -1)
    normed = ((grouped - mean[:, None]) / jnp.sqrt(variance + 1e-06)[:, None]).reshape(field.shape)
    return jax.nn.silu(normed * norm_gain + norm_shift)


def start_carry(heads_count, row_count, head_depth):
    return (
        jnp.full((heads_count, row_count), -1e30, jnp.float32),
        jnp.zeros((heads_count, row_count), jnp.float32),
        jnp.zeros((heads_count, row_count, head_depth), jnp.float32),
    )


def fold_block(carry, query_flat, key_flat, value_flat, scale):
    run_max, run_sum, run_acc = carry
    scores = (
        jnp.einsum("qhd,khd->hqk", query_flat, key_flat, preferred_element_type=jnp.float32) * scale
    )
    new_max = jnp.maximum(run_max, jnp.max(scores, axis=-1))
    decay = jnp.exp(run_max - new_max)
    expo = jnp.exp(scores - new_max[..., None])
    run_sum = run_sum * decay + jnp.sum(expo, axis=-1)
    added = jnp.einsum(
        "hqk,khd->hqd", expo.astype(jnp.bfloat16), value_flat, preferred_element_type=jnp.float32
    )
    run_acc = run_acc * decay[..., None] + added
    return (new_max, run_sum, run_acc)


def butterfly_step(stacked, own_bit, split_axis, stack_axis, swapper, bit):
    retained = lax.dynamic_index_in_dim(stacked, own_bit, split_axis, keepdims=False)
    outgoing = lax.dynamic_index_in_dim(stacked, 1 - own_bit, split_axis, keepdims=False)
    incoming = swapper(outgoing, bit)
    lower_half = jnp.where(own_bit == 0, retained, incoming)
    upper_half = jnp.where(own_bit == 0, incoming, retained)
    return jnp.stack([lower_half, upper_half], axis=stack_axis)


def shards(
    queries,
    keys,
    values,
    stream,
    head_weight,
    conv_in_weight,
    norm_gain,
    norm_shift,
    conv_mid_weight,
):
    frames, rows_here, cols, width = queries.shape
    depth = width // HEADS
    token_count = frames * rows_here * cols
    scale = 1.0 / depth**0.5
    heads_here = HEADS // 4
    group_width = width // 4
    position = lax.axis_index("seq")
    low_bit = position % 2
    high_bit = position // 2 % 2

    def head_swap(travelling, bit):
        return swapped(travelling, "seq", bit)

    def back_swap(travelling, bit):
        return swapped(travelling, "seq", bit)

    stacked = jnp.stack([queries, keys, values]).reshape(3, token_count, 2, 2, group_width)
    stacked = butterfly_step(stacked, low_bit, 3, 1, head_swap, 0)
    stacked = butterfly_step(stacked, high_bit, 3, 1, head_swap, 1)
    query_local = stacked[0].reshape(4 * token_count, heads_here, depth)
    key_value = stacked[1:].reshape(2, 4 * token_count, group_width)
    carry = fold_block(
        start_carry(heads_here, 4 * token_count, depth),
        query_local,
        key_value[0].reshape(-1, heads_here, depth),
        key_value[1].reshape(-1, heads_here, depth),
        scale,
    )

    def cycle_turn(turn_index, state):
        carry_now, travelling = state
        travelling = from_behind(travelling, "seq", 4)
        carry_now = fold_block(
            carry_now,
            query_local,
            travelling[0].reshape(-1, heads_here, depth),
            travelling[1].reshape(-1, heads_here, depth),
            scale,
        )
        return (carry_now, travelling)

    carry = lax.fori_loop(0, lax.axis_size("seq") // 4 - 1, cycle_turn, (carry, key_value))[0]
    run_max, run_sum, run_acc = carry
    local_out = (run_acc / run_sum[..., None]).astype(jnp.bfloat16)
    local_out = jnp.transpose(local_out, (1, 0, 2)).reshape(2, 2, token_count, group_width)
    local_out = butterfly_step(local_out, high_bit, 0, 2, back_swap, 1)
    local_out = butterfly_step(local_out, low_bit, 0, 2, back_swap, 0)
    attended = local_out.reshape(token_count, width)
    latent = jnp.dot(
        stream.reshape(token_count, width), head_weight, preferred_element_type=jnp.float32
    ) + jnp.dot(attended, head_weight, preferred_element_type=jnp.float32)
    latent = latent.reshape(frames, rows_here, cols, 2, 2, -1).transpose(0, 1, 3, 2, 4, 5)
    latent = latent.reshape(frames, 2 * rows_here, 2 * cols, -1).astype(jnp.bfloat16)
    rows, wide = (2 * rows_here, 2 * cols)
    rimmed = with_halo(latent, (("seq", 1),), 1)
    first = conv_taps(pad_local(rimmed), conv_in_weight, frames, rows, wide)
    mean, variance = group_stats(first)
    active = normalize(first, mean, variance, norm_gain, norm_shift).astype(jnp.bfloat16)
    active_rimmed = with_halo(active, (("seq", 1),), 1)
    second = conv_taps(pad_local(active_rimmed), conv_mid_weight, frames, rows, wide)
    return (first + second).astype(jnp.bfloat16)


def solution(mesh):
    placed = (
        P("groups", "seq", None, None),
        P("groups", "seq", None, None),
        P("groups", "seq", None, None),
        P("groups", "seq", None, None),
        P(),
        P(),
        P(),
        P(),
        P(),
    )
    return jax.shard_map(
        shards,
        mesh=mesh,
        in_specs=placed,
        out_specs=P("groups", "seq", None, None),
        check_vma=False,
    )
```

profile of v0, /device:TPU:0, one launch (start us, length us, event | category | flops | bytes accessed | tf_op | source)
XLA Modules:
  0.0 169.5 jit_solution(1733586858377465636)
XLA Ops:
  0.0 1.1 stack.48
  1.2 1.0 stack.49
  2.2 1.0 stack.50
  3.7 1.5 constant_dynamic-slice_fusion.1
  5.8 1.3 collective-permute-done.1
  7.4 3.0 %collective-permute-start.2 = (bf16[3,2,48,640]{3,2,1,0:T(8,128)(2,1)S(1)}, bf16[3,2,48,640]{3,2,1,0:T(8,128)(2,1)S(1)}, u32[]{:S(2)}, u32[]{:S(2)}) collective-permute-start(bf16[3,2,48,640]{3,2,1,0:T(8,128)(2,1)S(1)} %bitcast.412), channel_id=1, source_target_pairs={{0,2},{1,3},{2,0},{3,1},{4,6},{5,7},{6,4},{7,5},{8,10},{9,11},{10,... | collective-permute-start | bytes 1105928 | tf_op jit(solution)/shard_map/ppermute | solution.py:13
  10.3 8.9 %collective-permute-done.2 = bf16[3,2,48,640]{3,2,1,0:T(8,128)(2,1)S(1)} collective-permute-done((bf16[3,2,48,640]{3,2,1,0:T(8,128)(2,1)S(1)}, bf16[3,2,48,640]{3,2,1,0:T(8,128)(2,1)S(1)}, u32[]{:S(2)}, u32[]{:S(2)}) %collective-permute-start.2) | collective-permute-done | bytes 368672 | tf_op jit(solution)/shard_map/ppermute | solution.py:13
  21.4 45.8 %while.16 = (s32[]{:T(128)}, f32[5,192]{1,0:T(8,128)S(1)}, f32[5,192]{1,0:T(8,128)S(1)}, f32[5,192,128]{2,1,0:T(8,128)S(1)}, bf16[2,192,640]{2,1,0:T(8,128)(2,1)...) while((s32[]{:T(128)}, f32[5,192]{1,0:T(8,128)S(1)}, f32[5,192]{1,0:T(8,128)S(1)}, ...), condition=%wide.region_5.6_spmd, body=%wide.region_2.5_spmd.sunk | while | flops 95725440 | bytes 8908917 | solution.py:160
  21.4 1.8 %collective-permute-start = (bf16[2,192,640]{2,1,0:T(8,128)(2,1)S(1)}, bf16[2,192,640]{2,1,0:T(8,128)(2,1)S(1)}, u32[]{:S(2)}, u32[]{:S(2)}) collective-permute-start(bf16[2,192,640]{2,1,0:T(8,128)(2,1)S(1)} %get-tuple-element.213), channel_id=1, source_target_pairs={{0,4},{1,5},{2,6},{3,7},{4,8},{5,9},{6,10},{7,11},{8,12},{9,13},{1... | collective-permute-start | bytes 1474568 | tf_op jit(solution)/shard_map/while/body/eval_jaxpr/ppermute | solution.py:19
  23.2 12.8 %collective-permute-done = bf16[2,192,640]{2,1,0:T(8,128)(2,1)S(1)} collective-permute-done((bf16[2,192,640]{2,1,0:T(8,128)(2,1)S(1)}, bf16[2,192,640]{2,1,0:T(8,128)(2,1)S(1)}, u32[]{:S(2)}, u32[]{:S(2)}) %collective-permute-start) | collective-permute-done | bytes 491552 | tf_op jit(solution)/shard_map/while/body/eval_jaxpr/ppermute | solution.py:19
  37.6 13.6 %collective-permute-done = bf16[2,192,640]{2,1,0:T(8,128)(2,1)S(1)} collective-permute-done((bf16[2,192,640]{2,1,0:T(8,128)(2,1)S(1)}, bf16[2,192,640]{2,1,0:T(8,128)(2,1)S(1)}, u32[]{:S(2)}, u32[]{:S(2)}) %collective-permute-start) | collective-permute-done | bytes 491552 | tf_op jit(solution)/shard_map/while/body/eval_jaxpr/ppermute | solution.py:19
  52.9 12.7 %collective-permute-done = bf16[2,192,640]{2,1,0:T(8,128)(2,1)S(1)} collective-permute-done((bf16[2,192,640]{2,1,0:T(8,128)(2,1)S(1)}, bf16[2,192,640]{2,1,0:T(8,128)(2,1)S(1)}, u32[]{:S(2)}, u32[]{:S(2)}) %collective-permute-start) | collective-permute-done | bytes 491552 | tf_op jit(solution)/shard_map/while/body/eval_jaxpr/ppermute | solution.py:19
  68.0 1.0 collective-permute-start.3
  69.0 4.0 %collective-permute-done.3 = bf16[2,48,640]{2,1,0:T(8,128)(2,1)S(1)} collective-permute-done((bf16[2,48,640]{2,1,0:T(8,128)(2,1)S(1)}, bf16[2,48,640]{2,1,0:T(8,128)(2,1)S(1)}, u32[]{:S(2)}, u32[]{:S(2)}) %collective-permute-start.3) | collective-permute-done | bytes 122912 | tf_op jit(solution)/shard_map/ppermute | solution.py:13
  73.3 1.1 collective-permute-done.4
  75.2 2.1 %collective-permute-start.5 = (bf16[3,1,32,16]{3,2,1,0:T(8,128)(2,1)S(1)}, bf16[3,1,32,16]{3,2,1,0:T(8,128)(2,1)S(1)}, u32[]{:S(2)}, u32[]{:S(2)}) collective-permute-start(bf16[3,1,32,16]{3,2,1,0:T(8,128)(2,1)S(1)} %get-tuple-element.145), channel_id=1, source_target_pairs={{0,1},{1,2},{2,3},{3,4},{4,5},{5,6},{6,7},{7,8},{8,9},{9,10},{10,1... | collective-permute-start | bytes 9224 | tf_op jit(solution)/shard_map/ppermute | solution.py:30
  77.3 1.3 collective-permute-start.6
  78.6 2.2 %collective-permute-done.6 = bf16[3,1,32,16]{3,2,1,0:T(8,128)(2,1)S(1)} collective-permute-done((bf16[3,1,32,16]{3,2,1,0:T(8,128)(2,1)S(1)}, bf16[3,1,32,16]{3,2,1,0:T(8,128)(2,1)S(1)}, u32[]{:S(2)}, u32[]{:S(2)}) %collective-permute-start.6) | collective-permute-done | bytes 3104 | tf_op jit(solution)/shard_map/ppermute | solution.py:32
  85.9 32.0 %psum.14 = f32[32]{0:T(128)S(1)} all-reduce(f32[32]{0:T(128)S(1)} %reduce_sum.53), channel_id=1, replica_groups=mesh['groups'=2,'seq'=16] {'seq'}, use_global_device_ids=true, to_apply=%region_8.9 | all-reduce | flops 32 | bytes 256 | tf_op jit(solution)/shard_map/psum | solution.py:61
  118.4 29.5 %psum.15 = f32[32]{0:T(128)S(1)} all-reduce(f32[32]{0:T(128)S(1)} %reduce_sum.56), channel_id=1, replica_groups=mesh['groups'=2,'seq'=16] {'seq'}, use_global_device_ids=true, to_apply=%region_11.12 | all-reduce | flops 32 | bytes 256 | tf_op jit(solution)/shard_map/psum | solution.py:64
  148.2 2.0 %collective-permute-start.7 = (bf16[3,1,32,384]{3,2,1,0:T(8,128)(2,1)S(1)}, bf16[3,1,32,384]{3,2,1,0:T(8,128)(2,1)S(1)}, u32[]{:S(2)}, u32[]{:S(2)}) collective-permute-start(bf16[3,1,32,384]{3,2,1,0:T(8,128)(2,1)S(1)} %get-tuple-element.141), channel_id=1, source_target_pairs={{0,1},{1,2},{2,3},{3,4},{4,5},{5,6},{6,7},{7,8},{8,9},{9,10},{10,1... | collective-permute-start | bytes 221192 | tf_op jit(solution)/shard_map/ppermute | solution.py:30
  150.3 1.5 collective-permute-start.8
  151.8 1.7 collective-permute-done.8
  154.1 1.4 fusion.62
  155.6 1.2 fusion.41
  156.8 1.2 convolution_add_fusion.25
  158.0 1.2 convolution_add_fusion.24
  159.2 1.2 convolution_add_fusion.23
  160.4 1.2 convolution_add_fusion.22
  161.6 1.2 convolution_add_fusion.21
  162.8 1.2 convolution_add_fusion.20
  168.8 0.7 add_convert_fusion
  (153 shorter events, 20.8 us)
Async XLA Ops:
  0.0 73.1 %copy-start = (bf16[2560,64]{0,1:T(8,128)(2,1)S(1)}, bf16[2560,64]{0,1:T(8,128)(2,1)}, u32[]{:S(2)}) copy-start(bf16[2560,64]{0,1:T(8,128)(2,1)} %param.15) | copy-start | bytes 983044
  5.3 1.8 %collective-permute-start.1 = (bf16[3,48,2,640]{3,1,2,0:T(8,128)(2,1)S(1)}, bf16[3,48,2,640]{3,1,2,0:T(8,128)(2,1)S(1)}, u32[]{:S(2)}, u32[]{:S(2)}) collective-permute-start(bf16[3,48,2,640]{3,1,2,0:T(8,128)(2,1)S(1)} %bitcast.411), channel_id=1, source_target_pairs={{0,1},{1,0},{2,3},{3,2},{4,5},{5,4},{6,7},{7,6},{8,9},{9,8},{10,11... | collective-permute-start | bytes 1105928 | tf_op jit(solution)/shard_map/ppermute | solution.py:13
  7.4 11.9 %collective-permute-start.2 = (bf16[3,2,48,640]{3,2,1,0:T(8,128)(2,1)S(1)}, bf16[3,2,48,640]{3,2,1,0:T(8,128)(2,1)S(1)}, u32[]{:S(2)}, u32[]{:S(2)}) collective-permute-start(bf16[3,2,48,640]{3,2,1,0:T(8,128)(2,1)S(1)} %bitcast.412), channel_id=1, source_target_pairs={{0,2},{1,3},{2,0},{3,1},{4,6},{5,7},{6,4},{7,5},{8,10},{9,11},{10,... | collective-permute-start | bytes 1105928 | tf_op jit(solution)/shard_map/ppermute | solution.py:13
  21.4 51.7 %copy-start.2 = (bf16[3,1,16,2560]{3,2,1,0:T(8,128)(2,1)S(1)}, bf16[3,1,16,2560]{3,2,1,0:T(8,128)(2,1)}, u32[]{:S(2)}) copy-start(bf16[3,1,16,2560]{3,2,1,0:T(8,128)(2,1)} %param.14) | copy-start | bytes 737284
  21.4 14.6 %collective-permute-start = (bf16[2,192,640]{2,1,0:T(8,128)(2,1)S(1)}, bf16[2,192,640]{2,1,0:T(8,128)(2,1)S(1)}, u32[]{:S(2)}, u32[]{:S(2)}) collective-permute-start(bf16[2,192,640]{2,1,0:T(8,128)(2,1)S(1)} %get-tuple-element.213), channel_id=1, source_target_pairs={{0,4},{1,5},{2,6},{3,7},{4,8},{5,9},{6,10},{7,11},{8,12},{9,13},{1... | collective-permute-start | bytes 1474568 | tf_op jit(solution)/shard_map/while/body/eval_jaxpr/ppermute | solution.py:19
  37.6 13.7 %collective-permute-start = (bf16[2,192,640]{2,1,0:T(8,128)(2,1)S(1)}, bf16[2,192,640]{2,1,0:T(8,128)(2,1)S(1)}, u32[]{:S(2)}, u32[]{:S(2)}) collective-permute-start(bf16[2,192,640]{2,1,0:T(8,128)(2,1)S(1)} %get-tuple-element.213), channel_id=1, source_target_pairs={{0,4},{1,5},{2,6},{3,7},{4,8},{5,9},{6,10},{7,11},{8,12},{9,13},{1... | collective-permute-start | bytes 1474568 | tf_op jit(solution)/shard_map/while/body/eval_jaxpr/ppermute | solution.py:19
  52.9 12.8 %collective-permute-start = (bf16[2,192,640]{2,1,0:T(8,128)(2,1)S(1)}, bf16[2,192,640]{2,1,0:T(8,128)(2,1)S(1)}, u32[]{:S(2)}, u32[]{:S(2)}) collective-permute-start(bf16[2,192,640]{2,1,0:T(8,128)(2,1)S(1)} %get-tuple-element.213), channel_id=1, source_target_pairs={{0,4},{1,5},{2,6},{3,7},{4,8},{5,9},{6,10},{7,11},{8,12},{9,13},{1... | collective-permute-start | bytes 1474568 | tf_op jit(solution)/shard_map/while/body/eval_jaxpr/ppermute | solution.py:19
  67.2 13.8 %copy-start.1 = (bf16[3,3,3,16,384]{4,3,2,1,0:T(8,128)(2,1)S(1)}, bf16[3,3,3,16,384]{4,3,2,1,0:T(8,128)(2,1)}, u32[]{:S(2)}) copy-start(bf16[3,3,3,16,384]{4,3,2,1,0:T(8,128)(2,1)} %param.16) | copy-start | bytes 995332
  68.0 4.9 %collective-permute-start.3 = (bf16[2,48,640]{2,1,0:T(8,128)(2,1)S(1)}, bf16[2,48,640]{2,1,0:T(8,128)(2,1)S(1)}, u32[]{:S(2)}, u32[]{:S(2)}) collective-permute-start(bf16[2,48,640]{2,1,0:T(8,128)(2,1)S(1)} %dynamic-slice_bitcast_fusion), channel_id=1, source_target_pairs={{0,2},{1,3},{2,0},{3,1},{4,6},{5,7},{6,4},{7,5},{8,10},{9,11},{10,... | collective-permute-start | bytes 368648 | tf_op jit(solution)/shard_map/ppermute | solution.py:13
  73.0 1.4 collective-permute-start.4
  75.2 3.4 %collective-permute-start.5 = (bf16[3,1,32,16]{3,2,1,0:T(8,128)(2,1)S(1)}, bf16[3,1,32,16]{3,2,1,0:T(8,128)(2,1)S(1)}, u32[]{:S(2)}, u32[]{:S(2)}) collective-permute-start(bf16[3,1,32,16]{3,2,1,0:T(8,128)(2,1)S(1)} %get-tuple-element.145), channel_id=1, source_target_pairs={{0,1},{1,2},{2,3},{3,4},{4,5},{5,6},{6,7},{7,8},{8,9},{9,10},{10,1... | collective-permute-start | bytes 9224 | tf_op jit(solution)/shard_map/ppermute | solution.py:30
  77.3 3.5 %collective-permute-start.6 = (bf16[3,1,32,16]{3,2,1,0:T(8,128)(2,1)S(1)}, bf16[3,1,32,16]{3,2,1,0:T(8,128)(2,1)S(1)}, u32[]{:S(2)}, u32[]{:S(2)}) collective-permute-start(bf16[3,1,32,16]{3,2,1,0:T(8,128)(2,1)S(1)} %get-tuple-element.146), channel_id=1, source_target_pairs={{1,0},{2,1},{3,2},{4,3},{5,4},{6,5},{7,6},{8,7},{9,8},{10,9},{11,1... | collective-permute-start | bytes 9224 | tf_op jit(solution)/shard_map/ppermute | solution.py:32
  81.9 66.2 %copy-start.3 = (f32[384]{0:T(512)S(1)}, f32[384]{0:T(512)}, u32[]{:S(2)}) copy-start(f32[384]{0:T(512)} %param.18) | copy-start | bytes 4612
  81.9 66.2 %copy-start.4 = (f32[384]{0:T(512)S(1)}, f32[384]{0:T(512)}, u32[]{:S(2)}) copy-start(f32[384]{0:T(512)} %param.17) | copy-start | bytes 4612
  148.2 15.8 %slice-start = ((s8[7962624]{0:T(1024)(128)(4,1)}), s8[4194304]{0:T(1024)(128)(4,1)S(1)}, s32[]{:S(2)}) async-start(s8[7962624]{0:T(1024)(128)(4,1)} %bitcast.375), calls=%async_computation | async-start | bytes 8388608
  148.2 3.5 %collective-permute-start.7 = (bf16[3,1,32,384]{3,2,1,0:T(8,128)(2,1)S(1)}, bf16[3,1,32,384]{3,2,1,0:T(8,128)(2,1)S(1)}, u32[]{:S(2)}, u32[]{:S(2)}) collective-permute-start(bf16[3,1,32,384]{3,2,1,0:T(8,128)(2,1)S(1)} %get-tuple-element.141), channel_id=1, source_target_pairs={{0,1},{1,2},{2,3},{3,4},{4,5},{5,6},{6,7},{7,8},{8,9},{9,10},{10,1... | collective-permute-start | bytes 221192 | tf_op jit(solution)/shard_map/ppermute | solution.py:30
  150.3 3.2 %collective-permute-start.8 = (bf16[3,1,32,384]{3,2,1,0:T(8,128)(2,1)S(1)}, bf16[3,1,32,384]{3,2,1,0:T(8,128)(2,1)S(1)}, u32[]{:S(2)}, u32[]{:S(2)}) collective-permute-start(bf16[3,1,32,384]{3,2,1,0:T(8,128)(2,1)S(1)} %get-tuple-element.142), channel_id=1, source_target_pairs={{1,0},{2,1},{3,2},{4,3},{5,4},{6,5},{7,6},{8,7},{9,8},{10,9},{11,1... | collective-permute-start | bytes 221192 | tf_op jit(solution)/shard_map/ppermute | solution.py:32
  153.7 10.3 %slice-start.1 = ((s8[7962624]{0:T(1024)(128)(4,1)}), s8[3768320]{0:T(1024)(128)(4,1)S(1)}, s32[]{:S(2)}) async-start(s8[7962624]{0:T(1024)(128)(4,1)} %bitcast.375), calls=%async_computation.1 | async-start | bytes 7536640
where the time goes:
time: 172 us; the launch traced here: 169 us
  blocking collectives  61.5 us (36%)
  waiting for transfers between devices  58.2 us (34%)
  matrix products  22.5 us (13%)
  starting transfers between devices  13.4 us (8%)
  local copies, waits for them, and re-layouts  9.88 us (6%)
  other arithmetic  2.81 us (2%)
    ppermute x3, waiting for transfers between devices, from_behind(): return lax.ppermute(value, axis, pairs)  39.1 us
    psum x1, blocking collectives, group_stats(): sums = lax.psum(jnp.sum(grouped, axis=(0, 1, 2, 4)), 'seq')  32 us
    psum x1, blocking collectives, group_stats(): spread = lax.psum(jnp.sum(centered * centered, axis=(0, 1, 2, 4)), 'seq')  29.5 us
    dot_general x54, matrix products, conv_taps(): jnp.dot(piece, weight[step_t, step_h, step_w], preferred_element_type=jnp...  18.7 us
    ppermute x4, waiting for transfers between devices, swapped(): return lax.ppermute(value, axis, pairs)  15.3 us
    ppermute x4, starting transfers between devices, swapped(): return lax.ppermute(value, axis, pairs)  4.54 us
    ppermute x2, starting transfers between devices, with_halo(): lax.ppermute(tail, axis, [(i, (i + 1) % count) for i in range(ends)])  4.09 us
    ppermute x2, waiting for transfers between devices, with_halo(): lax.ppermute(head, axis, [((i + 1) % count, i) for i in range(ends)])  3.84 us
  transfers between devices with their start and end apart: 11, of which 9 were waited for; matrix products, arithmetic and copies ran while one was open for 0% of the time, Pallas kernels for 0%

commit v1 on v0

v1 whole, which is shorter than its diff:
```python
import functools

import jax
import jax.numpy as jnp
from jax import lax
from jax.experimental import pallas as pl
from jax.experimental.pallas import tpu as pltpu
from jax.sharding import PartitionSpec as P

HEADS = 20
GROUPS = 32
SPLIT = 4
EPS = 1e-06

VMEM = pl.BlockSpec(memory_space=pltpu.VMEM)
SMEM = pl.BlockSpec(memory_space=pltpu.SMEM)
ANY = pl.BlockSpec(memory_space=pl.ANY)


def exchanged(value, mask):
    pairs = [(source, source ^ mask) for source in range(lax.axis_size("seq"))]
    return lax.ppermute(value, "seq", pairs)


def rest_mask(member):
    return (member & 3) | ((member >> 2) << 4)


def dot(left, right):
    return jnp.dot(left, right, preferred_element_type=jnp.float32)


def prepare_kernel(depth, heads, index, q, k, v, s, w, *refs):
    kv_out, q_out, stream_out, projected = refs[:SPLIT], refs[SPLIT : 2 * SPLIT], refs[-2], refs[-1]
    tokens = q.shape[0]
    group = heads * depth
    place = (index[0] >> 2) & 3
    twice = jnp.concatenate([w[...], w[...]], axis=1)
    low = lax.broadcasted_iota(jnp.int32, (tokens, 2 * w.shape[1]), 1) < w.shape[1]

    def through(head):
        return dot(v[:, head * depth : (head + 1) * depth], twice[head * depth : (head + 1) * depth])

    wide = twice.shape[1]
    for owner in range(SPLIT):
        for pair in range((heads + 1) // 2):
            first = owner * heads + 2 * pair
            both = through(first)
            if 2 * pair + 1 < heads:
                both = jnp.where(low, both, through(first + 1))
            projected[owner, :, pair * wide : (pair + 1) * wide] = both.astype(jnp.bfloat16)
    for step in range(SPLIT):
        owner = place ^ step
        columns = pl.ds(pl.multiple_of(owner * group, 128), group)
        kv_out[step][:, :group] = k[:, columns]
        kv_out[step][:, group:] = projected[owner]
        q_out[step][...] = q[:, columns]
    stream_out[...] = dot(s[...], twice)


def attend_kernel(depth, heads, *refs):
    q, kv, stream, out = refs[:SPLIT], refs[SPLIT:-2], refs[-2], refs[-1]
    tokens = q[0].shape[0]
    wide = stream.shape[1]
    factor = 1.4426950408889634 / depth**0.5
    rows = SPLIT * tokens
    low = lax.broadcasted_iota(jnp.int32, (rows, wide), 1) < wide // 2
    total_out = jnp.zeros((rows, wide), jnp.float32)
    for head in range(heads):
        columns = slice(head * depth, (head + 1) * depth)
        query = jnp.concatenate([piece[:, columns] for piece in q], axis=0)
        key = jnp.concatenate([piece[:, columns] for piece in kv], axis=0)
        at = heads * depth + (head // 2) * wide
        value = jnp.concatenate([piece[:, at : at + wide] for piece in kv], axis=0)
        scores = lax.dot_general(query, key, (((1,), (1,)), ((), ())), preferred_element_type=jnp.float32)
        top = jnp.max(scores, axis=1, keepdims=True)
        expo = jnp.exp2((scores - top) * factor)
        total = jnp.sum(expo, axis=1, keepdims=True)
        mixed = dot(expo.astype(jnp.bfloat16), value) * (1.0 / total)
        mine = low if head % 2 == 0 else jnp.logical_not(low)
        total_out = total_out + jnp.where(mine, mixed, 0.0)
    total_out = total_out + pltpu.roll(total_out, wide // 2, 1)
    half = rows // 2
    upper = total_out[:half]
    upper = jnp.concatenate([upper[:tokens] + stream[...], upper[tokens:]], axis=0)
    out[...] = jnp.where(low[:half], upper, total_out[half:])


def gather_kernel(cols, own, one, two, three, chosen, out):
    rows, wide = own.shape
    half = rows // 2

    def swap_rows(x):
        return jnp.concatenate([x[half:], x[:half]], axis=0)

    far = two[...] + swap_rows(three[...])
    latent = (own[...] + swap_rows(one[...])) + pltpu.roll(far, wide // 2, 1)
    latent = latent.astype(jnp.bfloat16).astype(jnp.float32)
    column = lax.broadcasted_iota(jnp.int32, (rows, wide), 0) % cols
    before = jnp.where(column == 0, 0.0, pltpu.roll(latent, 1, 0))
    after = jnp.where(column == cols - 1, 0.0, pltpu.roll(latent, rows - 1, 0))
    row = jnp.concatenate([before, latent, after], axis=1).astype(jnp.bfloat16)
    out[...] = dot(row, chosen[...]).astype(jnp.bfloat16)


def finish_kernel(frames, n, cols, index, *refs):
    members = n // SPLIT
    patches, refs = refs[:members], refs[members:]
    (in_weight, mid_weight, grouped, gain, shift, out, grid, stacked, first, taps, held, merged, sem) = refs
    channels = gain.shape[1]
    wide = grid.shape[-1]
    half = wide // 2
    me = index[0]
    copies = [
        pltpu.make_async_copy(mid_weight.at[a], held.at[a], sem.at[a]) for a in range(mid_weight.shape[0])
    ]
    for copy in copies:
        copy.start()

    grid[:, 0] = jnp.zeros((frames, cols, wide), jnp.bfloat16)
    grid[:, n + 1] = jnp.zeros((frames, cols, wide), jnp.bfloat16)
    tokens = frames * cols
    for member in range(members):
        for step in range(SPLIT):
            row = me ^ (rest_mask(member) | (step << 2))
            at, lanes = (step % 2) * tokens, (step // 2) * wide
            for t in range(frames):
                grid[t, row + 1] = patches[member][at + t * cols : at + (t + 1) * cols, lanes : lanes + wide]

    cells = n * cols
    chunk = min(cells, 256)
    rows_in = chunk // cols
    upper = lax.broadcasted_iota(jnp.int32, (rows_in, cols, wide), 2) < half
    depth = 2 * wide
    for t in range(frames):
        for r in range(0, n, rows_in):
            near = grid[t, r + 1 : r + 1 + rows_in]
            far = jnp.where(upper, grid[t, r + 2 : r + 2 + rows_in], grid[t, r : r + rows_in])
            stacked[r * cols : r * cols + chunk, t * depth : t * depth + wide] = near.reshape(chunk, wide)
            stacked[r * cols : r * cols + chunk, t * depth + wide : (t + 1) * depth] = far.reshape(chunk, wide)

    sums = jnp.zeros((8, channels), jnp.float32)
    for t in range(frames):
        for r in range(0, n, rows_in):
            for part in range(4):
                lanes = slice(part * channels, (part + 1) * channels)
                here = dot(
                    stacked[r * cols : r * cols + chunk, : (t + 1) * depth],
                    in_weight[(frames - 1 - t) * depth :, lanes],
                )
                first[t, r : r + rows_in, :, lanes] = here.reshape(rows_in, cols, channels)
                sums = sums + jnp.sum(here.reshape(chunk // 8, 8, channels), axis=0)
    counted = 4.0 * frames * cells * (channels // GROUPS)

    def over_group(eight):
        line = jnp.sum(eight, axis=0, keepdims=True)
        return jnp.dot(line, grouped[...], precision=lax.Precision.HIGHEST, preferred_element_type=jnp.float32)

    mean = over_group(sums) / counted
    squares = jnp.zeros((8, channels), jnp.float32)
    for t in range(frames):
        for r in range(0, n, rows_in):
            for part in range(4):
                lanes = slice(part * channels, (part + 1) * channels)
                off = first[t, r : r + rows_in, :, lanes].reshape(chunk, channels) - mean
                squares = squares + jnp.sum((off * off).reshape(chunk // 8, 8, channels), axis=0)
    variance = over_group(squares) / counted
    slope = gain[...] * (1.0 / jnp.sqrt(variance + EPS))
    bias = shift[...]

    place = lax.broadcasted_iota(jnp.int32, (cols, channels), 0)
    for t in range(frames):
        for line in range(4):
            sub = 1 if line in (0, 2) else 0
            token_row = me - 1 if line == 0 else (me + 1 if line == 3 else me)
            inside = jnp.logical_and(token_row >= 0, token_row < n)
            token_row = jnp.clip(token_row, 0, n - 1)
            keep = jnp.where(inside, 1.0, 0.0)
            pair = []
            for side in range(2):
                part = sub * 2 + side
                x = first[t, token_row, :, part * channels : (part + 1) * channels]
                y = (x - mean) * slope + bias
                pair.append(y / (1.0 + jnp.exp(-y)) * keep)
            even, odd = pair
            taps[t, line, 0] = jnp.where(place == 0, 0.0, pltpu.roll(odd, 1, 0)).astype(jnp.bfloat16)
            taps[t, line, 1] = even.astype(jnp.bfloat16)
            taps[t, line, 2] = odd.astype(jnp.bfloat16)
            taps[t, line, 3] = jnp.where(place == cols - 1, 0.0, pltpu.roll(even, cols - 1, 0)).astype(jnp.bfloat16)

    for copy in copies:
        copy.wait()
    here = 4 * cols
    totals = [jnp.zeros((here, channels), jnp.float32) for _ in range(frames)]
    for a in range(frames):
        valid = a + 1
        for b in range(3):
            left = jnp.concatenate(
                [taps[:valid, b : b + 2, w : w + 2].reshape(valid * here, channels) for w in range(3)], axis=1
            )
            got = dot(left, held[a, b].reshape(3 * channels, channels))
            for t in range(valid):
                totals[frames - 1 - a + t] = totals[frames - 1 - a + t] + got[t * here : (t + 1) * here]
    for t in range(frames):
        for part in range(4):
            kept = first[t, me, :, part * channels : (part + 1) * channels]
            block = totals[t][part * cols : (part + 1) * cols] + kept
            for lane in range(channels // 128):
                tile = block[:, lane * 128 : (lane + 1) * 128]
                merged[t, part // 2, lane, pl.ds(part % 2, cols, stride=2), :] = tile
    for t in range(frames):
        for sub in range(2):
            for lane in range(channels // 128):
                out[t, sub, :, lane * 128 : (lane + 1) * 128] = merged[t, sub, lane].astype(jnp.bfloat16)


def widened(weight):
    blocks = []
    for row in range(2):
        for col in range(2):
            blocks.append(jnp.pad(weight, ((0, 0), (row, 1 - row), (col, 1 - col), (0, 0), (0, 0))))
    whole = jnp.concatenate(blocks, axis=-1)
    whole = jnp.concatenate([whole[:, 1:], whole[:, :1]], axis=1)
    return whole.reshape(-1, whole.shape[-1])


def chooser(latent):
    source = jnp.arange(3 * 8 * latent)
    target = jnp.arange(2 * 8 * latent)
    offset, lane = source // (8 * latent), source % (8 * latent)
    side, lane = lane // (4 * latent), lane % (4 * latent)
    row, col, channel = lane // (2 * latent), lane // latent % 2, lane % latent
    cell = 2 * (offset - 1) + col + 1
    to_side, to_lane = target // (8 * latent), target % (8 * latent)
    to_row, to_cell, to_channel = to_lane // (4 * latent), to_lane // latent % 4, to_lane % latent
    same = (
        (side[:, None] == to_side)
        & (row[:, None] == to_row)
        & (cell[:, None] == to_cell)
        & (channel[:, None] == to_channel)
    )
    return same.astype(jnp.bfloat16)


def shards(
    queries, keys, values, stream, head_weight, conv_in_weight, norm_gain, norm_shift, conv_mid_weight
):
    frames, _, cols, width = queries.shape
    n = lax.axis_size("seq")
    members = n // SPLIT
    depth = width // HEADS
    heads = HEADS // SPLIT
    tokens = frames * cols
    group = heads * depth
    latent = head_weight.shape[1] // 4
    wide = 2 * head_weight.shape[1]
    channels = norm_gain.shape[0]
    pairs = (heads + 1) // 2
    index = lax.axis_index("seq").astype(jnp.int32).reshape(1)
    bf16, f32 = jnp.bfloat16, jnp.float32

    prepared = pl.pallas_call(
        functools.partial(prepare_kernel, depth, heads),
        out_shape=[jax.ShapeDtypeStruct((tokens, group + pairs * wide), bf16)] * SPLIT
        + [jax.ShapeDtypeStruct((tokens, group), bf16)] * SPLIT
        + [jax.ShapeDtypeStruct((tokens, wide), f32)],
        in_specs=[SMEM] + [VMEM] * 5,
        out_specs=[VMEM] * (2 * SPLIT + 1),
        scratch_shapes=[pltpu.VMEM((SPLIT, tokens, pairs * wide), bf16)],
        compiler_params=pltpu.CompilerParams(vmem_limit_bytes=16 * 2**20),
        name="prepare",
    )(
        index,
        queries.reshape(tokens, width),
        keys.reshape(tokens, width),
        values.reshape(tokens, width),
        stream.reshape(tokens, width),
        head_weight,
    )
    kv, q, streamed = prepared[:SPLIT], prepared[SPLIT : 2 * SPLIT], prepared[-1]
    kv = [kv[0]] + [exchanged(kv[step], step << 2) for step in range(1, SPLIT)]
    q = [q[0]] + [exchanged(q[step], step << 2) for step in range(1, SPLIT)]
    mine = jnp.concatenate(kv, axis=0)
    blocks = [mine]
    for member in range(1, members):
        if member & 1 == 0 or member == 1:
            blocks.append(exchanged(mine, rest_mask(member)))
        else:
            blocks.append(exchanged(blocks[member - 1], 1))

    part = pl.pallas_call(
        functools.partial(attend_kernel, depth, heads),
        out_shape=jax.ShapeDtypeStruct((SPLIT * tokens // 2, wide), f32),
        in_specs=[VMEM] * (SPLIT + members + 1),
        out_specs=VMEM,
        compiler_params=pltpu.CompilerParams(vmem_limit_bytes=(16 + 2 * members // 4 * 4) * 2**20),
        name="attend",
    )(*q, *blocks, streamed)

    others = [exchanged(part, step << 2) for step in range(1, SPLIT)]
    patch = pl.pallas_call(
        functools.partial(gather_kernel, cols),
        out_shape=jax.ShapeDtypeStruct((part.shape[0], 2 * wide), bf16),
        in_specs=[VMEM] * 5,
        out_specs=VMEM,
        name="gather",
    )(part, *others, chooser(latent))
    patches = [patch] + [exchanged(patch, rest_mask(member)) for member in range(1, members)]

    in_weight = widened(conv_in_weight)
    lane = jnp.arange(channels) // (channels // GROUPS)
    grouped = (lane[:, None] == lane[None, :]).astype(f32)
    return pl.pallas_call(
        functools.partial(finish_kernel, frames, n, cols),
        out_shape=jax.ShapeDtypeStruct((frames, 2, 2 * cols, channels), bf16),
        in_specs=[SMEM] + [VMEM] * members + [VMEM, ANY, VMEM, VMEM, VMEM],
        out_specs=VMEM,
        scratch_shapes=[
            pltpu.VMEM((frames, n + 2, cols, wide), bf16),
            pltpu.VMEM((n * cols, frames * 2 * wide), bf16),
            pltpu.VMEM((frames, n, cols, 4 * channels), f32),
            pltpu.VMEM((frames, 4, 4, cols, channels), bf16),
            pltpu.VMEM(conv_mid_weight.shape, bf16),
            pltpu.VMEM((frames, 2, channels // 128, 2 * cols, 128), f32),
            pltpu.SemaphoreType.DMA((conv_mid_weight.shape[0],)),
        ],
        compiler_params=pltpu.CompilerParams(vmem_limit_bytes=(30 if n <= 16 else 52) * 2**20),
        name="finish",
    )(
        index,
        *patches,
        in_weight,
        conv_mid_weight,
        grouped,
        norm_gain.reshape(1, channels),
        norm_shift.reshape(1, channels),
    )


def solution(mesh):
    placed = (
        P("groups", "seq", None, None),
        P("groups", "seq", None, None),
        P("groups", "seq", None, None),
        P("groups", "seq", None, None),
        P(),
        P(),
        P(),
        P(),
        P(),
    )
    return jax.shard_map(
        shards,
        mesh=mesh,
        in_specs=placed,
        out_specs=P("groups", "seq", None, None),
        check_vma=False,
    )
```

time: 172 us -> 63.9 us (0.37); the launches traced: 169 us -> 63.6 us
  blocking collectives: 61.5 us -> 0 us
  waiting for transfers between devices: 58.2 us -> 20.2 us
  matrix products: 22.5 us -> 0 us
  Pallas kernels: 0 us -> 11.5 us
  starting transfers between devices: 13.4 us -> 19.5 us
    psum x2 -> x0, blocking collectives: 61.5 us -> none  [the longest x1 32 us: group_stats(): sums = lax.psum(jnp.sum(grouped, axis=(0, 1, 2, 4)), 'seq')]
    ppermute x11 -> x15, waiting for transfers between devices: 58.2 us -> 20.2 us  [exchanged(): return lax.ppermute(value, 'seq', pairs)]
    dot_general x64 -> x0, matrix products: 22.5 us -> none  [the longest x54 18.7 us: conv_taps(): jnp.dot(piece, weight[step_t, step_h, step_w], preferred_element_type=jnp...]
    pallas_call x0 -> x4, Pallas kernels: none -> 11.5 us  [the longest x1 7.05 us: shards(): pl.pallas_call(functools.partial(finish_kernel, frames, n, cols), out_sha...]
    unnamed x16 -> x30, local copies, waits for them, and re-layouts: 0.42 us -> 10.4 us
    ppermute x11 -> x15, starting transfers between devices: 13.4 us -> 19.5 us  [exchanged(): return lax.ppermute(value, 'seq', pairs)]
    another operation x9 -> x0, local copies, waits for them, and re-layouts: 4.35 us -> none  [the longest x4 3.27 us: shards(): jnp.stack([queries, keys, values])]
    slice x16 -> x2, local copies, waits for them, and re-layouts: 2 us -> 0.16 us  [widened(): whole = jnp.concatenate([whole[:, 1:], whole[:, :1]], axis=1)]
  transfers between devices with their start and end apart: 11 -> 15, of which waited for: 9 -> 7; matrix products, arithmetic and copies ran while one was open for 0% -> 3% of each run, Pallas kernels for 0% -> 0%
where the time goes in v1:
time: 63.9 us; the launch traced here: 63.6 us
  waiting for transfers between devices  20.2 us (32%)
  starting transfers between devices  19.5 us (31%)
  Pallas kernels  11.5 us (18%)
  local copies, waits for them, and re-layouts  10.6 us (17%)
  other arithmetic  1.61 us (3%)
    ppermute x15, waiting for transfers between devices, exchanged(): return lax.ppermute(value, 'seq', pairs)  20.2 us
    ppermute x15, starting transfers between devices, exchanged(): return lax.ppermute(value, 'seq', pairs)  19.5 us
    unnamed x30, local copies, waits for them, and re-layouts  10.4 us
    pallas_call x1, Pallas kernels, shards(): pl.pallas_call(functools.partial(finish_kernel, frames, n, cols), out_sha...  7.05 us
    pallas_call x1, Pallas kernels, shards(): pl.pallas_call(functools.partial(attend_kernel, depth, heads), out_shape=...  2.05 us
    pallas_call x1, Pallas kernels, shards(): pl.pallas_call(functools.partial(gather_kernel, cols), out_shape=jax.Shap...  1.88 us
  transfers between devices with their start and end apart: 15, of which 7 were waited for; matrix products, arithmetic and copies ran while one was open for 3% of the time, Pallas kernels for 0%

profile of v1, /device:TPU:0, one launch (start us, length us, event | category | flops | bytes accessed | tf_op | source)
XLA Modules:
  0.0 63.6 jit_solution(5127454354926692061)
XLA Ops:
  0.0 1.3 %copy.10.w = bf16[2560,64]{1,0:T(8,128)(2,1)S(1)} copy(bf16[2560,64]{0,1:T(8,128)(2,1)} %param.13) | data formatting | bytes 655360 | tf_op args[4]
  1.4 0.9 %copy-done.1 = bf16[3,1,16,2560]{3,2,1,0:T(8,128)(2,1)S(1)} copy-done((bf16[3,1,16,2560]{3,2,1,0:T(8,128)(2,1)S(1)}, bf16[3,1,16,2560]{3,2,1,0:T(8,128)(2,1)}, u32[]{:S(2)}) %copy-start.1) | copy-done | bytes 245784
  2.3 0.9 %copy-done.2 = bf16[3,1,16,2560]{3,2,1,0:T(8,128)(2,1)S(1)} copy-done((bf16[3,1,16,2560]{3,2,1,0:T(8,128)(2,1)S(1)}, bf16[3,1,16,2560]{3,2,1,0:T(8,128)(2,1)}, u32[]{:S(2)}) %copy-start.2) | copy-done | bytes 245784
  3.2 0.9 %copy-done.3 = bf16[3,1,16,2560]{3,2,1,0:T(8,128)(2,1)S(1)} copy-done((bf16[3,1,16,2560]{3,2,1,0:T(8,128)(2,1)S(1)}, bf16[3,1,16,2560]{3,2,1,0:T(8,128)(2,1)}, u32[]{:S(2)}) %copy-start.3) | copy-done | bytes 245784
  4.2 0.9 %copy-done.4 = bf16[3,1,16,2560]{3,2,1,0:T(8,128)(2,1)S(1)} copy-done((bf16[3,1,16,2560]{3,2,1,0:T(8,128)(2,1)S(1)}, bf16[3,1,16,2560]{3,2,1,0:T(8,128)(2,1)}, u32[]{:S(2)}) %copy-start.4) | copy-done | bytes 245784
  5.1 0.5 prepare.1
  5.6 3.1 %collective-permute-start.3 = (bf16[48,1024]{1,0:T(8,128)(2,1)S(1)}, bf16[48,1024]{1,0:T(8,128)(2,1)S(1)}, u32[]{:S(2)}, u32[]{:S(2)}) collective-permute-start(bf16[48,1024]{1,0:T(8,128)(2,1)S(1)} %get-tuple-element.19), channel_id=1, source_target_pairs={{0,4},{1,5},{2,6},{3,7},{4,0},{5,1},{6,2},{7,3},{8,12},{9,13},{10,... | collective-permute-start | bytes 294920 | tf_op jit(solution)/shard_map/ppermute | solution.py:22
  8.7 2.6 %collective-permute-start.4 = (bf16[48,1024]{1,0:T(8,128)(2,1)S(1)}, bf16[48,1024]{1,0:T(8,128)(2,1)S(1)}, u32[]{:S(2)}, u32[]{:S(2)}) collective-permute-start(bf16[48,1024]{1,0:T(8,128)(2,1)S(1)} %get-tuple-element.20), channel_id=1, source_target_pairs={{0,8},{1,9},{2,10},{3,11},{4,12},{5,13},{6,14},{7,15},{8,0},{9,1},... | collective-permute-start | bytes 294920 | tf_op jit(solution)/shard_map/ppermute | solution.py:22
  11.3 0.9 %collective-permute-start = (bf16[48,640]{1,0:T(8,128)(2,1)S(1)}, bf16[48,640]{1,0:T(8,128)(2,1)S(1)}, u32[]{:S(2)}, u32[]{:S(2)}) collective-permute-start(bf16[48,640]{1,0:T(8,128)(2,1)S(1)} %get-tuple-element.15), channel_id=1, source_target_pairs={{0,4},{1,5},{2,6},{3,7},{4,0},{5,1},{6,2},{7,3},{8,12},{9,13},{10,... | collective-permute-start | bytes 184328 | tf_op jit(solution)/shard_map/ppermute | solution.py:22
  12.2 3.5 %collective-permute-start.1 = (bf16[48,640]{1,0:T(8,128)(2,1)S(1)}, bf16[48,640]{1,0:T(8,128)(2,1)S(1)}, u32[]{:S(2)}, u32[]{:S(2)}) collective-permute-start(bf16[48,640]{1,0:T(8,128)(2,1)S(1)} %get-tuple-element.16), channel_id=1, source_target_pairs={{0,8},{1,9},{2,10},{3,11},{4,12},{5,13},{6,14},{7,15},{8,0},{9,1},... | collective-permute-start | bytes 184328 | tf_op jit(solution)/shard_map/ppermute | solution.py:22
  15.7 0.3 fusion.7
  16.4 4.9 %collective-permute-done.4 = bf16[48,1024]{1,0:T(8,128)(2,1)S(1)} collective-permute-done((bf16[48,1024]{1,0:T(8,128)(2,1)S(1)}, bf16[48,1024]{1,0:T(8,128)(2,1)S(1)}, u32[]{:S(2)}, u32[]{:S(2)}) %collective-permute-start.4) | collective-permute-done | bytes 98336 | tf_op jit(solution)/shard_map/ppermute | solution.py:22
  21.3 1.6 %collective-permute-start.7 = (bf16[192,1024]{1,0:T(8,128)(2,1)S(1)}, bf16[192,1024]{1,0:T(8,128)(2,1)S(1)}, u32[]{:S(2)}, u32[]{:S(2)}) collective-permute-start(bf16[192,1024]{1,0:T(8,128)(2,1)S(1)} %constant_dynamic-update-slice_fusion.refs_4_), channel_id=1, source_target_pairs={{0,2},{1,3},{2,0},{3,1},{4,6},{5,7},{6,4},{7,5},{8,10},{9,11},{10,... | collective-permute-start | bytes 1179656 | tf_op jit(solution)/shard_map/ppermute | solution.py:22
  22.9 0.2 pad_maximum_fusion
  23.2 5.9 %collective-permute-done.7.refs_6_ = bf16[192,1024]{1,0:T(8,128)(2,1)S(1)} collective-permute-done((bf16[192,1024]{1,0:T(8,128)(2,1)S(1)}, bf16[192,1024]{1,0:T(8,128)(2,1)S(1)}, u32[]{:S(2)}, u32[]{:S(2)}) %collective-permute-start.7) | collective-permute-done | bytes 393248 | tf_op jit(solution)/shard_map/ppermute | solution.py:22
  29.1 0.9 %and_convert_fusion.chosen = bf16[384,256]{1,0:T(8,128)(2,1)} fusion(s32[256]{0:T(256)S(1)} %get-tuple-element.27, s32[256]{0:T(256)S(1)} %get-tuple-element.28, s32[256]{0:T(256)S(1)} %get-tuple-element.29, s32[256]{0:T(256)S(1)} %get-tuple-element.30, s32[384]{0:T(512)S(1)} %get-tuple-element.23, s32[384]{0:T(512)S(1)} %get-tuple-element.26, ...), kind=kLoop, calls=%fused_computation.17 | loop fusion | flops 786432 | bytes 206848 | tf_op jit(solution)/shard_map/convert_element_type | solution.py:242
  30.1 0.7 %collective-permute-done.8.refs_7_ = bf16[192,1024]{1,0:T(8,128)(2,1)S(1)} collective-permute-done((bf16[192,1024]{1,0:T(8,128)(2,1)S(1)}, bf16[192,1024]{1,0:T(8,128)(2,1)S(1)}, u32[]{:S(2)}, u32[]{:S(2)}) %collective-permute-start.8) | collective-permute-done | bytes 393248 | tf_op jit(solution)/shard_map/ppermute | solution.py:22
  30.8 2.1 %attend.1.own = f32[96,128]{1,0:T(8,128)S(1)} custom-call(bf16[48,640]{1,0:T(8,128)(2,1)S(1)} %get-tuple-element.14.refs_0_, bf16[48,640]{1,0:T(8,128)(2,1)S(1)} %collective-permute-done.refs_1_, bf16[48,640]{1,0:T(8,128)(2,1)S(1)} %collective-permute-done.1.refs_2_, bf16[48,640]{1,0:T(8,128)(2,1)S(1)} %collective-permute-done.2.refs_3_, ...), custom_call_target="tpu_custom_call" | custom-call | tf_op jit(solution)/shard_map/attend/pallas_call | solution.py:291
  32.9 5.1 %collective-permute-start.10 = (f32[96,128]{1,0:T(8,128)S(1)}, f32[96,128]{1,0:T(8,128)S(1)}, u32[]{:S(2)}, u32[]{:S(2)}) collective-permute-start(f32[96,128]{1,0:T(8,128)S(1)} %attend.1.own), channel_id=1, source_target_pairs={{0,8},{1,9},{2,10},{3,11},{4,12},{5,13},{6,14},{7,15},{8,0},{9,1},... | collective-permute-start | bytes 147464 | tf_op jit(solution)/shard_map/ppermute | solution.py:22
  38.0 0.6 collective-permute-start.11
  38.7 2.8 %collective-permute-done.10.two = f32[96,128]{1,0:T(8,128)S(1)} collective-permute-done((f32[96,128]{1,0:T(8,128)S(1)}, f32[96,128]{1,0:T(8,128)S(1)}, u32[]{:S(2)}, u32[]{:S(2)}) %collective-permute-start.10) | collective-permute-done | bytes 49184 | tf_op jit(solution)/shard_map/ppermute | solution.py:22
  41.5 2.4 %collective-permute-done.11.three = f32[96,128]{1,0:T(8,128)S(1)} collective-permute-done((f32[96,128]{1,0:T(8,128)S(1)}, f32[96,128]{1,0:T(8,128)S(1)}, u32[]{:S(2)}, u32[]{:S(2)}) %collective-permute-start.11) | collective-permute-done | bytes 49184 | tf_op jit(solution)/shard_map/ppermute | solution.py:22
  43.9 0.6 copy-done.9
  44.5 0.6 copy-done.10
  45.1 1.9 %gather.1.refs_0_ = bf16[96,256]{1,0:T(8,128)(2,1)} custom-call(f32[96,128]{1,0:T(8,128)} %copy-done.6, f32[96,128]{1,0:T(8,128)} %copy-done.10, f32[96,128]{1,0:T(8,128)} %copy-done.8, f32[96,128]{1,0:T(8,128)} %copy-done.9, bf16[384,256]{1,0:T(8,128)(2,1)} %and_convert_fusion.chosen), custom_call_target="tpu_custom_call" | custom-call | tf_op jit(solution)/shard_map/gather/pallas_call | solution.py:301
  47.0 1.5 %collective-permute-start.13 = (bf16[96,256]{1,0:T(8,128)(2,1)}, bf16[96,256]{1,0:T(8,128)(2,1)S(1)}, u32[]{:S(2)}, u32[]{:S(2)}) collective-permute-start(bf16[96,256]{1,0:T(8,128)(2,1)} %gather.1.refs_0_), channel_id=1, source_target_pairs={{0,2},{1,3},{2,0},{3,1},{4,6},{5,7},{6,4},{7,5},{8,10},{9,11},{10,... | collective-permute-start | bytes 147464 | tf_op jit(solution)/shard_map/ppermute | solution.py:22
  48.5 0.3 collective-permute-start.14
  49.0 2.3 %collective-permute-done.13.refs_2_ = bf16[96,256]{1,0:T(8,128)(2,1)S(1)} collective-permute-done((bf16[96,256]{1,0:T(8,128)(2,1)}, bf16[96,256]{1,0:T(8,128)(2,1)S(1)}, u32[]{:S(2)}, u32[]{:S(2)}) %collective-permute-start.13) | collective-permute-done | bytes 49184 | tf_op jit(solution)/shard_map/ppermute | solution.py:22
  51.4 1.1 %collective-permute-done.14.refs_3_ = bf16[96,256]{1,0:T(8,128)(2,1)S(1)} collective-permute-done((bf16[96,256]{1,0:T(8,128)(2,1)}, bf16[96,256]{1,0:T(8,128)(2,1)S(1)}, u32[]{:S(2)}, u32[]{:S(2)}) %collective-permute-start.14) | collective-permute-done | bytes 49184 | tf_op jit(solution)/shard_map/ppermute | solution.py:22
  52.5 3.3 %copy-done = bf16[3,3,3,384,384]{4,3,2,1,0:T(8,128)(2,1)S(1)} copy-done((bf16[3,3,3,384,384]{4,3,2,1,0:T(8,128)(2,1)S(1)}, bf16[3,3,3,384,384]{4,3,2,1,0:T(8,128)(2,1)}, u32[]{:S(2)}) %copy-start) | copy-done | bytes 7962648
  55.7 0.8 %copy-done.5 = bf16[96,256]{1,0:T(8,128)(2,1)S(1)} copy-done((bf16[96,256]{1,0:T(8,128)(2,1)S(1)}, bf16[96,256]{1,0:T(8,128)(2,1)}, u32[]{:S(2)}) %copy-start.5) | copy-done | bytes 49176
  56.5 7.0 %finish.1 = bf16[3,2,32,384]{3,2,1,0:T(8,128)(2,1)} custom-call(s32[1]{0:T(128)} %bitcast.index, bf16[96,256]{1,0:T(8,128)(2,1)S(1)} %copy-done.5, bf16[96,256]{1,0:T(8,128)(2,1)S(1)} %collective-permute-done.12.refs_1_, bf16[96,256]{1,0:T(8,128)(2,1)S(1)} %collective-permute-done.13.refs_2_, bf16[96,256]{1,0:T(8,128)(2,1)S(1)} %collective-permute-done.14.refs_3_, ...), custom_call_target="tpu_custom_call" | custom-call | tf_op jit(solution)/shard_map/finish/pallas_call | solution.py:313
  (46 shorter events, 0.7 us)
Async XLA Ops:
  0.0 15.7 %copy-start.7 = (bf16[3,3,3,16,384]{4,3,2,1,0:T(8,128)(2,1)S(1)}, bf16[3,3,3,16,384]{4,3,2,1,0:T(8,128)(2,1)}, u32[]{:S(2)}) copy-start(bf16[3,3,3,16,384]{4,3,2,1,0:T(8,128)(2,1)} %param.14) | copy-start | bytes 995332
  1.4 0.9 %copy-start.1 = (bf16[3,1,16,2560]{3,2,1,0:T(8,128)(2,1)S(1)}, bf16[3,1,16,2560]{3,2,1,0:T(8,128)(2,1)}, u32[]{:S(2)}) copy-start(bf16[3,1,16,2560]{3,2,1,0:T(8,128)(2,1)} %param.9) | copy-start | bytes 737284
  2.3 0.9 %copy-start.2 = (bf16[3,1,16,2560]{3,2,1,0:T(8,128)(2,1)S(1)}, bf16[3,1,16,2560]{3,2,1,0:T(8,128)(2,1)}, u32[]{:S(2)}) copy-start(bf16[3,1,16,2560]{3,2,1,0:T(8,128)(2,1)} %param.10) | copy-start | bytes 737284
  3.2 0.9 %copy-start.3 = (bf16[3,1,16,2560]{3,2,1,0:T(8,128)(2,1)S(1)}, bf16[3,1,16,2560]{3,2,1,0:T(8,128)(2,1)}, u32[]{:S(2)}) copy-start(bf16[3,1,16,2560]{3,2,1,0:T(8,128)(2,1)} %param.11) | copy-start | bytes 737284
  4.2 0.9 %copy-start.4 = (bf16[3,1,16,2560]{3,2,1,0:T(8,128)(2,1)S(1)}, bf16[3,1,16,2560]{3,2,1,0:T(8,128)(2,1)}, u32[]{:S(2)}) copy-start(bf16[3,1,16,2560]{3,2,1,0:T(8,128)(2,1)} %param.12) | copy-start | bytes 737284
  5.6 10.6 %collective-permute-start.3 = (bf16[48,1024]{1,0:T(8,128)(2,1)S(1)}, bf16[48,1024]{1,0:T(8,128)(2,1)S(1)}, u32[]{:S(2)}, u32[]{:S(2)}) collective-permute-start(bf16[48,1024]{1,0:T(8,128)(2,1)S(1)} %get-tuple-element.19), channel_id=1, source_target_pairs={{0,4},{1,5},{2,6},{3,7},{4,0},{5,1},{6,2},{7,3},{8,12},{9,13},{10,... | collective-permute-start | bytes 294920 | tf_op jit(solution)/shard_map/ppermute | solution.py:22
  8.7 12.5 %collective-permute-start.4 = (bf16[48,1024]{1,0:T(8,128)(2,1)S(1)}, bf16[48,1024]{1,0:T(8,128)(2,1)S(1)}, u32[]{:S(2)}, u32[]{:S(2)}) collective-permute-start(bf16[48,1024]{1,0:T(8,128)(2,1)S(1)} %get-tuple-element.20), channel_id=1, source_target_pairs={{0,8},{1,9},{2,10},{3,11},{4,12},{5,13},{6,14},{7,15},{8,0},{9,1},... | collective-permute-start | bytes 294920 | tf_op jit(solution)/shard_map/ppermute | solution.py:22
  11.3 9.9 %collective-permute-start.5 = (bf16[48,1024]{1,0:T(8,128)(2,1)S(1)}, bf16[48,1024]{1,0:T(8,128)(2,1)S(1)}, u32[]{:S(2)}, u32[]{:S(2)}) collective-permute-start(bf16[48,1024]{1,0:T(8,128)(2,1)S(1)} %get-tuple-element.21), channel_id=1, source_target_pairs={{0,12},{1,13},{2,14},{3,15},{4,8},{5,9},{6,10},{7,11},{8,4},{9,5},... | collective-permute-start | bytes 294920 | tf_op jit(solution)/shard_map/ppermute | solution.py:22
  11.3 18.8 %collective-permute-start = (bf16[48,640]{1,0:T(8,128)(2,1)S(1)}, bf16[48,640]{1,0:T(8,128)(2,1)S(1)}, u32[]{:S(2)}, u32[]{:S(2)}) collective-permute-start(bf16[48,640]{1,0:T(8,128)(2,1)S(1)} %get-tuple-element.15), channel_id=1, source_target_pairs={{0,4},{1,5},{2,6},{3,7},{4,0},{5,1},{6,2},{7,3},{8,12},{9,13},{10,... | collective-permute-start | bytes 184328 | tf_op jit(solution)/shard_map/ppermute | solution.py:22
  12.2 17.9 %collective-permute-start.1 = (bf16[48,640]{1,0:T(8,128)(2,1)S(1)}, bf16[48,640]{1,0:T(8,128)(2,1)S(1)}, u32[]{:S(2)}, u32[]{:S(2)}) collective-permute-start(bf16[48,640]{1,0:T(8,128)(2,1)S(1)} %get-tuple-element.16), channel_id=1, source_target_pairs={{0,8},{1,9},{2,10},{3,11},{4,12},{5,13},{6,14},{7,15},{8,0},{9,1},... | collective-permute-start | bytes 184328 | tf_op jit(solution)/shard_map/ppermute | solution.py:22
  16.2 13.9 %collective-permute-start.2 = (bf16[48,640]{1,0:T(8,128)(2,1)S(1)}, bf16[48,640]{1,0:T(8,128)(2,1)S(1)}, u32[]{:S(2)}, u32[]{:S(2)}) collective-permute-start(bf16[48,640]{1,0:T(8,128)(2,1)S(1)} %get-tuple-element.17), channel_id=1, source_target_pairs={{0,12},{1,13},{2,14},{3,15},{4,8},{5,9},{6,10},{7,11},{8,4},{9,5},... | collective-permute-start | bytes 184328 | tf_op jit(solution)/shard_map/ppermute | solution.py:22
  21.3 7.8 %collective-permute-start.7 = (bf16[192,1024]{1,0:T(8,128)(2,1)S(1)}, bf16[192,1024]{1,0:T(8,128)(2,1)S(1)}, u32[]{:S(2)}, u32[]{:S(2)}) collective-permute-start(bf16[192,1024]{1,0:T(8,128)(2,1)S(1)} %constant_dynamic-update-slice_fusion.refs_4_), channel_id=1, source_target_pairs={{0,2},{1,3},{2,0},{3,1},{4,6},{5,7},{6,4},{7,5},{8,10},{9,11},{10,... | collective-permute-start | bytes 1179656 | tf_op jit(solution)/shard_map/ppermute | solution.py:22
  23.1 25.9 %copy-start.11 = (f32[384]{0:T(512)S(1)}, f32[384]{0:T(512)}, u32[]{:S(2)}) copy-start(f32[384]{0:T(512)} %param.15) | copy-start | bytes 4612
  23.1 25.9 %copy-start.12 = (f32[384]{0:T(512)S(1)}, f32[384]{0:T(512)}, u32[]{:S(2)}) copy-start(f32[384]{0:T(512)} %param.16) | copy-start | bytes 4612
  23.1 7.0 %collective-permute-start.6 = (bf16[192,1024]{1,0:T(8,128)(2,1)S(1)}, bf16[192,1024]{1,0:T(8,128)(2,1)S(1)}, u32[]{:S(2)}, u32[]{:S(2)}) collective-permute-start(bf16[192,1024]{1,0:T(8,128)(2,1)S(1)} %constant_dynamic-update-slice_fusion.refs_4_), channel_id=1, source_target_pairs={{0,1},{1,0},{2,3},{3,2},{4,5},{5,4},{6,7},{7,6},{8,9},{9,8},{10,11... | collective-permute-start | bytes 1179656 | tf_op jit(solution)/shard_map/ppermute | solution.py:22
  29.1 1.7 %collective-permute-start.8 = (bf16[192,1024]{1,0:T(8,128)(2,1)S(1)}, bf16[192,1024]{1,0:T(8,128)(2,1)S(1)}, u32[]{:S(2)}, u32[]{:S(2)}) collective-permute-start(bf16[192,1024]{1,0:T(8,128)(2,1)S(1)} %collective-permute-done.7.refs_6_), channel_id=1, source_target_pairs={{0,1},{1,0},{2,3},{3,2},{4,5},{5,4},{6,7},{7,6},{8,9},{9,8},{10,11... | collective-permute-start | bytes 1179656 | tf_op jit(solution)/shard_map/ppermute | solution.py:22
  32.9 11.0 %copy-start.6 = (f32[96,128]{1,0:T(8,128)}, f32[96,128]{1,0:T(8,128)S(1)}, u32[]{:S(2)}) copy-start(f32[96,128]{1,0:T(8,128)S(1)} %attend.1.own) | copy-start | bytes 147460
  32.9 8.6 %collective-permute-start.10 = (f32[96,128]{1,0:T(8,128)S(1)}, f32[96,128]{1,0:T(8,128)S(1)}, u32[]{:S(2)}, u32[]{:S(2)}) collective-permute-start(f32[96,128]{1,0:T(8,128)S(1)} %attend.1.own), channel_id=1, source_target_pairs={{0,8},{1,9},{2,10},{3,11},{4,12},{5,13},{6,14},{7,15},{8,0},{9,1},... | collective-permute-start | bytes 147464 | tf_op jit(solution)/shard_map/ppermute | solution.py:22
  38.0 5.9 %collective-permute-start.11 = (f32[96,128]{1,0:T(8,128)S(1)}, f32[96,128]{1,0:T(8,128)S(1)}, u32[]{:S(2)}, u32[]{:S(2)}) collective-permute-start(f32[96,128]{1,0:T(8,128)S(1)} %attend.1.own), channel_id=1, source_target_pairs={{0,12},{1,13},{2,14},{3,15},{4,8},{5,9},{6,10},{7,11},{8,4},{9,5},... | collective-permute-start | bytes 147464 | tf_op jit(solution)/shard_map/ppermute | solution.py:22
  38.6 5.3 %collective-permute-start.9 = (f32[96,128]{1,0:T(8,128)S(1)}, f32[96,128]{1,0:T(8,128)S(1)}, u32[]{:S(2)}, u32[]{:S(2)}) collective-permute-start(f32[96,128]{1,0:T(8,128)S(1)} %attend.1.own), channel_id=1, source_target_pairs={{0,4},{1,5},{2,6},{3,7},{4,0},{5,1},{6,2},{7,3},{8,12},{9,13},{10,... | collective-permute-start | bytes 147464 | tf_op jit(solution)/shard_map/ppermute | solution.py:22
  41.5 2.4 %copy-start.8 = (f32[96,128]{1,0:T(8,128)}, f32[96,128]{1,0:T(8,128)S(1)}, u32[]{:S(2)}) copy-start(f32[96,128]{1,0:T(8,128)S(1)} %collective-permute-done.10.two) | copy-start | bytes 147460
  43.9 0.6 copy-start.9
  44.5 0.6 copy-start.10
  47.0 2.0 %collective-permute-start.12 = (bf16[96,256]{1,0:T(8,128)(2,1)}, bf16[96,256]{1,0:T(8,128)(2,1)S(1)}, u32[]{:S(2)}, u32[]{:S(2)}) collective-permute-start(bf16[96,256]{1,0:T(8,128)(2,1)} %gather.1.refs_0_), channel_id=1, source_target_pairs={{0,1},{1,0},{2,3},{3,2},{4,5},{5,4},{6,7},{7,6},{8,9},{9,8},{10,11... | collective-permute-start | bytes 147464 | tf_op jit(solution)/shard_map/ppermute | solution.py:22
  47.0 4.4 %collective-permute-start.13 = (bf16[96,256]{1,0:T(8,128)(2,1)}, bf16[96,256]{1,0:T(8,128)(2,1)S(1)}, u32[]{:S(2)}, u32[]{:S(2)}) collective-permute-start(bf16[96,256]{1,0:T(8,128)(2,1)} %gather.1.refs_0_), channel_id=1, source_target_pairs={{0,2},{1,3},{2,0},{3,1},{4,6},{5,7},{6,4},{7,5},{8,10},{9,11},{10,... | collective-permute-start | bytes 147464 | tf_op jit(solution)/shard_map/ppermute | solution.py:22
  48.5 3.9 %collective-permute-start.14 = (bf16[96,256]{1,0:T(8,128)(2,1)}, bf16[96,256]{1,0:T(8,128)(2,1)S(1)}, u32[]{:S(2)}, u32[]{:S(2)}) collective-permute-start(bf16[96,256]{1,0:T(8,128)(2,1)} %gather.1.refs_0_), channel_id=1, source_target_pairs={{0,3},{1,2},{2,1},{3,0},{4,7},{5,6},{6,5},{7,4},{8,11},{9,10},{10,... | collective-permute-start | bytes 147464 | tf_op jit(solution)/shard_map/ppermute | solution.py:22
  52.5 3.3 %copy-start = (bf16[3,3,3,384,384]{4,3,2,1,0:T(8,128)(2,1)S(1)}, bf16[3,3,3,384,384]{4,3,2,1,0:T(8,128)(2,1)}, u32[]{:S(2)}) copy-start(bf16[3,3,3,384,384]{4,3,2,1,0:T(8,128)(2,1)} %refs_5_.1) | copy-start | bytes 23887876
  55.7 0.8 %copy-start.5 = (bf16[96,256]{1,0:T(8,128)(2,1)S(1)}, bf16[96,256]{1,0:T(8,128)(2,1)}, u32[]{:S(2)}) copy-start(bf16[96,256]{1,0:T(8,128)(2,1)} %gather.1.refs_0_) | copy-start | bytes 147460

commit v2 on v1

--- a/solution.py
+++ b/solution.py
@@ -14,7 +14,7 @@
 
 VMEM = pl.BlockSpec(memory_space=pltpu.VMEM)
 SMEM = pl.BlockSpec(memory_space=pltpu.SMEM)
-ANY = pl.BlockSpec(memory_space=pl.ANY)
+HBM = pl.BlockSpec(memory_space=pltpu.HBM)
 
 
 def exchanged(value, mask):
@@ -31,62 +31,103 @@
 
 
 def prepare_kernel(depth, heads, index, q, k, v, s, w, *refs):
-    kv_out, q_out, stream_out, projected = refs[:SPLIT], refs[SPLIT : 2 * SPLIT], refs[-2], refs[-1]
+    out, refs = refs[:SPLIT], refs[SPLIT:]
+    stream_out, v_here, s_here, w_here, projected, sem = refs
     tokens = q.shape[0]
     group = heads * depth
     place = (index[0] >> 2) & 3
-    twice = jnp.concatenate([w[...], w[...]], axis=1)
-    low = lax.broadcasted_iota(jnp.int32, (tokens, 2 * w.shape[1]), 1) < w.shape[1]
-
-    def through(head):
-        return dot(v[:, head * depth : (head + 1) * depth], twice[head * depth : (head + 1) * depth])
-
-    wide = twice.shape[1]
+    whole = [
+        pltpu.make_async_copy(source, target, sem.at[at])
+        for at, (source, target) in enumerate(((v, v_here), (w, w_here), (s, s_here)))
+    ]
+    parts = []
+    for step in range(SPLIT):
+        columns = pl.ds(pl.multiple_of((place ^ step) * group, 128), group)
+        at = len(whole) + 2 * step
+        parts.append(pltpu.make_async_copy(k.at[:, columns], out[step].at[:, :group], sem.at[at]))
+        parts.append(pltpu.make_async_copy(q.at[:, columns], out[step].at[:, -group:], sem.at[at + 1]))
+    for copy in whole + parts:
+        copy.start()
+    half = w.shape[0]
+    wide = 2 * half
+    low = lax.broadcasted_iota(jnp.int32, (tokens, wide), 1) < half
+
+    def through(rows, columns):
+        weight = w_here[:, columns]
+        return lax.dot_general(
+            rows[:, columns],
+            jnp.concatenate([weight, weight], axis=0),
+            (((1,), (1,)), ((), ())),
+            preferred_element_type=jnp.float32,
+        )
+
+    def head_through(head):
+        return through(v_here, slice(head * depth, (head + 1) * depth))
+
+    whole[0].wait()
+    whole[1].wait()
     for owner in range(SPLIT):
         for pair in range((heads + 1) // 2):
             first = owner * heads + 2 * pair
-            both = through(first)
+            both = head_through(first)
             if 2 * pair + 1 < heads:
-                both = jnp.where(low, both, through(first + 1))
+                both = jnp.where(low, both, head_through(first + 1))
             projected[owner, :, pair * wide : (pair + 1) * wide] = both.astype(jnp.bfloat16)
     for step in range(SPLIT):
-        owner = place ^ step
-        columns = pl.ds(pl.multiple_of(owner * group, 128), group)
-        kv_out[step][:, :group] = k[:, columns]
-        kv_out[step][:, group:] = projected[owner]
-        q_out[step][...] = q[:, columns]
-    stream_out[...] = dot(s[...], twice)
-
-
-def attend_kernel(depth, heads, *refs):
-    q, kv, stream, out = refs[:SPLIT], refs[SPLIT:-2], refs[-2], refs[-1]
+        out[step][:, group:-group] = projected[place ^ step]
+    whole[2].wait()
+    stream_out[...] = through(s_here, slice(None))
+    for copy in parts:
+        copy.wait()
+
+
+def attend_kernel(depth, heads, last, *refs):
+    q, refs = refs[:SPLIT], refs[SPLIT:]
+    if last:
+        kv, (stream, top_in, total_in, mixed_in, out) = refs[:-5], refs[-5:]
+    else:
+        kv, (top_out, total_out, mixed_out) = refs[:-3], refs[-3:]
     tokens = q[0].shape[0]
-    wide = stream.shape[1]
+    group = heads * depth
+    wide = 128
     factor = 1.4426950408889634 / depth**0.5
     rows = SPLIT * tokens
     low = lax.broadcasted_iota(jnp.int32, (rows, wide), 1) < wide // 2
-    total_out = jnp.zeros((rows, wide), jnp.float32)
+    summed = jnp.zeros((rows, wide), jnp.float32)
     for head in range(heads):
         columns = slice(head * depth, (head + 1) * depth)
-        query = jnp.concatenate([piece[:, columns] for piece in q], axis=0)
+        at = q[0].shape[1] - group + head * depth
+        query = jnp.concatenate([piece[:, at : at + depth] for piece in q], axis=0)
         key = jnp.concatenate([piece[:, columns] for piece in kv], axis=0)
-        at = heads * depth + (head // 2) * wide
+        at = group + (head // 2) * wide
         value = jnp.concatenate([piece[:, at : at + wide] for piece in kv], axis=0)
         scores = lax.dot_general(query, key, (((1,), (1,)), ((), ())), preferred_element_type=jnp.float32)
         top = jnp.max(scores, axis=1, keepdims=True)
+        if last:
+            before = top_in[head]
+            top = jnp.maximum(top, before[:, :1])
         expo = jnp.exp2((scores - top) * factor)
         total = jnp.sum(expo, axis=1, keepdims=True)
-        mixed = dot(expo.astype(jnp.bfloat16), value) * (1.0 / total)
+        mixed = dot(expo.astype(jnp.bfloat16), value)
+        if not last:
+            top_out[head] = jnp.broadcast_to(top, (rows, wide))
+            total_out[head] = jnp.broadcast_to(total, (rows, wide))
+            mixed_out[head] = mixed
+            continue
+        decay = jnp.exp2((before - top) * factor)
+        mixed = (mixed + mixed_in[head] * decay) * (1.0 / (total + total_in[head] * decay))
         mine = low if head % 2 == 0 else jnp.logical_not(low)
-        total_out = total_out + jnp.where(mine, mixed, 0.0)
-    total_out = total_out + pltpu.roll(total_out, wide // 2, 1)
+        summed = summed + jnp.where(mine, mixed, 0.0)
+    if not last:
+        return
+    summed = summed + pltpu.roll(summed, wide // 2, 1)
     half = rows // 2
-    upper = total_out[:half]
+    upper = summed[:half]
     upper = jnp.concatenate([upper[:tokens] + stream[...], upper[tokens:]], axis=0)
-    out[...] = jnp.where(low[:half], upper, total_out[half:])
-
-
-def gather_kernel(cols, own, one, two, three, chosen, out):
+    out[...] = jnp.where(low[:half], upper, summed[half:])
+
+
+def gather_kernel(own, one, two, three, out):
     rows, wide = own.shape
     half = rows // 2
 
@@ -95,37 +136,33 @@
 
     far = two[...] + swap_rows(three[...])
     latent = (own[...] + swap_rows(one[...])) + pltpu.roll(far, wide // 2, 1)
-    latent = latent.astype(jnp.bfloat16).astype(jnp.float32)
-    column = lax.broadcasted_iota(jnp.int32, (rows, wide), 0) % cols
-    before = jnp.where(column == 0, 0.0, pltpu.roll(latent, 1, 0))
-    after = jnp.where(column == cols - 1, 0.0, pltpu.roll(latent, rows - 1, 0))
-    row = jnp.concatenate([before, latent, after], axis=1).astype(jnp.bfloat16)
-    out[...] = dot(row, chosen[...]).astype(jnp.bfloat16)
+    out[...] = latent.astype(jnp.bfloat16)
 
 
 def finish_kernel(frames, n, cols, index, *refs):
     members = n // SPLIT
     patches, refs = refs[:members], refs[members:]
-    (in_weight, mid_weight, grouped, gain, shift, out, grid, stacked, first, taps, held, merged, sem) = refs
+    (chosen, in_weight, held, grouped, gain, shift, out, grid, stacked, first, taps, merged) = refs
     channels = gain.shape[1]
     wide = grid.shape[-1]
     half = wide // 2
     me = index[0]
-    copies = [
-        pltpu.make_async_copy(mid_weight.at[a], held.at[a], sem.at[a]) for a in range(mid_weight.shape[0])
-    ]
-    for copy in copies:
-        copy.start()
-
     grid[:, 0] = jnp.zeros((frames, cols, wide), jnp.bfloat16)
     grid[:, n + 1] = jnp.zeros((frames, cols, wide), jnp.bfloat16)
     tokens = frames * cols
     for member in range(members):
+        latent = patches[member][...].astype(jnp.float32)
+        rows = latent.shape[0]
+        column = lax.broadcasted_iota(jnp.int32, latent.shape, 0) % cols
+        before = jnp.where(column == 0, 0.0, pltpu.roll(latent, 1, 0))
+        after = jnp.where(column == cols - 1, 0.0, pltpu.roll(latent, rows - 1, 0))
+        around = jnp.concatenate([before, latent, after], axis=1).astype(jnp.bfloat16)
+        patch = dot(around, chosen[...]).astype(jnp.bfloat16)
         for step in range(SPLIT):
             row = me ^ (rest_mask(member) | (step << 2))
             at, lanes = (step % 2) * tokens, (step // 2) * wide
             for t in range(frames):
-                grid[t, row + 1] = patches[member][at + t * cols : at + (t + 1) * cols, lanes : lanes + wide]
+                grid[t, row + 1] = patch[at + t * cols : at + (t + 1) * cols, lanes : lanes + wide]
 
     cells = n * cols
     chunk = min(cells, 256)
@@ -188,8 +225,6 @@
             taps[t, line, 2] = odd.astype(jnp.bfloat16)
             taps[t, line, 3] = jnp.where(place == cols - 1, 0.0, pltpu.roll(even, cols - 1, 0)).astype(jnp.bfloat16)
 
-    for copy in copies:
-        copy.wait()
     here = 4 * cols
     totals = [jnp.zeros((here, channels), jnp.float32) for _ in range(frames)]
     for a in range(frames):
@@ -261,13 +296,18 @@
 
     prepared = pl.pallas_call(
         functools.partial(prepare_kernel, depth, heads),
-        out_shape=[jax.ShapeDtypeStruct((tokens, group + pairs * wide), bf16)] * SPLIT
-        + [jax.ShapeDtypeStruct((tokens, group), bf16)] * SPLIT
+        out_shape=[jax.ShapeDtypeStruct((tokens, 2 * group + pairs * wide), bf16)] * SPLIT
         + [jax.ShapeDtypeStruct((tokens, wide), f32)],
-        in_specs=[SMEM] + [VMEM] * 5,
-        out_specs=[VMEM] * (2 * SPLIT + 1),
-        scratch_shapes=[pltpu.VMEM((SPLIT, tokens, pairs * wide), bf16)],
-        compiler_params=pltpu.CompilerParams(vmem_limit_bytes=16 * 2**20),
+        in_specs=[SMEM] + [HBM] * 5,
+        out_specs=[VMEM] * (SPLIT + 1),
+        scratch_shapes=[
+            pltpu.VMEM((tokens, width), bf16),
+            pltpu.VMEM((tokens, width), bf16),
+            pltpu.VMEM((wide // 2, width), bf16),
+            pltpu.VMEM((SPLIT, tokens, pairs * wide), bf16),
+            pltpu.SemaphoreType.DMA((3 + 2 * SPLIT,)),
+        ],
+        compiler_params=pltpu.CompilerParams(vmem_limit_bytes=int(53.2 * 2**20)),
         name="prepare",
     )(
         index,
@@ -275,36 +315,49 @@
         keys.reshape(tokens, width),
         values.reshape(tokens, width),
         stream.reshape(tokens, width),
-        head_weight,
+        head_weight.T,
     )
-    kv, q, streamed = prepared[:SPLIT], prepared[SPLIT : 2 * SPLIT], prepared[-1]
-    kv = [kv[0]] + [exchanged(kv[step], step << 2) for step in range(1, SPLIT)]
-    q = [q[0]] + [exchanged(q[step], step << 2) for step in range(1, SPLIT)]
-    mine = jnp.concatenate(kv, axis=0)
-    blocks = [mine]
-    for member in range(1, members):
-        if member & 1 == 0 or member == 1:
-            blocks.append(exchanged(mine, rest_mask(member)))
-        else:
-            blocks.append(exchanged(blocks[member - 1], 1))
-
+    mine, streamed = prepared[:SPLIT], prepared[-1]
+    mine = [mine[0]] + [exchanged(mine[step], step << 2) for step in range(1, SPLIT)]
+
+    def spread(pieces):
+        blocks = [jnp.concatenate([piece[:, :-group] for piece in pieces], axis=0)]
+        for member in range(1, members):
+            if member & 1 == 0 or member == 1:
+                blocks.append(exchanged(blocks[0], rest_mask(member)))
+            else:
+                blocks.append(exchanged(blocks[member - 1], 1))
+        return blocks
+
+    near, far = spread(mine[:2]), spread(mine[2:])
+    limit = pltpu.CompilerParams(vmem_limit_bytes=(12 + 2 * members // 4 * 4) * 2**20)
+    state = jax.ShapeDtypeStruct((heads, SPLIT * tokens, wide), f32)
+    carried = pl.pallas_call(
+        functools.partial(attend_kernel, depth, heads, False),
+        out_shape=[state] * 3,
+        in_specs=[VMEM] * (SPLIT + members),
+        out_specs=[VMEM] * 3,
+        compiler_params=limit,
+        name="attend_near",
+    )(*mine, *near)
     part = pl.pallas_call(
-        functools.partial(attend_kernel, depth, heads),
+        functools.partial(attend_kernel, depth, heads, True),
         out_shape=jax.ShapeDtypeStruct((SPLIT * tokens // 2, wide), f32),
-        in_specs=[VMEM] * (SPLIT + members + 1),
+        in_specs=[VMEM] * (SPLIT + members + 4),
         out_specs=VMEM,
-        compiler_params=pltpu.CompilerParams(vmem_limit_bytes=(16 + 2 * members // 4 * 4) * 2**20),
-        name="attend",
-    )(*q, *blocks, streamed)
+        compiler_params=limit,
+        name="attend_far",
+    )(*mine, *far, streamed, *carried)
 
     others = [exchanged(part, step << 2) for step in range(1, SPLIT)]
     patch = pl.pallas_call(
-        functools.partial(gather_kernel, cols),
-        out_shape=jax.ShapeDtypeStruct((part.shape[0], 2 * wide), bf16),
-        in_specs=[VMEM] * 5,
+        gather_kernel,
+        out_shape=jax.ShapeDtypeStruct(part.shape, bf16),
+        in_specs=[VMEM] * 4,
         out_specs=VMEM,
+        compiler_params=pltpu.CompilerParams(vmem_limit_bytes=4 * 2**20),
         name="gather",
-    )(part, *others, chooser(latent))
+    )(part, *others)
     patches = [patch] + [exchanged(patch, rest_mask(member)) for member in range(1, members)]
 
     in_weight = widened(conv_in_weight)
@@ -313,22 +366,21 @@
     return pl.pallas_call(
         functools.partial(finish_kernel, frames, n, cols),
         out_shape=jax.ShapeDtypeStruct((frames, 2, 2 * cols, channels), bf16),
-        in_specs=[SMEM] + [VMEM] * members + [VMEM, ANY, VMEM, VMEM, VMEM],
+        in_specs=[SMEM] + [VMEM] * (members + 6),
         out_specs=VMEM,
         scratch_shapes=[
             pltpu.VMEM((frames, n + 2, cols, wide), bf16),
             pltpu.VMEM((n * cols, frames * 2 * wide), bf16),
             pltpu.VMEM((frames, n, cols, 4 * channels), f32),
             pltpu.VMEM((frames, 4, 4, cols, channels), bf16),
-            pltpu.VMEM(conv_mid_weight.shape, bf16),
             pltpu.VMEM((frames, 2, channels // 128, 2 * cols, 128), f32),
-            pltpu.SemaphoreType.DMA((conv_mid_weight.shape[0],)),
         ],
-        compiler_params=pltpu.CompilerParams(vmem_limit_bytes=(30 if n <= 16 else 52) * 2**20),
+        compiler_params=pltpu.CompilerParams(vmem_limit_bytes=(16 if n <= 16 else 40) * 2**20),
         name="finish",
     )(
         index,
         *patches,
+        chooser(latent),
         in_weight,
         conv_mid_weight,
         grouped,

time: 63.9 us -> 50.9 us (0.80)
  local copies, waits for them, and re-layouts: 10.6 us -> 0.22 us
  starting transfers between devices: 19.5 us -> 16.6 us
  waiting for transfers between devices: 20.2 us -> 19 us
  other arithmetic: 1.61 us -> 2.52 us
    unnamed x30 -> x8, local copies, waits for them, and re-layouts: 10.4 us -> 0.03 us
    ppermute x15, starting transfers between devices: 19.5 us -> 16.6 us  [exchanged(): return lax.ppermute(value, 'seq', pairs)]
    pallas_call x1, Pallas kernels: 0.49 us -> 2.35 us  [shards(): pl.pallas_call(functools.partial(prepare_kernel, depth, heads), out_shape...]
    concatenate x1, other arithmetic: 0.28 us -> 1.84 us  [widened(): whole = jnp.concatenate(blocks, axis=-1)]
    ppermute x15, waiting for transfers between devices: 20.2 us -> 19 us  [exchanged(): return lax.ppermute(value, 'seq', pairs)]
    pallas_call x1, Pallas kernels: 7.05 us -> 5.93 us  [shards(): pl.pallas_call(functools.partial(finish_kernel, frames, n, cols), out_sha...]
    convert_element_type x1, other arithmetic: 0.95 us -> 0.27 us  [chooser(): return same.astype(jnp.bfloat16)]
    pallas_call x2 -> x3, Pallas kernels: 3.93 us -> 3.8 us  [the longest x1 2.19 us: shards(): pl.pallas_call(functools.partial(attend_kernel, depth, heads, True), out_...]
  transfers between devices with their start and end apart: 15 -> 15, of which waited for: 7 -> 7; matrix products, arithmetic and copies ran while one was open for 3% -> 5% of each run, Pallas kernels for 0% -> 3%
where the time goes in v2:
time: 50.9 us; the launch traced here: 50.7 us
  waiting for transfers between devices  19 us (37%)
  starting transfers between devices  16.6 us (33%)
  Pallas kernels  12.1 us (24%)
  other arithmetic  2.52 us (5%)
    ppermute x15, waiting for transfers between devices, exchanged(): return lax.ppermute(value, 'seq', pairs)  19 us
    ppermute x15, starting transfers between devices, exchanged(): return lax.ppermute(value, 'seq', pairs)  16.6 us
    pallas_call x1, Pallas kernels, shards(): pl.pallas_call(functools.partial(finish_kernel, frames, n, cols), out_sha...  5.93 us
    pallas_call x1, Pallas kernels, shards(): pl.pallas_call(functools.partial(prepare_kernel, depth, heads), out_shape...  2.35 us
    pallas_call x1, Pallas kernels, shards(): pl.pallas_call(functools.partial(attend_kernel, depth, heads, True), out_...  2.19 us
    concatenate x1, other arithmetic, widened(): whole = jnp.concatenate(blocks, axis=-1)  1.84 us
    pallas_call x1, Pallas kernels, shards(): pl.pallas_call(functools.partial(attend_kernel, depth, heads, False), out...  1.52 us
  transfers between devices with their start and end apart: 15, of which 7 were waited for; matrix products, arithmetic and copies ran while one was open for 5% of the time, Pallas kernels for 3%

profile of v2, /device:TPU:0, one launch (start us, length us, event | category | flops | bytes accessed | tf_op | source)
XLA Modules:
  0.0 50.7 jit_solution(12550128514983115540)
XLA Ops:
  0.0 2.3 %prepare.1 = (bf16[48,1664]{1,0:T(8,128)(2,1)S(1)}, bf16[48,1664]{1,0:T(8,128)(2,1)S(1)}, bf16[48,1664]{1,0:T(8,128)(2,1)S(1)}, bf16[48,1664]{1,0:T(8,128)(2,1)S(1)}, f32[48,128]{1,0:T(8,128)S(1)}) custom-call(s32[1]{0:T(128)} %bitcast.index, bf16[48,2560]{1,0:T(8,128)(2,1)} %bitcast.11, bf16[48,2560]{1,0:T(8,128)(2,1)} %bitcast.12, ...), custom_call_target="tpu_custom_call" | custom-call | tf_op jit(solution)/shard_map/prepare/pallas_call | solution.py:297
  2.4 3.1 %collective-permute-start = (bf16[48,1664]{1,0:T(8,128)(2,1)S(1)}, bf16[48,1664]{1,0:T(8,128)(2,1)S(1)}, u32[]{:S(2)}, u32[]{:S(2)}) collective-permute-start(bf16[48,1664]{1,0:T(8,128)(2,1)S(1)} %get-tuple-element.14), channel_id=1, source_target_pairs={{0,4},{1,5},{2,6},{3,7},{4,0},{5,1},{6,2},{7,3},{8,12},{9,13},{10,... | collective-permute-start | bytes 479240 | tf_op jit(solution)/shard_map/ppermute | solution.py:22
  5.4 2.6 %collective-permute-start.1 = (bf16[48,1664]{1,0:T(8,128)(2,1)S(1)}, bf16[48,1664]{1,0:T(8,128)(2,1)S(1)}, u32[]{:S(2)}, u32[]{:S(2)}) collective-permute-start(bf16[48,1664]{1,0:T(8,128)(2,1)S(1)} %get-tuple-element.15), channel_id=1, source_target_pairs={{0,8},{1,9},{2,10},{3,11},{4,12},{5,13},{6,14},{7,15},{8,0},{9,1},... | collective-permute-start | bytes 479240 | tf_op jit(solution)/shard_map/ppermute | solution.py:22
  8.0 1.8 %fusion.7 = bf16[3,4,4,16,1536]{4,3,2,1,0:T(8,128)(2,1)S(1)} fusion(bf16[3,3,3,16,384]{4,3,2,1,0:T(8,128)(2,1)} %param.14), kind=kLoop, calls=%fused_computation.13 | loop fusion | flops 23592960 | bytes 2691072 | tf_op jit(solution)/shard_map/concatenate | solution.py:257
  9.9 0.0 slice-start
  9.9 0.1 slice.27
  10.1 0.0 slice-start.1
  10.1 0.2 pad_maximum_fusion
  10.4 1.6 %collective-permute-done.refs_1_ = bf16[48,1664]{1,0:T(8,128)(2,1)S(1)} collective-permute-done((bf16[48,1664]{1,0:T(8,128)(2,1)S(1)}, bf16[48,1664]{1,0:T(8,128)(2,1)S(1)}, u32[]{:S(2)}, u32[]{:S(2)}) %collective-permute-start) | collective-permute-done | bytes 159776 | tf_op jit(solution)/shard_map/ppermute | solution.py:22
  11.9 1.8 %collective-permute-start.7 = (bf16[96,1024]{1,0:T(8,128)(2,1)S(1)}, bf16[96,1024]{1,0:T(8,128)(2,1)S(1)}, u32[]{:S(2)}, u32[]{:S(2)}) collective-permute-start(bf16[96,1024]{1,0:T(8,128)(2,1)S(1)} %pad_maximum_fusion.2.refs_4_), channel_id=1, source_target_pairs={{0,2},{1,3},{2,0},{3,1},{4,6},{5,7},{6,4},{7,5},{8,10},{9,11},{10,... | collective-permute-start | bytes 589832 | tf_op jit(solution)/shard_map/ppermute | solution.py:22
  13.7 6.5 %collective-permute-done.1.refs_2_ = bf16[48,1664]{1,0:T(8,128)(2,1)S(1)} collective-permute-done((bf16[48,1664]{1,0:T(8,128)(2,1)S(1)}, bf16[48,1664]{1,0:T(8,128)(2,1)S(1)}, u32[]{:S(2)}, u32[]{:S(2)}) %collective-permute-start.1) | collective-permute-done | bytes 159776 | tf_op jit(solution)/shard_map/ppermute | solution.py:22
  20.3 1.6 %collective-permute-start.4 = (bf16[96,1024]{1,0:T(8,128)(2,1)S(1)}, bf16[96,1024]{1,0:T(8,128)(2,1)S(1)}, u32[]{:S(2)}, u32[]{:S(2)}) collective-permute-start(bf16[96,1024]{1,0:T(8,128)(2,1)S(1)} %pad_maximum_fusion.1.refs_4_), channel_id=1, source_target_pairs={{0,2},{1,3},{2,0},{3,1},{4,6},{5,7},{6,4},{7,5},{8,10},{9,11},{10,... | collective-permute-start | bytes 589832 | tf_op jit(solution)/shard_map/ppermute | solution.py:22
  21.9 0.1 collective-permute-start.6
  22.0 0.5 collective-permute-start.3
  22.5 0.1 collective-permute-start.8
  22.6 3.5 %collective-permute-done.4.refs_6_ = bf16[96,1024]{1,0:T(8,128)(2,1)S(1)} collective-permute-done((bf16[96,1024]{1,0:T(8,128)(2,1)S(1)}, bf16[96,1024]{1,0:T(8,128)(2,1)S(1)}, u32[]{:S(2)}, u32[]{:S(2)}) %collective-permute-start.4) | collective-permute-done | bytes 196640 | tf_op jit(solution)/shard_map/ppermute | solution.py:22
  26.0 0.1 compare_convert_fusion.refs_7_
  26.1 0.0 copy-start
  26.2 1.5 %attend_near.1 = (f32[5,192,128]{2,1,0:T(8,128)S(1)}, f32[5,192,128]{2,1,0:T(8,128)S(1)}, f32[5,192,128]{2,1,0:T(8,128)S(1)}) custom-call(bf16[48,1664]{1,0:T(8,128)(2,1)S(1)} %get-tuple-element.13.refs_0_, bf16[48,1664]{1,0:T(8,128)(2,1)S(1)} %collective-permute-done.refs_1_, bf16[48,1664]{1,0:T(8,128)(2,1)S(1)} %collective-permute-done.1.refs_2_, ...), custom_call_target="tpu_custom_call" | custom-call | tf_op jit(solution)/shard_map/attend_near/pallas_call | solution.py:335
  27.7 2.2 %attend_far.1.own = f32[96,128]{1,0:T(8,128)S(1)} custom-call(bf16[48,1664]{1,0:T(8,128)(2,1)S(1)} %get-tuple-element.13.refs_0_, bf16[48,1664]{1,0:T(8,128)(2,1)S(1)} %collective-permute-done.refs_1_, bf16[48,1664]{1,0:T(8,128)(2,1)S(1)} %collective-permute-done.1.refs_2_, bf16[48,1664]{1,0:T(8,128)(2,1)S(1)} %collective-permute-done.2.refs_3_, ...), custom_call_target="tpu_custom_call" | custom-call | tf_op jit(solution)/shard_map/attend_far/pallas_call | solution.py:343
  29.9 3.6 %collective-permute-start.10 = (f32[96,128]{1,0:T(8,128)S(1)}, f32[96,128]{1,0:T(8,128)S(1)}, u32[]{:S(2)}, u32[]{:S(2)}) collective-permute-start(f32[96,128]{1,0:T(8,128)S(1)} %attend_far.1.own), channel_id=1, source_target_pairs={{0,8},{1,9},{2,10},{3,11},{4,12},{5,13},{6,14},{7,15},{8,0},{9,1},... | collective-permute-start | bytes 147464 | tf_op jit(solution)/shard_map/ppermute | solution.py:22
  33.6 1.3 %collective-permute-start.11 = (f32[96,128]{1,0:T(8,128)S(1)}, f32[96,128]{1,0:T(8,128)S(1)}, u32[]{:S(2)}, u32[]{:S(2)}) collective-permute-start(f32[96,128]{1,0:T(8,128)S(1)} %attend_far.1.own), channel_id=1, source_target_pairs={{0,12},{1,13},{2,14},{3,15},{4,8},{5,9},{6,10},{7,11},{8,4},{9,5},... | collective-permute-start | bytes 147464 | tf_op jit(solution)/shard_map/ppermute | solution.py:22
  34.9 2.3 %collective-permute-done.10.two = f32[96,128]{1,0:T(8,128)S(1)} collective-permute-done((f32[96,128]{1,0:T(8,128)S(1)}, f32[96,128]{1,0:T(8,128)S(1)}, u32[]{:S(2)}, u32[]{:S(2)}) %collective-permute-start.10) | collective-permute-done | bytes 49184 | tf_op jit(solution)/shard_map/ppermute | solution.py:22
  37.2 2.6 %collective-permute-done.11.three = f32[96,128]{1,0:T(8,128)S(1)} collective-permute-done((f32[96,128]{1,0:T(8,128)S(1)}, f32[96,128]{1,0:T(8,128)S(1)}, u32[]{:S(2)}, u32[]{:S(2)}) %collective-permute-start.11) | collective-permute-done | bytes 49184 | tf_op jit(solution)/shard_map/ppermute | solution.py:22
  39.8 0.1 gather.1.refs_0_
  39.9 0.1 collective-permute-start.12
  39.9 1.6 %collective-permute-start.13 = (bf16[96,128]{1,0:T(8,128)(2,1)S(1)}, bf16[96,128]{1,0:T(8,128)(2,1)S(1)}, u32[]{:S(2)}, u32[]{:S(2)}) collective-permute-start(bf16[96,128]{1,0:T(8,128)(2,1)S(1)} %gather.1.refs_0_), channel_id=1, source_target_pairs={{0,2},{1,3},{2,0},{3,1},{4,6},{5,7},{6,4},{7,5},{8,10},{9,11},{10,... | collective-permute-start | bytes 73736 | tf_op jit(solution)/shard_map/ppermute | solution.py:22
  41.5 0.3 collective-permute-start.14
  41.8 0.3 and_convert_fusion.refs_4_
  42.1 1.7 %collective-permute-done.13.refs_2_ = bf16[96,128]{1,0:T(8,128)(2,1)S(1)} collective-permute-done((bf16[96,128]{1,0:T(8,128)(2,1)S(1)}, bf16[96,128]{1,0:T(8,128)(2,1)S(1)}, u32[]{:S(2)}, u32[]{:S(2)}) %collective-permute-start.13) | collective-permute-done | bytes 24608 | tf_op jit(solution)/shard_map/ppermute | solution.py:22
  43.8 0.9 %collective-permute-done.14.refs_3_ = bf16[96,128]{1,0:T(8,128)(2,1)S(1)} collective-permute-done((bf16[96,128]{1,0:T(8,128)(2,1)S(1)}, bf16[96,128]{1,0:T(8,128)(2,1)S(1)}, u32[]{:S(2)}, u32[]{:S(2)}) %collective-permute-start.14) | collective-permute-done | bytes 24608 | tf_op jit(solution)/shard_map/ppermute | solution.py:22
  44.8 5.9 %finish.1 = bf16[3,2,32,384]{3,2,1,0:T(8,128)(2,1)} custom-call(s32[1]{0:T(128)} %bitcast.index, bf16[96,128]{1,0:T(8,128)(2,1)S(1)} %gather.1.refs_0_, bf16[96,128]{1,0:T(8,128)(2,1)S(1)} %collective-permute-done.12.refs_1_, bf16[96,128]{1,0:T(8,128)(2,1)S(1)} %collective-permute-done.13.refs_2_, bf16[96,128]{1,0:T(8,128)(2,1)S(1)} %collective-permute-done.14.refs_3_, ...), custom_call_target="tpu_custom_call" | custom-call | tf_op jit(solution)/shard_map/finish/pallas_call | solution.py:366
  (31 shorter events, 0.2 us)
Async XLA Ops:
  2.4 9.6 %collective-permute-start = (bf16[48,1664]{1,0:T(8,128)(2,1)S(1)}, bf16[48,1664]{1,0:T(8,128)(2,1)S(1)}, u32[]{:S(2)}, u32[]{:S(2)}) collective-permute-start(bf16[48,1664]{1,0:T(8,128)(2,1)S(1)} %get-tuple-element.14), channel_id=1, source_target_pairs={{0,4},{1,5},{2,6},{3,7},{4,0},{5,1},{6,2},{7,3},{8,12},{9,13},{10,... | collective-permute-start | bytes 479240 | tf_op jit(solution)/shard_map/ppermute | solution.py:22
  5.4 14.8 %collective-permute-start.1 = (bf16[48,1664]{1,0:T(8,128)(2,1)S(1)}, bf16[48,1664]{1,0:T(8,128)(2,1)S(1)}, u32[]{:S(2)}, u32[]{:S(2)}) collective-permute-start(bf16[48,1664]{1,0:T(8,128)(2,1)S(1)} %get-tuple-element.15), channel_id=1, source_target_pairs={{0,8},{1,9},{2,10},{3,11},{4,12},{5,13},{6,14},{7,15},{8,0},{9,1},... | collective-permute-start | bytes 479240 | tf_op jit(solution)/shard_map/ppermute | solution.py:22
  8.0 12.2 %collective-permute-start.2 = (bf16[48,1664]{1,0:T(8,128)(2,1)S(1)}, bf16[48,1664]{1,0:T(8,128)(2,1)S(1)}, u32[]{:S(2)}, u32[]{:S(2)}) collective-permute-start(bf16[48,1664]{1,0:T(8,128)(2,1)S(1)} %get-tuple-element.16), channel_id=1, source_target_pairs={{0,12},{1,13},{2,14},{3,15},{4,8},{5,9},{6,10},{7,11},{8,4},{9,5},... | collective-permute-start | bytes 479240 | tf_op jit(solution)/shard_map/ppermute | solution.py:22
  9.9 34.9 %slice-start = ((s8[7962624]{0:T(1024)(128)(4,1)}), s8[4194304]{0:T(1024)(128)(4,1)S(1)}, s32[]{:S(2)}) async-start(s8[7962624]{0:T(1024)(128)(4,1)} %bitcast.8), calls=%async_computation | async-start | bytes 8388608
  10.1 34.7 %slice-start.1 = ((s8[7962624]{0:T(1024)(128)(4,1)}), s8[3768320]{0:T(1024)(128)(4,1)S(1)}, s32[]{:S(2)}) async-start(s8[7962624]{0:T(1024)(128)(4,1)} %bitcast.8), calls=%async_computation.1 | async-start | bytes 7536640
  11.9 10.5 %collective-permute-start.7 = (bf16[96,1024]{1,0:T(8,128)(2,1)S(1)}, bf16[96,1024]{1,0:T(8,128)(2,1)S(1)}, u32[]{:S(2)}, u32[]{:S(2)}) collective-permute-start(bf16[96,1024]{1,0:T(8,128)(2,1)S(1)} %pad_maximum_fusion.2.refs_4_), channel_id=1, source_target_pairs={{0,2},{1,3},{2,0},{3,1},{4,6},{5,7},{6,4},{7,5},{8,10},{9,11},{10,... | collective-permute-start | bytes 589832 | tf_op jit(solution)/shard_map/ppermute | solution.py:22
  20.3 5.7 %collective-permute-start.4 = (bf16[96,1024]{1,0:T(8,128)(2,1)S(1)}, bf16[96,1024]{1,0:T(8,128)(2,1)S(1)}, u32[]{:S(2)}, u32[]{:S(2)}) collective-permute-start(bf16[96,1024]{1,0:T(8,128)(2,1)S(1)} %pad_maximum_fusion.1.refs_4_), channel_id=1, source_target_pairs={{0,2},{1,3},{2,0},{3,1},{4,6},{5,7},{6,4},{7,5},{8,10},{9,11},{10,... | collective-permute-start | bytes 589832 | tf_op jit(solution)/shard_map/ppermute | solution.py:22
  21.9 4.3 %collective-permute-start.6 = (bf16[96,1024]{1,0:T(8,128)(2,1)S(1)}, bf16[96,1024]{1,0:T(8,128)(2,1)S(1)}, u32[]{:S(2)}, u32[]{:S(2)}) collective-permute-start(bf16[96,1024]{1,0:T(8,128)(2,1)S(1)} %pad_maximum_fusion.2.refs_4_), channel_id=1, source_target_pairs={{0,1},{1,0},{2,3},{3,2},{4,5},{5,4},{6,7},{7,6},{8,9},{9,8},{10,11... | collective-permute-start | bytes 589832 | tf_op jit(solution)/shard_map/ppermute | solution.py:22
  22.0 5.7 %collective-permute-start.3 = (bf16[96,1024]{1,0:T(8,128)(2,1)S(1)}, bf16[96,1024]{1,0:T(8,128)(2,1)S(1)}, u32[]{:S(2)}, u32[]{:S(2)}) collective-permute-start(bf16[96,1024]{1,0:T(8,128)(2,1)S(1)} %pad_maximum_fusion.1.refs_4_), channel_id=1, source_target_pairs={{0,1},{1,0},{2,3},{3,2},{4,5},{5,4},{6,7},{7,6},{8,9},{9,8},{10,11... | collective-permute-start | bytes 589832 | tf_op jit(solution)/shard_map/ppermute | solution.py:22
  22.5 3.7 %collective-permute-start.8 = (bf16[96,1024]{1,0:T(8,128)(2,1)S(1)}, bf16[96,1024]{1,0:T(8,128)(2,1)S(1)}, u32[]{:S(2)}, u32[]{:S(2)}) collective-permute-start(bf16[96,1024]{1,0:T(8,128)(2,1)S(1)} %collective-permute-done.7.refs_6_), channel_id=1, source_target_pairs={{0,1},{1,0},{2,3},{3,2},{4,5},{5,4},{6,7},{7,6},{8,9},{9,8},{10,11... | collective-permute-start | bytes 589832 | tf_op jit(solution)/shard_map/ppermute | solution.py:22
  26.0 1.7 %collective-permute-start.5 = (bf16[96,1024]{1,0:T(8,128)(2,1)S(1)}, bf16[96,1024]{1,0:T(8,128)(2,1)S(1)}, u32[]{:S(2)}, u32[]{:S(2)}) collective-permute-start(bf16[96,1024]{1,0:T(8,128)(2,1)S(1)} %collective-permute-done.4.refs_6_), channel_id=1, source_target_pairs={{0,1},{1,0},{2,3},{3,2},{4,5},{5,4},{6,7},{7,6},{8,9},{9,8},{10,11... | collective-permute-start | bytes 589832 | tf_op jit(solution)/shard_map/ppermute | solution.py:22
  26.1 15.9 %copy-start = (f32[384]{0:T(512)S(1)}, f32[384]{0:T(512)}, u32[]{:S(2)}) copy-start(f32[384]{0:T(512)} %param.15) | copy-start | bytes 4612
  26.2 15.9 %copy-start.1 = (f32[384]{0:T(512)S(1)}, f32[384]{0:T(512)}, u32[]{:S(2)}) copy-start(f32[384]{0:T(512)} %param.16) | copy-start | bytes 4612
  29.9 7.3 %collective-permute-start.10 = (f32[96,128]{1,0:T(8,128)S(1)}, f32[96,128]{1,0:T(8,128)S(1)}, u32[]{:S(2)}, u32[]{:S(2)}) collective-permute-start(f32[96,128]{1,0:T(8,128)S(1)} %attend_far.1.own), channel_id=1, source_target_pairs={{0,8},{1,9},{2,10},{3,11},{4,12},{5,13},{6,14},{7,15},{8,0},{9,1},... | collective-permute-start | bytes 147464 | tf_op jit(solution)/shard_map/ppermute | solution.py:22
  33.6 6.2 %collective-permute-start.11 = (f32[96,128]{1,0:T(8,128)S(1)}, f32[96,128]{1,0:T(8,128)S(1)}, u32[]{:S(2)}, u32[]{:S(2)}) collective-permute-start(f32[96,128]{1,0:T(8,128)S(1)} %attend_far.1.own), channel_id=1, source_target_pairs={{0,12},{1,13},{2,14},{3,15},{4,8},{5,9},{6,10},{7,11},{8,4},{9,5},... | collective-permute-start | bytes 147464 | tf_op jit(solution)/shard_map/ppermute | solution.py:22
  34.9 4.9 %collective-permute-start.9 = (f32[96,128]{1,0:T(8,128)S(1)}, f32[96,128]{1,0:T(8,128)S(1)}, u32[]{:S(2)}, u32[]{:S(2)}) collective-permute-start(f32[96,128]{1,0:T(8,128)S(1)} %attend_far.1.own), channel_id=1, source_target_pairs={{0,4},{1,5},{2,6},{3,7},{4,0},{5,1},{6,2},{7,3},{8,12},{9,13},{10,... | collective-permute-start | bytes 147464 | tf_op jit(solution)/shard_map/ppermute | solution.py:22
  39.9 2.3 %collective-permute-start.12 = (bf16[96,128]{1,0:T(8,128)(2,1)S(1)}, bf16[96,128]{1,0:T(8,128)(2,1)S(1)}, u32[]{:S(2)}, u32[]{:S(2)}) collective-permute-start(bf16[96,128]{1,0:T(8,128)(2,1)S(1)} %gather.1.refs_0_), channel_id=1, source_target_pairs={{0,1},{1,0},{2,3},{3,2},{4,5},{5,4},{6,7},{7,6},{8,9},{9,8},{10,11... | collective-permute-start | bytes 73736 | tf_op jit(solution)/shard_map/ppermute | solution.py:22
  39.9 3.9 %collective-permute-start.13 = (bf16[96,128]{1,0:T(8,128)(2,1)S(1)}, bf16[96,128]{1,0:T(8,128)(2,1)S(1)}, u32[]{:S(2)}, u32[]{:S(2)}) collective-permute-start(bf16[96,128]{1,0:T(8,128)(2,1)S(1)} %gather.1.refs_0_), channel_id=1, source_target_pairs={{0,2},{1,3},{2,0},{3,1},{4,6},{5,7},{6,4},{7,5},{8,10},{9,11},{10,... | collective-permute-start | bytes 73736 | tf_op jit(solution)/shard_map/ppermute | solution.py:22
  41.5 3.3 %collective-permute-start.14 = (bf16[96,128]{1,0:T(8,128)(2,1)S(1)}, bf16[96,128]{1,0:T(8,128)(2,1)S(1)}, u32[]{:S(2)}, u32[]{:S(2)}) collective-permute-start(bf16[96,128]{1,0:T(8,128)(2,1)S(1)} %gather.1.refs_0_), channel_id=1, source_target_pairs={{0,3},{1,2},{2,1},{3,0},{4,7},{5,6},{6,5},{7,4},{8,11},{9,10},{10,... | collective-permute-start | bytes 73736 | tf_op jit(solution)/shard_map/ppermute | solution.py:22

commit v3 on v2

--- a/solution.py
+++ b/solution.py
@@ -30,42 +30,43 @@
     return jnp.dot(left, right, preferred_element_type=jnp.float32)
 
 
-def prepare_kernel(depth, heads, index, q, k, v, s, w, *refs):
-    out, refs = refs[:SPLIT], refs[SPLIT:]
-    stream_out, v_here, s_here, w_here, projected, sem = refs
+def through_twice(rows, weight, columns):
+    part = weight[:, columns]
+    return lax.dot_general(
+        rows[:, columns],
+        jnp.concatenate([part, part], axis=0),
+        (((1,), (1,)), ((), ())),
+        preferred_element_type=jnp.float32,
+    )
+
+
+def prepare_kernel(depth, heads, index, q, k, v, w, *refs):
+    kv_out, q_out, refs = refs[:SPLIT], refs[SPLIT : 2 * SPLIT], refs[2 * SPLIT :]
+    v_here, w_here, projected, sem = refs
     tokens = q.shape[0]
     group = heads * depth
     place = (index[0] >> 2) & 3
     whole = [
         pltpu.make_async_copy(source, target, sem.at[at])
-        for at, (source, target) in enumerate(((v, v_here), (w, w_here), (s, s_here)))
+        for at, (source, target) in enumerate(((v, v_here), (w, w_here)))
     ]
     parts = []
     for step in range(SPLIT):
         columns = pl.ds(pl.multiple_of((place ^ step) * group, 128), group)
         at = len(whole) + 2 * step
-        parts.append(pltpu.make_async_copy(k.at[:, columns], out[step].at[:, :group], sem.at[at]))
-        parts.append(pltpu.make_async_copy(q.at[:, columns], out[step].at[:, -group:], sem.at[at + 1]))
+        parts.append(pltpu.make_async_copy(k.at[:, columns], kv_out[step].at[:, :group], sem.at[at]))
+        parts.append(pltpu.make_async_copy(q.at[:, columns], q_out[step], sem.at[at + 1]))
     for copy in whole + parts:
         copy.start()
     half = w.shape[0]
     wide = 2 * half
     low = lax.broadcasted_iota(jnp.int32, (tokens, wide), 1) < half
 
-    def through(rows, columns):
-        weight = w_here[:, columns]
-        return lax.dot_general(
-            rows[:, columns],
-            jnp.concatenate([weight, weight], axis=0),
-            (((1,), (1,)), ((), ())),
-            preferred_element_type=jnp.float32,
-        )
-
     def head_through(head):
-        return through(v_here, slice(head * depth, (head + 1) * depth))
-
-    whole[0].wait()
-    whole[1].wait()
+        return through_twice(v_here, w_here, slice(head * depth, (head + 1) * depth))
+
+    for copy in whole:
+        copy.wait()
     for owner in range(SPLIT):
         for pair in range((heads + 1) // 2):
             first = owner * heads + 2 * pair
@@ -74,57 +75,73 @@
                 both = jnp.where(low, both, head_through(first + 1))
             projected[owner, :, pair * wide : (pair + 1) * wide] = both.astype(jnp.bfloat16)
     for step in range(SPLIT):
-        out[step][:, group:-group] = projected[place ^ step]
-    whole[2].wait()
-    stream_out[...] = through(s_here, slice(None))
+        kv_out[step][:, group:] = projected[place ^ step]
     for copy in parts:
         copy.wait()
+
+
+def stream_kernel(s, w, out):
+    out[...] = through_twice(s, w, slice(None))
 
 
 def attend_kernel(depth, heads, last, *refs):
     q, refs = refs[:SPLIT], refs[SPLIT:]
     if last:
-        kv, (stream, top_in, total_in, mixed_in, out) = refs[:-5], refs[-5:]
+        kv, (stream, top_in, mixed_in, out) = refs[:-4], refs[-4:]
     else:
-        kv, (top_out, total_out, mixed_out) = refs[:-3], refs[-3:]
+        kv, (top_out, mixed_out) = refs[:-2], refs[-2:]
     tokens = q[0].shape[0]
     group = heads * depth
     wide = 128
     factor = 1.4426950408889634 / depth**0.5
     rows = SPLIT * tokens
+    half = rows // 2
     low = lax.broadcasted_iota(jnp.int32, (rows, wide), 1) < wide // 2
-    summed = jnp.zeros((rows, wide), jnp.float32)
-    for head in range(heads):
+    keys = sum(piece.shape[0] for piece in kv)
+    ones = jnp.ones((keys, wide), jnp.bfloat16)
+
+    def scores_of(head):
         columns = slice(head * depth, (head + 1) * depth)
         at = q[0].shape[1] - group + head * depth
         query = jnp.concatenate([piece[:, at : at + depth] for piece in q], axis=0)
         key = jnp.concatenate([piece[:, columns] for piece in kv], axis=0)
+        return lax.dot_general(query, key, (((1,), (1,)), ((), ())), preferred_element_type=jnp.float32)
+
+    summed = jnp.zeros((rows, wide), jnp.float32)
+    upcoming = scores_of(0)
+    for head in range(heads):
+        scores = upcoming
+        if head + 1 < heads:
+            upcoming = scores_of(head + 1)
+        top = jnp.broadcast_to(jnp.max(scores, axis=1, keepdims=True), (rows, wide))
+        if last:
+            before = top_in[head]
+            top = jnp.maximum(top, before)
+        expo = jnp.concatenate(
+            [
+                jnp.exp2((scores[:, at : at + wide] - top) * factor).astype(jnp.bfloat16)
+                for at in range(0, keys, wide)
+            ],
+            axis=1,
+        )
         at = group + (head // 2) * wide
         value = jnp.concatenate([piece[:, at : at + wide] for piece in kv], axis=0)
-        scores = lax.dot_general(query, key, (((1,), (1,)), ((), ())), preferred_element_type=jnp.float32)
-        top = jnp.max(scores, axis=1, keepdims=True)
-        if last:
-            before = top_in[head]
-            top = jnp.maximum(top, before[:, :1])
-        expo = jnp.exp2((scores - top) * factor)
-        total = jnp.sum(expo, axis=1, keepdims=True)
-        mixed = dot(expo.astype(jnp.bfloat16), value)
+        mixed = dot(expo, jnp.concatenate([value, ones], axis=1))
         if not last:
-            top_out[head] = jnp.broadcast_to(top, (rows, wide))
-            total_out[head] = jnp.broadcast_to(total, (rows, wide))
+            top_out[head] = top
             mixed_out[head] = mixed
             continue
         decay = jnp.exp2((before - top) * factor)
-        mixed = (mixed + mixed_in[head] * decay) * (1.0 / (total + total_in[head] * decay))
+        weighed = mixed[:, :wide] + mixed_in[head, :, :wide] * decay
+        total = mixed[:, wide:] + mixed_in[head, :, wide:] * decay
         mine = low if head % 2 == 0 else jnp.logical_not(low)
-        summed = summed + jnp.where(mine, mixed, 0.0)
+        summed = summed + jnp.where(mine, weighed / total, 0.0)
     if not last:
         return
     summed = summed + pltpu.roll(summed, wide // 2, 1)
-    half = rows // 2
     upper = summed[:half]
     upper = jnp.concatenate([upper[:tokens] + stream[...], upper[tokens:]], axis=0)
-    out[...] = jnp.where(low[:half], upper, summed[half:])
+    out[...] = jnp.where(low[:half], upper, summed[half:]).astype(out.dtype)
 
 
 def gather_kernel(own, one, two, three, out):
@@ -134,8 +151,9 @@
     def swap_rows(x):
         return jnp.concatenate([x[half:], x[:half]], axis=0)
 
-    far = two[...] + swap_rows(three[...])
-    latent = (own[...] + swap_rows(one[...])) + pltpu.roll(far, wide // 2, 1)
+    own, one, two, three = (ref[...].astype(jnp.float32) for ref in (own, one, two, three))
+    far = two + swap_rows(three)
+    latent = (own + swap_rows(one)) + pltpu.roll(far, wide // 2, 1)
     out[...] = latent.astype(jnp.bfloat16)
 
 
@@ -176,7 +194,11 @@
             stacked[r * cols : r * cols + chunk, t * depth : t * depth + wide] = near.reshape(chunk, wide)
             stacked[r * cols : r * cols + chunk, t * depth + wide : (t + 1) * depth] = far.reshape(chunk, wide)
 
+    counted = 4.0 * frames * cells
+    members_of = channels // GROUPS
     sums = jnp.zeros((8, channels), jnp.float32)
+    squares = jnp.zeros((8, channels), jnp.float32)
+    pivot = None
     for t in range(frames):
         for r in range(0, n, rows_in):
             for part in range(4):
@@ -186,23 +208,28 @@
                     in_weight[(frames - 1 - t) * depth :, lanes],
                 )
                 first[t, r : r + rows_in, :, lanes] = here.reshape(rows_in, cols, channels)
-                sums = sums + jnp.sum(here.reshape(chunk // 8, 8, channels), axis=0)
-    counted = 4.0 * frames * cells * (channels // GROUPS)
-
-    def over_group(eight):
-        line = jnp.sum(eight, axis=0, keepdims=True)
-        return jnp.dot(line, grouped[...], precision=lax.Precision.HIGHEST, preferred_element_type=jnp.float32)
-
-    mean = over_group(sums) / counted
-    squares = jnp.zeros((8, channels), jnp.float32)
-    for t in range(frames):
-        for r in range(0, n, rows_in):
-            for part in range(4):
-                lanes = slice(part * channels, (part + 1) * channels)
-                off = first[t, r : r + rows_in, :, lanes].reshape(chunk, channels) - mean
-                squares = squares + jnp.sum((off * off).reshape(chunk // 8, 8, channels), axis=0)
-    variance = over_group(squares) / counted
-    slope = gain[...] * (1.0 / jnp.sqrt(variance + EPS))
+                if pivot is None:
+                    pivot = jnp.sum(here, axis=0, keepdims=True) / chunk
+                off = (here - pivot).reshape(chunk // 8, 8, channels)
+                sums = sums + jnp.sum(off, axis=0)
+                squares = squares + jnp.sum(off * off, axis=0)
+
+    def over_group(line):
+        high = line.astype(jnp.bfloat16)
+        rest = line - high.astype(jnp.float32)
+        middle = rest.astype(jnp.bfloat16)
+        lower = (rest - middle.astype(jnp.float32)).astype(jnp.bfloat16)
+        none = jnp.zeros((13, channels), jnp.bfloat16)
+        terms = jnp.concatenate([high, middle, lower, none], axis=0)
+        return jnp.sum(dot(terms, grouped[...])[:8], axis=0, keepdims=True)
+
+    offset = jnp.sum(sums, axis=0, keepdims=True) / counted
+    channel_mean = pivot + offset
+    mean = over_group(channel_mean) / members_of
+    apart = channel_mean - mean
+    within = jnp.sum(squares, axis=0, keepdims=True) / counted - offset * offset
+    variance = over_group(within + apart * apart) / members_of
+    slope = gain[...] / jnp.sqrt(variance + EPS)
     bias = shift[...]
 
     place = lax.broadcasted_iota(jnp.int32, (cols, channels), 0)
@@ -212,13 +239,13 @@
             token_row = me - 1 if line == 0 else (me + 1 if line == 3 else me)
             inside = jnp.logical_and(token_row >= 0, token_row < n)
             token_row = jnp.clip(token_row, 0, n - 1)
-            keep = jnp.where(inside, 1.0, 0.0)
+            keep = jnp.where(inside, 0.5, 0.0)
             pair = []
             for side in range(2):
                 part = sub * 2 + side
                 x = first[t, token_row, :, part * channels : (part + 1) * channels]
                 y = (x - mean) * slope + bias
-                pair.append(y / (1.0 + jnp.exp(-y)) * keep)
+                pair.append((y * keep) * (1.0 + jnp.tanh(0.5 * y)))
             even, odd = pair
             taps[t, line, 0] = jnp.where(place == 0, 0.0, pltpu.roll(odd, 1, 0)).astype(jnp.bfloat16)
             taps[t, line, 1] = even.astype(jnp.bfloat16)
@@ -294,18 +321,18 @@
     index = lax.axis_index("seq").astype(jnp.int32).reshape(1)
     bf16, f32 = jnp.bfloat16, jnp.float32
 
+    head_lanes = head_weight.T
     prepared = pl.pallas_call(
         functools.partial(prepare_kernel, depth, heads),
-        out_shape=[jax.ShapeDtypeStruct((tokens, 2 * group + pairs * wide), bf16)] * SPLIT
-        + [jax.ShapeDtypeStruct((tokens, wide), f32)],
-        in_specs=[SMEM] + [HBM] * 5,
-        out_specs=[VMEM] * (SPLIT + 1),
+        out_shape=[jax.ShapeDtypeStruct((tokens, group + pairs * wide), bf16)] * SPLIT
+        + [jax.ShapeDtypeStruct((tokens, group), bf16)] * SPLIT,
+        in_specs=[SMEM] + [HBM] * 4,
+        out_specs=[VMEM] * (2 * SPLIT),
         scratch_shapes=[
-            pltpu.VMEM((tokens, width), bf16),
             pltpu.VMEM((tokens, width), bf16),
             pltpu.VMEM((wide // 2, width), bf16),
             pltpu.VMEM((SPLIT, tokens, pairs * wide), bf16),
-            pltpu.SemaphoreType.DMA((3 + 2 * SPLIT,)),
+            pltpu.SemaphoreType.DMA((2 + 2 * SPLIT,)),
         ],
         compiler_params=pltpu.CompilerParams(vmem_limit_bytes=int(53.2 * 2**20)),
         name="prepare",
@@ -314,14 +341,24 @@
         queries.reshape(tokens, width),
         keys.reshape(tokens, width),
         values.reshape(tokens, width),
-        stream.reshape(tokens, width),
-        head_weight.T,
-    )
-    mine, streamed = prepared[:SPLIT], prepared[-1]
-    mine = [mine[0]] + [exchanged(mine[step], step << 2) for step in range(1, SPLIT)]
+        head_lanes,
+    )
+    streamed = pl.pallas_call(
+        stream_kernel,
+        out_shape=jax.ShapeDtypeStruct((tokens, wide), f32),
+        in_specs=[VMEM] * 2,
+        out_specs=VMEM,
+        compiler_params=pltpu.CompilerParams(vmem_limit_bytes=4 * 2**20),
+        cost_estimate=pl.CostEstimate(flops=2 * 10**8, bytes_accessed=10**6, transcendentals=0),
+        name="stream",
+    )(stream.reshape(tokens, width), head_lanes)
+    kv, q = prepared[:SPLIT], prepared[SPLIT:]
+    kv = [kv[0]] + [exchanged(kv[step], step << 2) for step in range(1, SPLIT)]
+    pass
+    q = [q[0]] + [exchanged(q[step], step << 2) for step in range(1, SPLIT)]
 
     def spread(pieces):
-        blocks = [jnp.concatenate([piece[:, :-group] for piece in pieces], axis=0)]
+        blocks = [jnp.concatenate(pieces, axis=0)]
         for member in range(1, members):
             if member & 1 == 0 or member == 1:
                 blocks.append(exchanged(blocks[0], rest_mask(member)))
@@ -329,25 +366,27 @@
                 blocks.append(exchanged(blocks[member - 1], 1))
         return blocks
 
-    near, far = spread(mine[:2]), spread(mine[2:])
+    near = spread(kv[:2])
+    far = spread(kv[2:])
     limit = pltpu.CompilerParams(vmem_limit_bytes=(12 + 2 * members // 4 * 4) * 2**20)
-    state = jax.ShapeDtypeStruct((heads, SPLIT * tokens, wide), f32)
+    state = [jax.ShapeDtypeStruct((heads, SPLIT * tokens, size), f32) for size in (wide, 2 * wide)]
     carried = pl.pallas_call(
         functools.partial(attend_kernel, depth, heads, False),
-        out_shape=[state] * 3,
+        out_shape=state,
         in_specs=[VMEM] * (SPLIT + members),
-        out_specs=[VMEM] * 3,
+        out_specs=[VMEM] * 2,
         compiler_params=limit,
+        cost_estimate=pl.CostEstimate(flops=10**9, bytes_accessed=4 * 10**6, transcendentals=4 * 10**5),
         name="attend_near",
-    )(*mine, *near)
+    )(*q, *near)
     part = pl.pallas_call(
         functools.partial(attend_kernel, depth, heads, True),
-        out_shape=jax.ShapeDtypeStruct((SPLIT * tokens // 2, wide), f32),
-        in_specs=[VMEM] * (SPLIT + members + 4),
+        out_shape=jax.ShapeDtypeStruct((SPLIT * tokens // 2, wide), bf16),
+        in_specs=[VMEM] * (SPLIT + members + 3),
         out_specs=VMEM,
         compiler_params=limit,
         name="attend_far",
-    )(*mine, *far, streamed, *carried)
+    )(*q, *far, streamed, *carried)
 
     others = [exchanged(part, step << 2) for step in range(1, SPLIT)]
     patch = pl.pallas_call(
@@ -360,9 +399,9 @@
     )(part, *others)
     patches = [patch] + [exchanged(patch, rest_mask(member)) for member in range(1, members)]
 
+    lane = jnp.arange(channels) // (channels // GROUPS)
     in_weight = widened(conv_in_weight)
-    lane = jnp.arange(channels) // (channels // GROUPS)
-    grouped = (lane[:, None] == lane[None, :]).astype(f32)
+    grouped = (lane[:, None] == lane[None, :]).astype(bf16)
     return pl.pallas_call(
         functools.partial(finish_kernel, frames, n, cols),
         out_shape=jax.ShapeDtypeStruct((frames, 2, 2 * cols, channels), bf16),

time: 50.9 us -> 47.9 us (0.941)
  waiting for transfers between devices: 19 us -> 12.6 us
  starting transfers between devices: 16.6 us -> 22.7 us
  Pallas kernels: 12.1 us -> 9.47 us
    ppermute x15 -> x18, waiting for transfers between devices: 19 us -> 12.6 us  [exchanged(): return lax.ppermute(value, 'seq', pairs)]
    ppermute x15 -> x18, starting transfers between devices: 16.6 us -> 22.7 us  [exchanged(): return lax.ppermute(value, 'seq', pairs)]
    pallas_call x1, Pallas kernels: 2.19 us -> 1.05 us  [shards(): pl.pallas_call(functools.partial(attend_kernel, depth, heads, True), out_...]
    pallas_call x1, Pallas kernels: 1.52 us -> 0.92 us  [shards(): pl.pallas_call(functools.partial(attend_kernel, depth, heads, False), out...]
    pallas_call x1, Pallas kernels: 2.35 us -> 1.77 us  [shards(): pl.pallas_call(functools.partial(prepare_kernel, depth, heads), out_shape...]
    pallas_call x1, Pallas kernels: 5.93 us -> 5.36 us  [shards(): pl.pallas_call(functools.partial(finish_kernel, frames, n, cols), out_sha...]
  transfers between devices with their start and end apart: 15 -> 18, of which waited for: 7 -> 6; matrix products, arithmetic and copies ran while one was open for 5% -> 6% of each run, Pallas kernels for 3% -> 3%
where the time goes in v3:
time: 47.9 us; the launch traced here: 47.8 us
  starting transfers between devices  22.7 us (47%)
  waiting for transfers between devices  12.6 us (26%)
  Pallas kernels  9.47 us (20%)
  other arithmetic  2.49 us (5%)
    ppermute x18, starting transfers between devices, exchanged(): return lax.ppermute(value, 'seq', pairs)  22.7 us
    ppermute x18, waiting for transfers between devices, exchanged(): return lax.ppermute(value, 'seq', pairs)  12.6 us
    pallas_call x1, Pallas kernels, shards(): pl.pallas_call(functools.partial(finish_kernel, frames, n, cols), out_sha...  5.36 us
    concatenate x1, other arithmetic, widened(): whole = jnp.concatenate(blocks, axis=-1)  1.84 us
    pallas_call x1, Pallas kernels, shards(): pl.pallas_call(functools.partial(prepare_kernel, depth, heads), out_shape...  1.77 us
    pallas_call x1, Pallas kernels, shards(): pl.pallas_call(functools.partial(attend_kernel, depth, heads, True), out_...  1.05 us
  transfers between devices with their start and end apart: 18, of which 6 were waited for; matrix products, arithmetic and copies ran while one was open for 6% of the time, Pallas kernels for 3%

profile of v3, /device:TPU:0, one launch (start us, length us, event | category | flops | bytes accessed | tf_op | source)
XLA Modules:
  0.0 47.8 jit_solution(2882472920080286843)
XLA Ops:
  0.0 1.8 %prepare.1 = (bf16[48,1024]{1,0:T(8,128)(2,1)S(1)}, bf16[48,1024]{1,0:T(8,128)(2,1)S(1)}, bf16[48,1024]{1,0:T(8,128)(2,1)S(1)}, bf16[48,1024]{1,0:T(8,128)(2,1)S...) custom-call(s32[1]{0:T(128)} %bitcast.index, ...), custom_call_target="tpu_custom_call" | custom-call | tf_op jit(solution)/shard_map/prepare/pallas_call | solution.py:325
  1.8 3.1 %collective-permute-start.8 = (bf16[48,1024]{1,0:T(8,128)(2,1)S(1)}, bf16[48,1024]{1,0:T(8,128)(2,1)S(1)}, u32[]{:S(2)}, u32[]{:S(2)}) collective-permute-start(bf16[48,1024]{1,0:T(8,128)(2,1)S(1)} %get-tuple-element.22), channel_id=1, source_target_pairs={{0,4},{1,5},{2,6},{3,7},{4,0},{5,1},{6,2},{7,3},{8,12},{9,13},{10,... | collective-permute-start | bytes 294920 | tf_op jit(solution)/shard_map/ppermute | solution.py:22
  4.9 0.1 collective-permute-start
  4.9 3.0 %collective-permute-start.1 = (bf16[48,640]{1,0:T(8,128)(2,1)S(1)}, bf16[48,640]{1,0:T(8,128)(2,1)S(1)}, u32[]{:S(2)}, u32[]{:S(2)}) collective-permute-start(bf16[48,640]{1,0:T(8,128)(2,1)S(1)} %get-tuple-element.17), channel_id=1, source_target_pairs={{0,8},{1,9},{2,10},{3,11},{4,12},{5,13},{6,14},{7,15},{8,0},{9,1},... | collective-permute-start | bytes 184328 | tf_op jit(solution)/shard_map/ppermute | solution.py:22
  7.9 0.0 collective-permute-start.3
  7.9 3.9 %collective-permute-start.4 = (bf16[48,1024]{1,0:T(8,128)(2,1)S(1)}, bf16[48,1024]{1,0:T(8,128)(2,1)S(1)}, u32[]{:S(2)}, u32[]{:S(2)}) collective-permute-start(bf16[48,1024]{1,0:T(8,128)(2,1)S(1)} %get-tuple-element.20), channel_id=1, source_target_pairs={{0,12},{1,13},{2,14},{3,15},{4,8},{5,9},{6,10},{7,11},{8,4},{9,5},... | collective-permute-start | bytes 294920 | tf_op jit(solution)/shard_map/ppermute | solution.py:22
  11.9 1.8 %fusion.7 = bf16[3,4,4,16,1536]{4,3,2,1,0:T(8,128)(2,1)S(1)} fusion(bf16[3,3,3,16,384]{4,3,2,1,0:T(8,128)(2,1)} %param.14), kind=kLoop, calls=%fused_computation.13 | loop fusion | flops 23592960 | bytes 2691072 | tf_op jit(solution)/shard_map/concatenate | solution.py:284
  13.7 0.1 slice.8
  13.9 0.1 compare_convert_fusion.refs_7_
  14.1 0.2 pad_maximum_fusion
  14.3 1.6 %collective-permute-start.10 = (bf16[96,1024]{1,0:T(8,128)(2,1)S(1)}, bf16[96,1024]{1,0:T(8,128)(2,1)S(1)}, u32[]{:S(2)}, u32[]{:S(2)}) collective-permute-start(bf16[96,1024]{1,0:T(8,128)(2,1)S(1)} %constant_dynamic-update-slice_fusion.2.refs_4_), channel_id=1, source_target_pairs={{0,2},{1,3},{2,0},{3,1},{4,6},{5,7},{6,4},{7,5},{8,10},{9,11},{10,... | collective-permute-start | bytes 589832 | tf_op jit(solution)/shard_map/ppermute | solution.py:22
  15.9 3.1 %collective-permute-done.3 = bf16[48,1024]{1,0:T(8,128)(2,1)S(1)} collective-permute-done((bf16[48,1024]{1,0:T(8,128)(2,1)S(1)}, bf16[48,1024]{1,0:T(8,128)(2,1)S(1)}, u32[]{:S(2)}, u32[]{:S(2)}) %collective-permute-start.3) | collective-permute-done | bytes 98336 | tf_op jit(solution)/shard_map/ppermute | solution.py:22
  19.1 1.6 %collective-permute-start.6 = (bf16[96,1024]{1,0:T(8,128)(2,1)S(1)}, bf16[96,1024]{1,0:T(8,128)(2,1)S(1)}, u32[]{:S(2)}, u32[]{:S(2)}) collective-permute-start(bf16[96,1024]{1,0:T(8,128)(2,1)S(1)} %constant_dynamic-update-slice_fusion.refs_4_), channel_id=1, source_target_pairs={{0,2},{1,3},{2,0},{3,1},{4,6},{5,7},{6,4},{7,5},{8,10},{9,11},{10,... | collective-permute-start | bytes 589832 | tf_op jit(solution)/shard_map/ppermute | solution.py:22
  20.7 0.5 %collective-permute-start.11 = (bf16[96,1024]{1,0:T(8,128)(2,1)S(1)}, bf16[96,1024]{1,0:T(8,128)(2,1)S(1)}, u32[]{:S(2)}, u32[]{:S(2)}) collective-permute-start(bf16[96,1024]{1,0:T(8,128)(2,1)S(1)} %collective-permute-done.10.refs_6_), channel_id=1, source_target_pairs={{0,1},{1,0},{2,3},{3,2},{4,5},{5,4},{6,7},{7,6},{8,9},{9,8},{10,11... | collective-permute-start | bytes 589832 | tf_op jit(solution)/shard_map/ppermute | solution.py:22
  21.2 2.5 %collective-permute-start.2 = (bf16[48,640]{1,0:T(8,128)(2,1)S(1)}, bf16[48,640]{1,0:T(8,128)(2,1)S(1)}, u32[]{:S(2)}, u32[]{:S(2)}) collective-permute-start(bf16[48,640]{1,0:T(8,128)(2,1)S(1)} %get-tuple-element.18), channel_id=1, source_target_pairs={{0,12},{1,13},{2,14},{3,15},{4,8},{5,9},{6,10},{7,11},{8,4},{9,5},... | collective-permute-start | bytes 184328 | tf_op jit(solution)/shard_map/ppermute | solution.py:22
  23.8 1.1 %collective-permute-done.6.refs_6_ = bf16[96,1024]{1,0:T(8,128)(2,1)S(1)} collective-permute-done((bf16[96,1024]{1,0:T(8,128)(2,1)S(1)}, bf16[96,1024]{1,0:T(8,128)(2,1)S(1)}, u32[]{:S(2)}, u32[]{:S(2)}) %collective-permute-start.6) | collective-permute-done | bytes 196640 | tf_op jit(solution)/shard_map/ppermute | solution.py:22
  24.9 0.3 stream.1.refs_8_
  25.1 2.2 %collective-permute-done.2.refs_3_ = bf16[48,640]{1,0:T(8,128)(2,1)S(1)} collective-permute-done((bf16[48,640]{1,0:T(8,128)(2,1)S(1)}, bf16[48,640]{1,0:T(8,128)(2,1)S(1)}, u32[]{:S(2)}, u32[]{:S(2)}) %collective-permute-start.2) | collective-permute-done | bytes 61472 | tf_op jit(solution)/shard_map/ppermute | solution.py:22
  27.4 0.9 %attend_near.1 = (f32[5,192,128]{2,1,0:T(8,128)S(1)}, f32[5,192,256]{2,1,0:T(8,128)S(1)}) custom-call(bf16[48,640]{1,0:T(8,128)(2,1)S(1)} %get-tuple-element.15.refs_0_, bf16[48,640]{1,0:T(8,128)(2,1)S(1)} %collective-permute-done.refs_1_, bf16[48,640]{1,0:T(8,128)(2,1)S(1)} %collective-permute-done.1.refs_2_, ...), custom_call_target="tpu_custom_call" | custom-call | flops 1000000000 | bytes 4000000 | tf_op jit(solution)/shard_map/attend_near/pallas_call | solution.py:373
  28.3 1.1 %attend_far.1.own = bf16[96,128]{1,0:T(8,128)(2,1)S(1)} custom-call(bf16[48,640]{1,0:T(8,128)(2,1)S(1)} %get-tuple-element.15.refs_0_, bf16[48,640]{1,0:T(8,128)(2,1)S(1)} %collective-permute-done.refs_1_, bf16[48,640]{1,0:T(8,128)(2,1)S(1)} %collective-permute-done.1.refs_2_, bf16[48,640]{1,0:T(8,128)(2,1)S(1)} %collective-permute-done.2.refs_3_, ...), custom_call_target="tpu_custom_call" | custom-call | tf_op jit(solution)/shard_map/attend_far/pallas_call | solution.py:382
  29.4 1.0 %collective-permute-start.12 = (bf16[96,128]{1,0:T(8,128)(2,1)S(1)}, bf16[96,128]{1,0:T(8,128)(2,1)S(1)}, u32[]{:S(2)}, u32[]{:S(2)}) collective-permute-start(bf16[96,128]{1,0:T(8,128)(2,1)S(1)} %attend_far.1.own), channel_id=1, source_target_pairs={{0,4},{1,5},{2,6},{3,7},{4,0},{5,1},{6,2},{7,3},{8,12},{9,13},{10,... | collective-permute-start | bytes 73736 | tf_op jit(solution)/shard_map/ppermute | solution.py:22
  30.4 2.1 %collective-permute-start.13 = (bf16[96,128]{1,0:T(8,128)(2,1)S(1)}, bf16[96,128]{1,0:T(8,128)(2,1)S(1)}, u32[]{:S(2)}, u32[]{:S(2)}) collective-permute-start(bf16[96,128]{1,0:T(8,128)(2,1)S(1)} %attend_far.1.own), channel_id=1, source_target_pairs={{0,8},{1,9},{2,10},{3,11},{4,12},{5,13},{6,14},{7,15},{8,0},{9,1},... | collective-permute-start | bytes 73736 | tf_op jit(solution)/shard_map/ppermute | solution.py:22
  32.5 1.3 %collective-permute-start.14 = (bf16[96,128]{1,0:T(8,128)(2,1)S(1)}, bf16[96,128]{1,0:T(8,128)(2,1)S(1)}, u32[]{:S(2)}, u32[]{:S(2)}) collective-permute-start(bf16[96,128]{1,0:T(8,128)(2,1)S(1)} %attend_far.1.own), channel_id=1, source_target_pairs={{0,12},{1,13},{2,14},{3,15},{4,8},{5,9},{6,10},{7,11},{8,4},{9,5},... | collective-permute-start | bytes 73736 | tf_op jit(solution)/shard_map/ppermute | solution.py:22
  33.9 1.3 %collective-permute-done.13.two = bf16[96,128]{1,0:T(8,128)(2,1)S(1)} collective-permute-done((bf16[96,128]{1,0:T(8,128)(2,1)S(1)}, bf16[96,128]{1,0:T(8,128)(2,1)S(1)}, u32[]{:S(2)}, u32[]{:S(2)}) %collective-permute-start.13) | collective-permute-done | bytes 24608 | tf_op jit(solution)/shard_map/ppermute | solution.py:22
  35.1 3.0 %collective-permute-done.14.three = bf16[96,128]{1,0:T(8,128)(2,1)S(1)} collective-permute-done((bf16[96,128]{1,0:T(8,128)(2,1)S(1)}, bf16[96,128]{1,0:T(8,128)(2,1)S(1)}, u32[]{:S(2)}, u32[]{:S(2)}) %collective-permute-start.14) | collective-permute-done | bytes 24608 | tf_op jit(solution)/shard_map/ppermute | solution.py:22
  38.1 0.1 gather.1.refs_0_
  38.2 0.1 collective-permute-start.15
  38.3 0.6 %collective-permute-start.16 = (bf16[96,128]{1,0:T(8,128)(2,1)S(1)}, bf16[96,128]{1,0:T(8,128)(2,1)S(1)}, u32[]{:S(2)}, u32[]{:S(2)}) collective-permute-start(bf16[96,128]{1,0:T(8,128)(2,1)S(1)} %gather.1.refs_0_), channel_id=1, source_target_pairs={{0,2},{1,3},{2,0},{3,1},{4,6},{5,7},{6,4},{7,5},{8,10},{9,11},{10,... | collective-permute-start | bytes 73736 | tf_op jit(solution)/shard_map/ppermute | solution.py:22
  38.9 1.3 %collective-permute-start.17 = (bf16[96,128]{1,0:T(8,128)(2,1)S(1)}, bf16[96,128]{1,0:T(8,128)(2,1)S(1)}, u32[]{:S(2)}, u32[]{:S(2)}) collective-permute-start(bf16[96,128]{1,0:T(8,128)(2,1)S(1)} %gather.1.refs_0_), channel_id=1, source_target_pairs={{0,3},{1,2},{2,1},{3,0},{4,7},{5,6},{6,5},{7,4},{8,11},{9,10},{10,... | collective-permute-start | bytes 73736 | tf_op jit(solution)/shard_map/ppermute | solution.py:22
  40.2 0.3 and_convert_fusion.refs_4_
  40.5 1.9 %collective-permute-done.16.refs_2_ = bf16[96,128]{1,0:T(8,128)(2,1)S(1)} collective-permute-done((bf16[96,128]{1,0:T(8,128)(2,1)S(1)}, bf16[96,128]{1,0:T(8,128)(2,1)S(1)}, u32[]{:S(2)}, u32[]{:S(2)}) %collective-permute-start.16) | collective-permute-done | bytes 24608 | tf_op jit(solution)/shard_map/ppermute | solution.py:22
  42.4 5.4 %finish.1 = bf16[3,2,32,384]{3,2,1,0:T(8,128)(2,1)} custom-call(s32[1]{0:T(128)} %bitcast.index, bf16[96,128]{1,0:T(8,128)(2,1)S(1)} %gather.1.refs_0_, bf16[96,128]{1,0:T(8,128)(2,1)S(1)} %collective-permute-done.15.refs_1_, bf16[96,128]{1,0:T(8,128)(2,1)S(1)} %collective-permute-done.16.refs_2_, bf16[96,128]{1,0:T(8,128)(2,1)S(1)} %collective-permute-done.17.refs_3_, ...), custom_call_target="tpu_custom_call" | custom-call | tf_op jit(solution)/shard_map/finish/pallas_call | solution.py:405
  (40 shorter events, 0.2 us)
Async XLA Ops:
  1.8 12.5 %collective-permute-start.8 = (bf16[48,1024]{1,0:T(8,128)(2,1)S(1)}, bf16[48,1024]{1,0:T(8,128)(2,1)S(1)}, u32[]{:S(2)}, u32[]{:S(2)}) collective-permute-start(bf16[48,1024]{1,0:T(8,128)(2,1)S(1)} %get-tuple-element.22), channel_id=1, source_target_pairs={{0,4},{1,5},{2,6},{3,7},{4,0},{5,1},{6,2},{7,3},{8,12},{9,13},{10,... | collective-permute-start | bytes 294920 | tf_op jit(solution)/shard_map/ppermute | solution.py:22
  4.9 16.4 %collective-permute-start = (bf16[48,640]{1,0:T(8,128)(2,1)S(1)}, bf16[48,640]{1,0:T(8,128)(2,1)S(1)}, u32[]{:S(2)}, u32[]{:S(2)}) collective-permute-start(bf16[48,640]{1,0:T(8,128)(2,1)S(1)} %get-tuple-element.16), channel_id=1, source_target_pairs={{0,4},{1,5},{2,6},{3,7},{4,0},{5,1},{6,2},{7,3},{8,12},{9,13},{10,... | collective-permute-start | bytes 184328 | tf_op jit(solution)/shard_map/ppermute | solution.py:22
  4.9 18.8 %collective-permute-start.1 = (bf16[48,640]{1,0:T(8,128)(2,1)S(1)}, bf16[48,640]{1,0:T(8,128)(2,1)S(1)}, u32[]{:S(2)}, u32[]{:S(2)}) collective-permute-start(bf16[48,640]{1,0:T(8,128)(2,1)S(1)} %get-tuple-element.17), channel_id=1, source_target_pairs={{0,8},{1,9},{2,10},{3,11},{4,12},{5,13},{6,14},{7,15},{8,0},{9,1},... | collective-permute-start | bytes 184328 | tf_op jit(solution)/shard_map/ppermute | solution.py:22
  7.9 11.1 %collective-permute-start.3 = (bf16[48,1024]{1,0:T(8,128)(2,1)S(1)}, bf16[48,1024]{1,0:T(8,128)(2,1)S(1)}, u32[]{:S(2)}, u32[]{:S(2)}) collective-permute-start(bf16[48,1024]{1,0:T(8,128)(2,1)S(1)} %get-tuple-element.19), channel_id=1, source_target_pairs={{0,8},{1,9},{2,10},{3,11},{4,12},{5,13},{6,14},{7,15},{8,0},{9,1},... | collective-permute-start | bytes 294920 | tf_op jit(solution)/shard_map/ppermute | solution.py:22
  7.9 11.1 %collective-permute-start.4 = (bf16[48,1024]{1,0:T(8,128)(2,1)S(1)}, bf16[48,1024]{1,0:T(8,128)(2,1)S(1)}, u32[]{:S(2)}, u32[]{:S(2)}) collective-permute-start(bf16[48,1024]{1,0:T(8,128)(2,1)S(1)} %get-tuple-element.20), channel_id=1, source_target_pairs={{0,12},{1,13},{2,14},{3,15},{4,8},{5,9},{6,10},{7,11},{8,4},{9,5},... | collective-permute-start | bytes 294920 | tf_op jit(solution)/shard_map/ppermute | solution.py:22
  13.7 28.7 %slice-start = ((s8[7962624]{0:T(1024)(128)(4,1)}), s8[4194304]{0:T(1024)(128)(4,1)S(1)}, s32[]{:S(2)}) async-start(s8[7962624]{0:T(1024)(128)(4,1)} %bitcast.8), calls=%async_computation | async-start | bytes 8388608
  14.0 10.8 %copy-start = (bf16[2560,64]{0,1:T(8,128)(2,1)S(1)}, bf16[2560,64]{0,1:T(8,128)(2,1)}, u32[]{:S(2)}) copy-start(bf16[2560,64]{0,1:T(8,128)(2,1)} %param.13) | copy-start | bytes 983044
  14.0 10.8 %copy-start.1 = (bf16[3,1,16,2560]{3,2,1,0:T(8,128)(2,1)S(1)}, bf16[3,1,16,2560]{3,2,1,0:T(8,128)(2,1)}, u32[]{:S(2)}) copy-start(bf16[3,1,16,2560]{3,2,1,0:T(8,128)(2,1)} %param.12) | copy-start | bytes 737284
  14.1 28.3 %slice-start.1 = ((s8[7962624]{0:T(1024)(128)(4,1)}), s8[3768320]{0:T(1024)(128)(4,1)S(1)}, s32[]{:S(2)}) async-start(s8[7962624]{0:T(1024)(128)(4,1)} %bitcast.8), calls=%async_computation.1 | async-start | bytes 7536640
  14.3 6.4 %collective-permute-start.10 = (bf16[96,1024]{1,0:T(8,128)(2,1)S(1)}, bf16[96,1024]{1,0:T(8,128)(2,1)S(1)}, u32[]{:S(2)}, u32[]{:S(2)}) collective-permute-start(bf16[96,1024]{1,0:T(8,128)(2,1)S(1)} %constant_dynamic-update-slice_fusion.2.refs_4_), channel_id=1, source_target_pairs={{0,2},{1,3},{2,0},{3,1},{4,6},{5,7},{6,4},{7,5},{8,10},{9,11},{10,... | collective-permute-start | bytes 589832 | tf_op jit(solution)/shard_map/ppermute | solution.py:22
  19.1 5.7 %collective-permute-start.6 = (bf16[96,1024]{1,0:T(8,128)(2,1)S(1)}, bf16[96,1024]{1,0:T(8,128)(2,1)S(1)}, u32[]{:S(2)}, u32[]{:S(2)}) collective-permute-start(bf16[96,1024]{1,0:T(8,128)(2,1)S(1)} %constant_dynamic-update-slice_fusion.refs_4_), channel_id=1, source_target_pairs={{0,2},{1,3},{2,0},{3,1},{4,6},{5,7},{6,4},{7,5},{8,10},{9,11},{10,... | collective-permute-start | bytes 589832 | tf_op jit(solution)/shard_map/ppermute | solution.py:22
  20.7 6.7 %collective-permute-start.9 = (bf16[96,1024]{1,0:T(8,128)(2,1)S(1)}, bf16[96,1024]{1,0:T(8,128)(2,1)S(1)}, u32[]{:S(2)}, u32[]{:S(2)}) collective-permute-start(bf16[96,1024]{1,0:T(8,128)(2,1)S(1)} %constant_dynamic-update-slice_fusion.2.refs_4_), channel_id=1, source_target_pairs={{0,1},{1,0},{2,3},{3,2},{4,5},{5,4},{6,7},{7,6},{8,9},{9,8},{10,11... | collective-permute-start | bytes 589832 | tf_op jit(solution)/shard_map/ppermute | solution.py:22
  20.7 6.7 %collective-permute-start.11 = (bf16[96,1024]{1,0:T(8,128)(2,1)S(1)}, bf16[96,1024]{1,0:T(8,128)(2,1)S(1)}, u32[]{:S(2)}, u32[]{:S(2)}) collective-permute-start(bf16[96,1024]{1,0:T(8,128)(2,1)S(1)} %collective-permute-done.10.refs_6_), channel_id=1, source_target_pairs={{0,1},{1,0},{2,3},{3,2},{4,5},{5,4},{6,7},{7,6},{8,9},{9,8},{10,11... | collective-permute-start | bytes 589832 | tf_op jit(solution)/shard_map/ppermute | solution.py:22
  21.2 6.1 %collective-permute-start.2 = (bf16[48,640]{1,0:T(8,128)(2,1)S(1)}, bf16[48,640]{1,0:T(8,128)(2,1)S(1)}, u32[]{:S(2)}, u32[]{:S(2)}) collective-permute-start(bf16[48,640]{1,0:T(8,128)(2,1)S(1)} %get-tuple-element.18), channel_id=1, source_target_pairs={{0,12},{1,13},{2,14},{3,15},{4,8},{5,9},{6,10},{7,11},{8,4},{9,5},... | collective-permute-start | bytes 184328 | tf_op jit(solution)/shard_map/ppermute | solution.py:22
  23.8 4.6 %collective-permute-start.5 = (bf16[96,1024]{1,0:T(8,128)(2,1)S(1)}, bf16[96,1024]{1,0:T(8,128)(2,1)S(1)}, u32[]{:S(2)}, u32[]{:S(2)}) collective-permute-start(bf16[96,1024]{1,0:T(8,128)(2,1)S(1)} %constant_dynamic-update-slice_fusion.refs_4_), channel_id=1, source_target_pairs={{0,1},{1,0},{2,3},{3,2},{4,5},{5,4},{6,7},{7,6},{8,9},{9,8},{10,11... | collective-permute-start | bytes 589832 | tf_op jit(solution)/shard_map/ppermute | solution.py:22
  24.8 3.5 %collective-permute-start.7 = (bf16[96,1024]{1,0:T(8,128)(2,1)S(1)}, bf16[96,1024]{1,0:T(8,128)(2,1)S(1)}, u32[]{:S(2)}, u32[]{:S(2)}) collective-permute-start(bf16[96,1024]{1,0:T(8,128)(2,1)S(1)} %collective-permute-done.6.refs_6_), channel_id=1, source_target_pairs={{0,1},{1,0},{2,3},{3,2},{4,5},{5,4},{6,7},{7,6},{8,9},{9,8},{10,11... | collective-permute-start | bytes 589832 | tf_op jit(solution)/shard_map/ppermute | solution.py:22
  28.3 12.1 %copy-start.2 = (f32[384]{0:T(512)S(1)}, f32[384]{0:T(512)}, u32[]{:S(2)}) copy-start(f32[384]{0:T(512)} %param.15) | copy-start | bytes 4612
  28.3 12.2 %copy-start.3 = (f32[384]{0:T(512)S(1)}, f32[384]{0:T(512)}, u32[]{:S(2)}) copy-start(f32[384]{0:T(512)} %param.16) | copy-start | bytes 4612
  29.4 4.5 %collective-permute-start.12 = (bf16[96,128]{1,0:T(8,128)(2,1)S(1)}, bf16[96,128]{1,0:T(8,128)(2,1)S(1)}, u32[]{:S(2)}, u32[]{:S(2)}) collective-permute-start(bf16[96,128]{1,0:T(8,128)(2,1)S(1)} %attend_far.1.own), channel_id=1, source_target_pairs={{0,4},{1,5},{2,6},{3,7},{4,0},{5,1},{6,2},{7,3},{8,12},{9,13},{10,... | collective-permute-start | bytes 73736 | tf_op jit(solution)/shard_map/ppermute | solution.py:22
  30.4 4.7 %collective-permute-start.13 = (bf16[96,128]{1,0:T(8,128)(2,1)S(1)}, bf16[96,128]{1,0:T(8,128)(2,1)S(1)}, u32[]{:S(2)}, u32[]{:S(2)}) collective-permute-start(bf16[96,128]{1,0:T(8,128)(2,1)S(1)} %attend_far.1.own), channel_id=1, source_target_pairs={{0,8},{1,9},{2,10},{3,11},{4,12},{5,13},{6,14},{7,15},{8,0},{9,1},... | collective-permute-start | bytes 73736 | tf_op jit(solution)/shard_map/ppermute | solution.py:22
  32.5 5.6 %collective-permute-start.14 = (bf16[96,128]{1,0:T(8,128)(2,1)S(1)}, bf16[96,128]{1,0:T(8,128)(2,1)S(1)}, u32[]{:S(2)}, u32[]{:S(2)}) collective-permute-start(bf16[96,128]{1,0:T(8,128)(2,1)S(1)} %attend_far.1.own), channel_id=1, source_target_pairs={{0,12},{1,13},{2,14},{3,15},{4,8},{5,9},{6,10},{7,11},{8,4},{9,5},... | collective-permute-start | bytes 73736 | tf_op jit(solution)/shard_map/ppermute | solution.py:22
  38.2 2.3 %collective-permute-start.15 = (bf16[96,128]{1,0:T(8,128)(2,1)S(1)}, bf16[96,128]{1,0:T(8,128)(2,1)S(1)}, u32[]{:S(2)}, u32[]{:S(2)}) collective-permute-start(bf16[96,128]{1,0:T(8,128)(2,1)S(1)} %gather.1.refs_0_), channel_id=1, source_target_pairs={{0,1},{1,0},{2,3},{3,2},{4,5},{5,4},{6,7},{7,6},{8,9},{9,8},{10,11... | collective-permute-start | bytes 73736 | tf_op jit(solution)/shard_map/ppermute | solution.py:22
  38.3 4.1 %collective-permute-start.16 = (bf16[96,128]{1,0:T(8,128)(2,1)S(1)}, bf16[96,128]{1,0:T(8,128)(2,1)S(1)}, u32[]{:S(2)}, u32[]{:S(2)}) collective-permute-start(bf16[96,128]{1,0:T(8,128)(2,1)S(1)} %gather.1.refs_0_), channel_id=1, source_target_pairs={{0,2},{1,3},{2,0},{3,1},{4,6},{5,7},{6,4},{7,5},{8,10},{9,11},{10,... | collective-permute-start | bytes 73736 | tf_op jit(solution)/shard_map/ppermute | solution.py:22
  38.9 3.5 %collective-permute-start.17 = (bf16[96,128]{1,0:T(8,128)(2,1)S(1)}, bf16[96,128]{1,0:T(8,128)(2,1)S(1)}, u32[]{:S(2)}, u32[]{:S(2)}) collective-permute-start(bf16[96,128]{1,0:T(8,128)(2,1)S(1)} %gather.1.refs_0_), channel_id=1, source_target_pairs={{0,3},{1,2},{2,1},{3,0},{4,7},{5,6},{6,5},{7,4},{8,11},{9,10},{10,... | collective-permute-start | bytes 73736 | tf_op jit(solution)/shard_map/ppermute | solution.py:22

commit v4 on v3

--- a/solution.py
+++ b/solution.py
@@ -85,16 +85,16 @@
 
 
 def attend_kernel(depth, heads, last, *refs):
-    q, refs = refs[:SPLIT], refs[SPLIT:]
+    q, refs = refs[0], refs[1:]
     if last:
         kv, (stream, top_in, mixed_in, out) = refs[:-4], refs[-4:]
     else:
         kv, (top_out, mixed_out) = refs[:-2], refs[-2:]
-    tokens = q[0].shape[0]
     group = heads * depth
     wide = 128
     factor = 1.4426950408889634 / depth**0.5
-    rows = SPLIT * tokens
+    rows = q.shape[0]
+    tokens = rows // SPLIT
     half = rows // 2
     low = lax.broadcasted_iota(jnp.int32, (rows, wide), 1) < wide // 2
     keys = sum(piece.shape[0] for piece in kv)
@@ -102,8 +102,7 @@
 
     def scores_of(head):
         columns = slice(head * depth, (head + 1) * depth)
-        at = q[0].shape[1] - group + head * depth
-        query = jnp.concatenate([piece[:, at : at + depth] for piece in q], axis=0)
+        query = q[:, columns]
         key = jnp.concatenate([piece[:, columns] for piece in kv], axis=0)
         return lax.dot_general(query, key, (((1,), (1,)), ((), ())), preferred_element_type=jnp.float32)
 
@@ -144,7 +143,14 @@
     out[...] = jnp.where(low[:half], upper, summed[half:]).astype(out.dtype)
 
 
-def gather_kernel(own, one, two, three, out):
+def collect_kernel(*refs):
+    pieces, out = refs[:-1], refs[-1]
+    tokens = pieces[0].shape[0]
+    for at, piece in enumerate(pieces):
+        out[at * tokens : (at + 1) * tokens, :] = piece[...]
+
+
+def gather_kernel(own, three, two, one, out):
     rows, wide = own.shape
     half = rows // 2
 
@@ -352,43 +358,54 @@
         cost_estimate=pl.CostEstimate(flops=2 * 10**8, bytes_accessed=10**6, transcendentals=0),
         name="stream",
     )(stream.reshape(tokens, width), head_lanes)
-    kv, q = prepared[:SPLIT], prepared[SPLIT:]
-    kv = [kv[0]] + [exchanged(kv[step], step << 2) for step in range(1, SPLIT)]
-    pass
-    q = [q[0]] + [exchanged(q[step], step << 2) for step in range(1, SPLIT)]
+    kv, q = list(prepared[:SPLIT]), list(prepared[SPLIT:])
+    both = exchanged(jnp.concatenate([kv[1], q[1]], axis=1), 1 << 2)
+    kv[1], q[1] = both[:, : kv[1].shape[1]], both[:, kv[1].shape[1] :]
+    for step in range(2, SPLIT):
+        kv[step] = exchanged(kv[step], step << 2)
+    q[2:] = lax.optimization_barrier((q[2:], both))[0]
+    for step in range(2, SPLIT):
+        q[step] = exchanged(q[step], step << 2)
 
     def spread(pieces):
-        blocks = [jnp.concatenate(pieces, axis=0)]
-        for member in range(1, members):
-            if member & 1 == 0 or member == 1:
-                blocks.append(exchanged(blocks[0], rest_mask(member)))
-            else:
-                blocks.append(exchanged(blocks[member - 1], 1))
-        return blocks
-
-    near = spread(kv[:2])
-    far = spread(kv[2:])
+        block = jnp.concatenate(pieces, axis=0)
+        return [block] + [exchanged(block, rest_mask(member)) for member in range(2, members, 2)]
+
+    near = jnp.concatenate(spread(kv[:2]), axis=0)
+    near = [near, exchanged(near, 1)]
+    far = spread(lax.optimization_barrier((kv[2:], near[0]))[0])
     limit = pltpu.CompilerParams(vmem_limit_bytes=(12 + 2 * members // 4 * 4) * 2**20)
     state = [jax.ShapeDtypeStruct((heads, SPLIT * tokens, size), f32) for size in (wide, 2 * wide)]
+    queried = pl.pallas_call(
+        collect_kernel,
+        out_shape=jax.ShapeDtypeStruct((SPLIT * tokens, group), bf16),
+        in_specs=[VMEM] * SPLIT,
+        out_specs=VMEM,
+        compiler_params=pltpu.CompilerParams(vmem_limit_bytes=4 * 2**20),
+        cost_estimate=pl.CostEstimate(flops=5 * 10**9, bytes_accessed=10**6, transcendentals=0),
+        name="collect",
+    )(*q)
     carried = pl.pallas_call(
         functools.partial(attend_kernel, depth, heads, False),
         out_shape=state,
-        in_specs=[VMEM] * (SPLIT + members),
+        in_specs=[VMEM] * (1 + len(near)),
         out_specs=[VMEM] * 2,
         compiler_params=limit,
-        cost_estimate=pl.CostEstimate(flops=10**9, bytes_accessed=4 * 10**6, transcendentals=4 * 10**5),
+        cost_estimate=pl.CostEstimate(flops=1000000000, bytes_accessed=4 * 10**6, transcendentals=4 * 10**5),
         name="attend_near",
-    )(*q, *near)
+    )(queried, *near)
+    passed = lax.optimization_barrier((far[1:], carried))[0]
+    far = far + [exchanged(block, 1) for block in [far[0]] + passed]
     part = pl.pallas_call(
         functools.partial(attend_kernel, depth, heads, True),
         out_shape=jax.ShapeDtypeStruct((SPLIT * tokens // 2, wide), bf16),
-        in_specs=[VMEM] * (SPLIT + members + 3),
+        in_specs=[VMEM] * (1 + len(far) + 3),
         out_specs=VMEM,
         compiler_params=limit,
         name="attend_far",
-    )(*q, *far, streamed, *carried)
-
-    others = [exchanged(part, step << 2) for step in range(1, SPLIT)]
+    )(queried, *far, streamed, *carried)
+
+    others = [exchanged(part, step << 2) for step in (3, 2, 1)]
     patch = pl.pallas_call(
         gather_kernel,
         out_shape=jax.ShapeDtypeStruct(part.shape, bf16),

time: 47.9 us -> 46 us (0.960)
  starting transfers between devices: 22.7 us -> 19.6 us
  local copies, waits for them, and re-layouts: 0.24 us -> 1.01 us
    ppermute x18 -> x16, starting transfers between devices: 22.7 us -> 19.6 us  [exchanged(): return lax.ppermute(value, 'seq', pairs)]
    unnamed x14 -> x13, local copies, waits for them, and re-layouts: 0.06 us -> 0.83 us
    ppermute x18 -> x16, waiting for transfers between devices: 12.6 us -> 13 us  [exchanged(): return lax.ppermute(value, 'seq', pairs)]
  transfers between devices with their start and end apart: 18 -> 16, of which waited for: 6 -> 8; matrix products, arithmetic and copies ran while one was open for 6% -> 6% of each run, Pallas kernels for 3% -> 3%
where the time goes in v4:
time: 46 us; the launch traced here: 45.9 us
  starting transfers between devices  19.6 us (43%)
  waiting for transfers between devices  13 us (28%)
  Pallas kernels  9.45 us (21%)
  other arithmetic  2.58 us (6%)
  local copies, waits for them, and re-layouts  1.01 us (2%)
    ppermute x16, starting transfers between devices, exchanged(): return lax.ppermute(value, 'seq', pairs)  19.6 us
    ppermute x16, waiting for transfers between devices, exchanged(): return lax.ppermute(value, 'seq', pairs)  13 us
    pallas_call x1, Pallas kernels, shards(): pl.pallas_call(functools.partial(finish_kernel, frames, n, cols), out_sha...  5.35 us
    concatenate x1, other arithmetic, widened(): whole = jnp.concatenate(blocks, axis=-1)  1.84 us
    pallas_call x1, Pallas kernels, shards(): pl.pallas_call(functools.partial(prepare_kernel, depth, heads), out_shape...  1.77 us
    pallas_call x1, Pallas kernels, shards(): pl.pallas_call(functools.partial(attend_kernel, depth, heads, True), out_...  1.03 us
  transfers between devices with their start and end apart: 16, of which 8 were waited for; matrix products, arithmetic and copies ran while one was open for 6% of the time, Pallas kernels for 3%

profile of v4, /device:TPU:0, one launch (start us, length us, event | category | flops | bytes accessed | tf_op | source)
XLA Modules:
  0.0 45.9 jit_solution(10296846309813902397)
XLA Ops:
  0.0 1.8 %prepare.1 = (bf16[48,1024]{1,0:T(8,128)(2,1)S(1)}, bf16[48,1024]{1,0:T(8,128)(2,1)S(1)}, bf16[48,1024]{1,0:T(8,128)(2,1)S(1)}, bf16[48,1024]{1,0:T(8,128)(2,1)S...) custom-call(s32[1]{0:T(128)} %bitcast.index, ...), custom_call_target="tpu_custom_call" | custom-call | tf_op jit(solution)/shard_map/prepare/pallas_call | solution.py:331
  1.8 3.1 %collective-permute-start = (bf16[48,1664]{1,0:T(8,128)(2,1)S(1)}, bf16[48,1664]{1,0:T(8,128)(2,1)S(1)}, u32[]{:S(2)}, u32[]{:S(2)}) collective-permute-start(bf16[48,1664]{1,0:T(8,128)(2,1)S(1)} %pad_maximum_fusion.3), channel_id=1, source_target_pairs={{0,4},{1,5},{2,6},{3,7},{4,0},{5,1},{6,2},{7,3},{8,12},{9,13},{10,... | collective-permute-start | bytes 479240 | tf_op jit(solution)/shard_map/ppermute | solution.py:22
  4.9 2.6 %collective-permute-start.3 = (bf16[48,1024]{1,0:T(8,128)(2,1)S(1)}, bf16[48,1024]{1,0:T(8,128)(2,1)S(1)}, u32[]{:S(2)}, u32[]{:S(2)}) collective-permute-start(bf16[48,1024]{1,0:T(8,128)(2,1)S(1)} %get-tuple-element.27), channel_id=1, source_target_pairs={{0,8},{1,9},{2,10},{3,11},{4,12},{5,13},{6,14},{7,15},{8,0},{9,1},... | collective-permute-start | bytes 294920 | tf_op jit(solution)/shard_map/ppermute | solution.py:22
  7.5 1.8 %fusion.7 = bf16[3,4,4,16,1536]{4,3,2,1,0:T(8,128)(2,1)S(1)} fusion(bf16[3,3,3,16,384]{4,3,2,1,0:T(8,128)(2,1)} %param.14), kind=kLoop, calls=%fused_computation.13 | loop fusion | flops 23592960 | bytes 2691072 | tf_op jit(solution)/shard_map/concatenate | solution.py:290
  9.3 0.1 slice.18
  9.5 0.2 pad_maximum_fusion
  9.8 0.7 %copy-done = bf16[2560,64]{0,1:T(8,128)(2,1)S(1)} copy-done((bf16[2560,64]{0,1:T(8,128)(2,1)S(1)}, bf16[2560,64]{0,1:T(8,128)(2,1)}, u32[]{:S(2)}) %copy-start) | copy-done | bytes 327704
  10.6 0.3 stream.1.refs_5_
  10.9 1.8 %collective-permute-start.5 = (bf16[96,1024]{1,0:T(8,128)(2,1)S(1)}, bf16[96,1024]{1,0:T(8,128)(2,1)S(1)}, u32[]{:S(2)}, u32[]{:S(2)}) collective-permute-start(bf16[96,1024]{1,0:T(8,128)(2,1)S(1)} %pad_maximum_fusion.2), channel_id=1, source_target_pairs={{0,2},{1,3},{2,0},{3,1},{4,6},{5,7},{6,4},{7,5},{8,10},{9,11},{10,... | collective-permute-start | bytes 589832 | tf_op jit(solution)/shard_map/ppermute | solution.py:22
  12.8 1.9 %collective-permute-start.1 = (bf16[48,640]{1,0:T(8,128)(2,1)S(1)}, bf16[48,640]{1,0:T(8,128)(2,1)S(1)}, u32[]{:S(2)}, u32[]{:S(2)}) collective-permute-start(bf16[48,640]{1,0:T(8,128)(2,1)S(1)} %get-tuple-element.25), channel_id=1, source_target_pairs={{0,8},{1,9},{2,10},{3,11},{4,12},{5,13},{6,14},{7,15},{8,0},{9,1},... | collective-permute-start | bytes 184328 | tf_op jit(solution)/shard_map/ppermute | solution.py:22
  14.6 2.1 %collective-permute-start.2 = (bf16[48,640]{1,0:T(8,128)(2,1)S(1)}, bf16[48,640]{1,0:T(8,128)(2,1)S(1)}, u32[]{:S(2)}, u32[]{:S(2)}) collective-permute-start(bf16[48,640]{1,0:T(8,128)(2,1)S(1)} %get-tuple-element.26), channel_id=1, source_target_pairs={{0,12},{1,13},{2,14},{3,15},{4,8},{5,9},{6,10},{7,11},{8,4},{9,5},... | collective-permute-start | bytes 184328 | tf_op jit(solution)/shard_map/ppermute | solution.py:22
  16.7 0.3 collective-permute-done.5
  17.1 0.1 collective-permute-start.8
  17.2 1.6 %collective-permute-start.6 = (bf16[96,1024]{1,0:T(8,128)(2,1)S(1)}, bf16[96,1024]{1,0:T(8,128)(2,1)S(1)}, u32[]{:S(2)}, u32[]{:S(2)}) collective-permute-start(bf16[96,1024]{1,0:T(8,128)(2,1)S(1)} %constant_dynamic-update-slice_fusion.refs_1_), channel_id=1, source_target_pairs={{0,2},{1,3},{2,0},{3,1},{4,6},{5,7},{6,4},{7,5},{8,10},{9,11},{10,... | collective-permute-start | bytes 589832 | tf_op jit(solution)/shard_map/ppermute | solution.py:22
  18.8 2.4 %collective-permute-done.1.refs_2_ = bf16[48,640]{1,0:T(8,128)(2,1)S(1)} collective-permute-done((bf16[48,640]{1,0:T(8,128)(2,1)S(1)}, bf16[48,640]{1,0:T(8,128)(2,1)S(1)}, u32[]{:S(2)}, u32[]{:S(2)}) %collective-permute-start.1) | collective-permute-done | bytes 61472 | tf_op jit(solution)/shard_map/ppermute | solution.py:22
  21.2 0.1 collective-permute-start.7
  21.3 0.9 %attend_near.1 = (f32[5,192,128]{2,1,0:T(8,128)S(1)}, f32[5,192,256]{2,1,0:T(8,128)S(1)}) custom-call(bf16[192,640]{1,0:T(8,128)(2,1)S(1)} %collect.1.refs_0_, bf16[192,1024]{1,0:T(8,128)(2,1)S(1)} %pad_maximum_fusion.1.refs_1_, bf16[192,1024]{1,0:T(8,128)(2,1)S(1)} %collective-permute-done.8.refs_2_), custom_call_target="tpu_custom_call" | custom-call | flops 1000000000 | bytes 4000000 | tf_op jit(solution)/shard_map/attend_near/pallas_call | solution.py:388
  22.3 2.3 %collective-permute-done.6.refs_2_ = bf16[96,1024]{1,0:T(8,128)(2,1)S(1)} collective-permute-done((bf16[96,1024]{1,0:T(8,128)(2,1)S(1)}, bf16[96,1024]{1,0:T(8,128)(2,1)S(1)}, u32[]{:S(2)}, u32[]{:S(2)}) %collective-permute-start.6) | collective-permute-done | bytes 196640 | tf_op jit(solution)/shard_map/ppermute | solution.py:22
  24.6 0.1 compare_convert_fusion.refs_7_
  24.7 1.3 %collective-permute-done.9.refs_4_ = bf16[96,1024]{1,0:T(8,128)(2,1)S(1)} collective-permute-done((bf16[96,1024]{1,0:T(8,128)(2,1)S(1)}, bf16[96,1024]{1,0:T(8,128)(2,1)S(1)}, u32[]{:S(2)}, u32[]{:S(2)}) %collective-permute-start.9) | collective-permute-done | bytes 196640 | tf_op jit(solution)/shard_map/ppermute | solution.py:22
  26.0 1.0 %attend_far.1.own = bf16[96,128]{1,0:T(8,128)(2,1)S(1)} custom-call(bf16[192,640]{1,0:T(8,128)(2,1)S(1)} %collect.1.refs_0_, bf16[96,1024]{1,0:T(8,128)(2,1)S(1)} %constant_dynamic-update-slice_fusion.refs_1_, bf16[96,1024]{1,0:T(8,128)(2,1)S(1)} %collective-permute-done.6.refs_2_, bf16[96,1024]{1,0:T(8,128)(2,1)S(1)} %collective-permute-done.7.refs_3_, ...), custom_call_target="tpu_custom_call" | custom-call | tf_op jit(solution)/shard_map/attend_far/pallas_call | solution.py:399
  27.1 3.7 %collective-permute-start.10 = (bf16[96,128]{1,0:T(8,128)(2,1)S(1)}, bf16[96,128]{1,0:T(8,128)(2,1)S(1)}, u32[]{:S(2)}, u32[]{:S(2)}) collective-permute-start(bf16[96,128]{1,0:T(8,128)(2,1)S(1)} %attend_far.1.own), channel_id=1, source_target_pairs={{0,12},{1,13},{2,14},{3,15},{4,8},{5,9},{6,10},{7,11},{8,4},{9,5},... | collective-permute-start | bytes 73736 | tf_op jit(solution)/shard_map/ppermute | solution.py:22
  30.8 0.8 %collective-permute-start.12 = (bf16[96,128]{1,0:T(8,128)(2,1)S(1)}, bf16[96,128]{1,0:T(8,128)(2,1)S(1)}, u32[]{:S(2)}, u32[]{:S(2)}) collective-permute-start(bf16[96,128]{1,0:T(8,128)(2,1)S(1)} %attend_far.1.own), channel_id=1, source_target_pairs={{0,4},{1,5},{2,6},{3,7},{4,0},{5,1},{6,2},{7,3},{8,12},{9,13},{10,... | collective-permute-start | bytes 73736 | tf_op jit(solution)/shard_map/ppermute | solution.py:22
  31.5 1.2 %collective-permute-done.10.three = bf16[96,128]{1,0:T(8,128)(2,1)S(1)} collective-permute-done((bf16[96,128]{1,0:T(8,128)(2,1)S(1)}, bf16[96,128]{1,0:T(8,128)(2,1)S(1)}, u32[]{:S(2)}, u32[]{:S(2)}) %collective-permute-start.10) | collective-permute-done | bytes 24608 | tf_op jit(solution)/shard_map/ppermute | solution.py:22
  32.8 2.7 %collective-permute-done.11.two = bf16[96,128]{1,0:T(8,128)(2,1)S(1)} collective-permute-done((bf16[96,128]{1,0:T(8,128)(2,1)S(1)}, bf16[96,128]{1,0:T(8,128)(2,1)S(1)}, u32[]{:S(2)}, u32[]{:S(2)}) %collective-permute-start.11) | collective-permute-done | bytes 24608 | tf_op jit(solution)/shard_map/ppermute | solution.py:22
  35.5 0.1 gather.1.refs_0_
  35.7 1.6 %collective-permute-start.14 = (bf16[96,128]{1,0:T(8,128)(2,1)S(1)}, bf16[96,128]{1,0:T(8,128)(2,1)S(1)}, u32[]{:S(2)}, u32[]{:S(2)}) collective-permute-start(bf16[96,128]{1,0:T(8,128)(2,1)S(1)} %gather.1.refs_0_), channel_id=1, source_target_pairs={{0,2},{1,3},{2,0},{3,1},{4,6},{5,7},{6,4},{7,5},{8,10},{9,11},{10,... | collective-permute-start | bytes 73736 | tf_op jit(solution)/shard_map/ppermute | solution.py:22
  37.2 0.3 collective-permute-start.15
  37.5 0.3 and_convert_fusion.refs_4_
  37.9 1.7 %collective-permute-done.14.refs_2_ = bf16[96,128]{1,0:T(8,128)(2,1)S(1)} collective-permute-done((bf16[96,128]{1,0:T(8,128)(2,1)S(1)}, bf16[96,128]{1,0:T(8,128)(2,1)S(1)}, u32[]{:S(2)}, u32[]{:S(2)}) %collective-permute-start.14) | collective-permute-done | bytes 24608 | tf_op jit(solution)/shard_map/ppermute | solution.py:22
  39.6 0.9 %collective-permute-done.15.refs_3_ = bf16[96,128]{1,0:T(8,128)(2,1)S(1)} collective-permute-done((bf16[96,128]{1,0:T(8,128)(2,1)S(1)}, bf16[96,128]{1,0:T(8,128)(2,1)S(1)}, u32[]{:S(2)}, u32[]{:S(2)}) %collective-permute-start.15) | collective-permute-done | bytes 24608 | tf_op jit(solution)/shard_map/ppermute | solution.py:22
  40.5 5.4 %finish.1 = bf16[3,2,32,384]{3,2,1,0:T(8,128)(2,1)} custom-call(s32[1]{0:T(128)} %bitcast.index, bf16[96,128]{1,0:T(8,128)(2,1)S(1)} %gather.1.refs_0_, bf16[96,128]{1,0:T(8,128)(2,1)S(1)} %collective-permute-done.13.refs_1_, bf16[96,128]{1,0:T(8,128)(2,1)S(1)} %collective-permute-done.14.refs_2_, bf16[96,128]{1,0:T(8,128)(2,1)S(1)} %collective-permute-done.15.refs_3_, ...), custom_call_target="tpu_custom_call" | custom-call | tf_op jit(solution)/shard_map/finish/pallas_call | solution.py:422
  (40 shorter events, 0.4 us)
Async XLA Ops:
  1.8 9.1 %collective-permute-start = (bf16[48,1664]{1,0:T(8,128)(2,1)S(1)}, bf16[48,1664]{1,0:T(8,128)(2,1)S(1)}, u32[]{:S(2)}, u32[]{:S(2)}) collective-permute-start(bf16[48,1664]{1,0:T(8,128)(2,1)S(1)} %pad_maximum_fusion.3), channel_id=1, source_target_pairs={{0,4},{1,5},{2,6},{3,7},{4,0},{5,1},{6,2},{7,3},{8,12},{9,13},{10,... | collective-permute-start | bytes 479240 | tf_op jit(solution)/shard_map/ppermute | solution.py:22
  4.9 12.3 %collective-permute-start.3 = (bf16[48,1024]{1,0:T(8,128)(2,1)S(1)}, bf16[48,1024]{1,0:T(8,128)(2,1)S(1)}, u32[]{:S(2)}, u32[]{:S(2)}) collective-permute-start(bf16[48,1024]{1,0:T(8,128)(2,1)S(1)} %get-tuple-element.27), channel_id=1, source_target_pairs={{0,8},{1,9},{2,10},{3,11},{4,12},{5,13},{6,14},{7,15},{8,0},{9,1},... | collective-permute-start | bytes 294920 | tf_op jit(solution)/shard_map/ppermute | solution.py:22
  7.5 9.7 %collective-permute-start.4 = (bf16[48,1024]{1,0:T(8,128)(2,1)S(1)}, bf16[48,1024]{1,0:T(8,128)(2,1)S(1)}, u32[]{:S(2)}, u32[]{:S(2)}) collective-permute-start(bf16[48,1024]{1,0:T(8,128)(2,1)S(1)} %get-tuple-element.28), channel_id=1, source_target_pairs={{0,12},{1,13},{2,14},{3,15},{4,8},{5,9},{6,10},{7,11},{8,4},{9,5},... | collective-permute-start | bytes 294920 | tf_op jit(solution)/shard_map/ppermute | solution.py:22
  9.5 1.0 %copy-start = (bf16[2560,64]{0,1:T(8,128)(2,1)S(1)}, bf16[2560,64]{0,1:T(8,128)(2,1)}, u32[]{:S(2)}) copy-start(bf16[2560,64]{0,1:T(8,128)(2,1)} %param.13) | copy-start | bytes 983044
  9.5 1.0 %copy-start.1 = (bf16[3,1,16,2560]{3,2,1,0:T(8,128)(2,1)S(1)}, bf16[3,1,16,2560]{3,2,1,0:T(8,128)(2,1)}, u32[]{:S(2)}) copy-start(bf16[3,1,16,2560]{3,2,1,0:T(8,128)(2,1)} %param.12) | copy-start | bytes 737284
  10.9 6.1 %collective-permute-start.5 = (bf16[96,1024]{1,0:T(8,128)(2,1)S(1)}, bf16[96,1024]{1,0:T(8,128)(2,1)S(1)}, u32[]{:S(2)}, u32[]{:S(2)}) collective-permute-start(bf16[96,1024]{1,0:T(8,128)(2,1)S(1)} %pad_maximum_fusion.2), channel_id=1, source_target_pairs={{0,2},{1,3},{2,0},{3,1},{4,6},{5,7},{6,4},{7,5},{8,10},{9,11},{10,... | collective-permute-start | bytes 589832 | tf_op jit(solution)/shard_map/ppermute | solution.py:22
  12.8 8.5 %collective-permute-start.1 = (bf16[48,640]{1,0:T(8,128)(2,1)S(1)}, bf16[48,640]{1,0:T(8,128)(2,1)S(1)}, u32[]{:S(2)}, u32[]{:S(2)}) collective-permute-start(bf16[48,640]{1,0:T(8,128)(2,1)S(1)} %get-tuple-element.25), channel_id=1, source_target_pairs={{0,8},{1,9},{2,10},{3,11},{4,12},{5,13},{6,14},{7,15},{8,0},{9,1},... | collective-permute-start | bytes 184328 | tf_op jit(solution)/shard_map/ppermute | solution.py:22
  14.6 6.6 %collective-permute-start.2 = (bf16[48,640]{1,0:T(8,128)(2,1)S(1)}, bf16[48,640]{1,0:T(8,128)(2,1)S(1)}, u32[]{:S(2)}, u32[]{:S(2)}) collective-permute-start(bf16[48,640]{1,0:T(8,128)(2,1)S(1)} %get-tuple-element.26), channel_id=1, source_target_pairs={{0,12},{1,13},{2,14},{3,15},{4,8},{5,9},{6,10},{7,11},{8,4},{9,5},... | collective-permute-start | bytes 184328 | tf_op jit(solution)/shard_map/ppermute | solution.py:22
  17.1 4.2 %collective-permute-start.8 = (bf16[192,1024]{1,0:T(8,128)(2,1)S(1)}, bf16[192,1024]{1,0:T(8,128)(2,1)S(1)}, u32[]{:S(2)}, u32[]{:S(2)}) collective-permute-start(bf16[192,1024]{1,0:T(8,128)(2,1)S(1)} %pad_maximum_fusion.1.refs_1_), channel_id=1, source_target_pairs={{0,1},{1,0},{2,3},{3,2},{4,5},{5,4},{6,7},{7,6},{8,9},{9,8},{10,11... | collective-permute-start | bytes 1179656 | tf_op jit(solution)/shard_map/ppermute | solution.py:22
  17.2 7.3 %collective-permute-start.6 = (bf16[96,1024]{1,0:T(8,128)(2,1)S(1)}, bf16[96,1024]{1,0:T(8,128)(2,1)S(1)}, u32[]{:S(2)}, u32[]{:S(2)}) collective-permute-start(bf16[96,1024]{1,0:T(8,128)(2,1)S(1)} %constant_dynamic-update-slice_fusion.refs_1_), channel_id=1, source_target_pairs={{0,2},{1,3},{2,0},{3,1},{4,6},{5,7},{6,4},{7,5},{8,10},{9,11},{10,... | collective-permute-start | bytes 589832 | tf_op jit(solution)/shard_map/ppermute | solution.py:22
  21.2 19.3 %slice-start = ((s8[7962624]{0:T(1024)(128)(4,1)}), s8[4194304]{0:T(1024)(128)(4,1)S(1)}, s32[]{:S(2)}) async-start(s8[7962624]{0:T(1024)(128)(4,1)} %bitcast.8), calls=%async_computation | async-start | bytes 8388608
  21.2 19.3 %slice-start.1 = ((s8[7962624]{0:T(1024)(128)(4,1)}), s8[3768320]{0:T(1024)(128)(4,1)S(1)}, s32[]{:S(2)}) async-start(s8[7962624]{0:T(1024)(128)(4,1)} %bitcast.8), calls=%async_computation.1 | async-start | bytes 7536640
  21.2 3.5 %collective-permute-start.7 = (bf16[96,1024]{1,0:T(8,128)(2,1)S(1)}, bf16[96,1024]{1,0:T(8,128)(2,1)S(1)}, u32[]{:S(2)}, u32[]{:S(2)}) collective-permute-start(bf16[96,1024]{1,0:T(8,128)(2,1)S(1)} %constant_dynamic-update-slice_fusion.refs_1_), channel_id=1, source_target_pairs={{0,1},{1,0},{2,3},{3,2},{4,5},{5,4},{6,7},{7,6},{8,9},{9,8},{10,11... | collective-permute-start | bytes 589832 | tf_op jit(solution)/shard_map/ppermute | solution.py:22
  22.3 15.5 %copy-start.2 = (f32[384]{0:T(512)S(1)}, f32[384]{0:T(512)}, u32[]{:S(2)}) copy-start(f32[384]{0:T(512)} %param.15) | copy-start | bytes 4612
  22.3 15.6 %copy-start.3 = (f32[384]{0:T(512)S(1)}, f32[384]{0:T(512)}, u32[]{:S(2)}) copy-start(f32[384]{0:T(512)} %param.16) | copy-start | bytes 4612
  24.6 1.4 %collective-permute-start.9 = (bf16[96,1024]{1,0:T(8,128)(2,1)S(1)}, bf16[96,1024]{1,0:T(8,128)(2,1)S(1)}, u32[]{:S(2)}, u32[]{:S(2)}) collective-permute-start(bf16[96,1024]{1,0:T(8,128)(2,1)S(1)} %collective-permute-done.6.refs_2_), channel_id=1, source_target_pairs={{0,1},{1,0},{2,3},{3,2},{4,5},{5,4},{6,7},{7,6},{8,9},{9,8},{10,11... | collective-permute-start | bytes 589832 | tf_op jit(solution)/shard_map/ppermute | solution.py:22
  27.1 5.7 %collective-permute-start.10 = (bf16[96,128]{1,0:T(8,128)(2,1)S(1)}, bf16[96,128]{1,0:T(8,128)(2,1)S(1)}, u32[]{:S(2)}, u32[]{:S(2)}) collective-permute-start(bf16[96,128]{1,0:T(8,128)(2,1)S(1)} %attend_far.1.own), channel_id=1, source_target_pairs={{0,12},{1,13},{2,14},{3,15},{4,8},{5,9},{6,10},{7,11},{8,4},{9,5},... | collective-permute-start | bytes 73736 | tf_op jit(solution)/shard_map/ppermute | solution.py:22
  30.8 4.7 %collective-permute-start.11 = (bf16[96,128]{1,0:T(8,128)(2,1)S(1)}, bf16[96,128]{1,0:T(8,128)(2,1)S(1)}, u32[]{:S(2)}, u32[]{:S(2)}) collective-permute-start(bf16[96,128]{1,0:T(8,128)(2,1)S(1)} %attend_far.1.own), channel_id=1, source_target_pairs={{0,8},{1,9},{2,10},{3,11},{4,12},{5,13},{6,14},{7,15},{8,0},{9,1},... | collective-permute-start | bytes 73736 | tf_op jit(solution)/shard_map/ppermute | solution.py:22
  30.8 4.7 %collective-permute-start.12 = (bf16[96,128]{1,0:T(8,128)(2,1)S(1)}, bf16[96,128]{1,0:T(8,128)(2,1)S(1)}, u32[]{:S(2)}, u32[]{:S(2)}) collective-permute-start(bf16[96,128]{1,0:T(8,128)(2,1)S(1)} %attend_far.1.own), channel_id=1, source_target_pairs={{0,4},{1,5},{2,6},{3,7},{4,0},{5,1},{6,2},{7,3},{8,12},{9,13},{10,... | collective-permute-start | bytes 73736 | tf_op jit(solution)/shard_map/ppermute | solution.py:22
  35.6 2.3 %collective-permute-start.13 = (bf16[96,128]{1,0:T(8,128)(2,1)S(1)}, bf16[96,128]{1,0:T(8,128)(2,1)S(1)}, u32[]{:S(2)}, u32[]{:S(2)}) collective-permute-start(bf16[96,128]{1,0:T(8,128)(2,1)S(1)} %gather.1.refs_0_), channel_id=1, source_target_pairs={{0,1},{1,0},{2,3},{3,2},{4,5},{5,4},{6,7},{7,6},{8,9},{9,8},{10,11... | collective-permute-start | bytes 73736 | tf_op jit(solution)/shard_map/ppermute | solution.py:22
  35.7 3.9 %collective-permute-start.14 = (bf16[96,128]{1,0:T(8,128)(2,1)S(1)}, bf16[96,128]{1,0:T(8,128)(2,1)S(1)}, u32[]{:S(2)}, u32[]{:S(2)}) collective-permute-start(bf16[96,128]{1,0:T(8,128)(2,1)S(1)} %gather.1.refs_0_), channel_id=1, source_target_pairs={{0,2},{1,3},{2,0},{3,1},{4,6},{5,7},{6,4},{7,5},{8,10},{9,11},{10,... | collective-permute-start | bytes 73736 | tf_op jit(solution)/shard_map/ppermute | solution.py:22
  37.2 3.3 %collective-permute-start.15 = (bf16[96,128]{1,0:T(8,128)(2,1)S(1)}, bf16[96,128]{1,0:T(8,128)(2,1)S(1)}, u32[]{:S(2)}, u32[]{:S(2)}) collective-permute-start(bf16[96,128]{1,0:T(8,128)(2,1)S(1)} %gather.1.refs_0_), channel_id=1, source_target_pairs={{0,3},{1,2},{2,1},{3,0},{4,7},{5,6},{6,5},{7,4},{8,11},{9,10},{10,... | collective-permute-start | bytes 73736 | tf_op jit(solution)/shard_map/ppermute | solution.py:22

commit v5 on v4

--- a/solution.py
+++ b/solution.py
@@ -84,12 +84,17 @@
     out[...] = through_twice(s, w, slice(None))
 
 
-def attend_kernel(depth, heads, last, *refs):
+def attend_kernel(depth, heads, first, last, *refs):
     q, refs = refs[0], refs[1:]
     if last:
-        kv, (stream, top_in, mixed_in, out) = refs[:-4], refs[-4:]
+        refs, out = refs[:-1], refs[-1]
+        refs, stream = refs[:-1], refs[-1]
     else:
-        kv, (top_out, mixed_out) = refs[:-2], refs[-2:]
+        refs, (top_out, mixed_out) = refs[:-2], refs[-2:]
+    if first:
+        kv = refs
+    else:
+        kv, (top_in, mixed_in) = refs[:-2], refs[-2:]
     group = heads * depth
     wide = 128
     factor = 1.4426950408889634 / depth**0.5
@@ -113,12 +118,12 @@
         if head + 1 < heads:
             upcoming = scores_of(head + 1)
         top = jnp.broadcast_to(jnp.max(scores, axis=1, keepdims=True), (rows, wide))
-        if last:
+        if not first:
             before = top_in[head]
             top = jnp.maximum(top, before)
         expo = jnp.concatenate(
             [
-                jnp.exp2((scores[:, at : at + wide] - top) * factor).astype(jnp.bfloat16)
+                jnp.exp2((scores[:, at : at + wide] - top[:, : min(wide, keys - at)]) * factor).astype(jnp.bfloat16)
                 for at in range(0, keys, wide)
             ],
             axis=1,
@@ -126,13 +131,16 @@
         at = group + (head // 2) * wide
         value = jnp.concatenate([piece[:, at : at + wide] for piece in kv], axis=0)
         mixed = dot(expo, jnp.concatenate([value, ones], axis=1))
+        weighed, total = mixed[:, :wide], mixed[:, wide:]
+        if not first:
+            decay = jnp.exp2((before - top) * factor)
+            weighed = weighed + mixed_in[head, :, :wide] * decay
+            total = total + mixed_in[head, :, wide:] * decay
         if not last:
             top_out[head] = top
-            mixed_out[head] = mixed
+            mixed_out[head, :, :wide] = weighed
+            mixed_out[head, :, wide:] = total
             continue
-        decay = jnp.exp2((before - top) * factor)
-        weighed = mixed[:, :wide] + mixed_in[head, :, :wide] * decay
-        total = mixed[:, wide:] + mixed_in[head, :, wide:] * decay
         mine = low if head % 2 == 0 else jnp.logical_not(low)
         summed = summed + jnp.where(mine, weighed / total, 0.0)
     if not last:
@@ -163,7 +171,7 @@
     out[...] = latent.astype(jnp.bfloat16)
 
 
-def finish_kernel(frames, n, cols, index, *refs):
+def finish_kernel(frames, n, cols, order, index, *refs):
     members = n // SPLIT
     patches, refs = refs[:members], refs[members:]
     (chosen, in_weight, held, grouped, gain, shift, out, grid, stacked, first, taps, merged) = refs
@@ -183,7 +191,7 @@
         around = jnp.concatenate([before, latent, after], axis=1).astype(jnp.bfloat16)
         patch = dot(around, chosen[...]).astype(jnp.bfloat16)
         for step in range(SPLIT):
-            row = me ^ (rest_mask(member) | (step << 2))
+            row = me ^ (rest_mask(order[member]) | (step << 2))
             at, lanes = (step % 2) * tokens, (step // 2) * wide
             for t in range(frames):
                 grid[t, row + 1] = patch[at + t * cols : at + (t + 1) * cols, lanes : lanes + wide]
@@ -207,18 +215,19 @@
     pivot = None
     for t in range(frames):
         for r in range(0, n, rows_in):
-            for part in range(4):
-                lanes = slice(part * channels, (part + 1) * channels)
-                here = dot(
+            for row in range(2):
+                lanes = slice(row * 2 * channels, (row + 1) * 2 * channels)
+                both = dot(
                     stacked[r * cols : r * cols + chunk, : (t + 1) * depth],
                     in_weight[(frames - 1 - t) * depth :, lanes],
                 )
-                first[t, r : r + rows_in, :, lanes] = here.reshape(rows_in, cols, channels)
-                if pivot is None:
-                    pivot = jnp.sum(here, axis=0, keepdims=True) / chunk
-                off = (here - pivot).reshape(chunk // 8, 8, channels)
-                sums = sums + jnp.sum(off, axis=0)
-                squares = squares + jnp.sum(off * off, axis=0)
+                first[t, r : r + rows_in, :, lanes] = both.reshape(rows_in, cols, 2 * channels)
+                for here in (both[:, :channels], both[:, channels:]):
+                    if pivot is None:
+                        pivot = jnp.sum(here, axis=0, keepdims=True) / chunk
+                    off = (here - pivot).reshape(chunk // 8, 8, channels)
+                    sums = sums + jnp.sum(off, axis=0)
+                    squares = squares + jnp.sum(off * off, axis=0)
 
     def over_group(line):
         high = line.astype(jnp.bfloat16)
@@ -260,15 +269,19 @@
 
     here = 4 * cols
     totals = [jnp.zeros((here, channels), jnp.float32) for _ in range(frames)]
-    for a in range(frames):
-        valid = a + 1
-        for b in range(3):
-            left = jnp.concatenate(
-                [taps[:valid, b : b + 2, w : w + 2].reshape(valid * here, channels) for w in range(3)], axis=1
-            )
-            got = dot(left, held[a, b].reshape(3 * channels, channels))
-            for t in range(valid):
-                totals[frames - 1 - a + t] = totals[frames - 1 - a + t] + got[t * here : (t + 1) * here]
+    left = jnp.concatenate(
+        [taps[:, b : b + 2, w : w + 2].reshape(frames * here, channels) for b in range(3) for w in range(3)], axis=1
+    )
+    deep = 9 * channels
+    now = held[2].reshape(deep, channels)
+    then = held[1].reshape(deep, channels)
+    got = dot(left, jnp.concatenate([now, then], axis=1))
+    first_got = dot(left[:here], held[0].reshape(deep, channels))
+    for t in range(frames):
+        totals[t] = totals[t] + got[t * here : (t + 1) * here, :channels]
+        if t + 1 < frames:
+            totals[t + 1] = totals[t + 1] + got[t * here : (t + 1) * here, channels:]
+    totals[2] = totals[2] + first_got
     for t in range(frames):
         for part in range(4):
             kept = first[t, me, :, part * channels : (part + 1) * channels]
@@ -375,7 +388,6 @@
     near = [near, exchanged(near, 1)]
     far = spread(lax.optimization_barrier((kv[2:], near[0]))[0])
     limit = pltpu.CompilerParams(vmem_limit_bytes=(12 + 2 * members // 4 * 4) * 2**20)
-    state = [jax.ShapeDtypeStruct((heads, SPLIT * tokens, size), f32) for size in (wide, 2 * wide)]
     queried = pl.pallas_call(
         collect_kernel,
         out_shape=jax.ShapeDtypeStruct((SPLIT * tokens, group), bf16),
@@ -385,25 +397,26 @@
         cost_estimate=pl.CostEstimate(flops=5 * 10**9, bytes_accessed=10**6, transcendentals=0),
         name="collect",
     )(*q)
-    carried = pl.pallas_call(
-        functools.partial(attend_kernel, depth, heads, False),
-        out_shape=state,
-        in_specs=[VMEM] * (1 + len(near)),
-        out_specs=[VMEM] * 2,
-        compiler_params=limit,
-        cost_estimate=pl.CostEstimate(flops=1000000000, bytes_accessed=4 * 10**6, transcendentals=4 * 10**5),
-        name="attend_near",
-    )(queried, *near)
-    passed = lax.optimization_barrier((far[1:], carried))[0]
-    far = far + [exchanged(block, 1) for block in [far[0]] + passed]
-    part = pl.pallas_call(
-        functools.partial(attend_kernel, depth, heads, True),
-        out_shape=jax.ShapeDtypeStruct((SPLIT * tokens // 2, wide), bf16),
-        in_specs=[VMEM] * (1 + len(far) + 3),
-        out_specs=VMEM,
-        compiler_params=limit,
-        name="attend_far",
-    )(queried, *far, streamed, *carried)
+    state = [jax.ShapeDtypeStruct((heads, SPLIT * tokens, size), f32) for size in (wide, 2 * wide)]
+
+    def attended(blocks, carried, last, name):
+        return pl.pallas_call(
+            functools.partial(attend_kernel, depth, heads, not carried, bool(last)),
+            out_shape=jax.ShapeDtypeStruct((SPLIT * tokens // 2, wide), bf16) if last else state,
+            in_specs=[VMEM] * (1 + len(blocks) + len(carried) + len(last)),
+            out_specs=VMEM if last else [VMEM] * 2,
+            compiler_params=limit,
+            cost_estimate=pl.CostEstimate(flops=10**9, bytes_accessed=4 * 10**6, transcendentals=4 * 10**5),
+            name=name,
+        )(queried, *blocks, *carried, *last)
+
+    carried = attended(near, [], [], "attend_near")
+    beside = exchanged(far[0], 1)
+    middle = carried
+    carried = attended([far[0], beside], carried, [], "attend_middle")
+    passed = lax.optimization_barrier((far[1:], middle))[0]
+    far = passed + [exchanged(block, 1) for block in passed]
+    part = attended(far, carried, [streamed], "attend_far")
 
     others = [exchanged(part, step << 2) for step in (3, 2, 1)]
     patch = pl.pallas_call(
@@ -414,13 +427,14 @@
         compiler_params=pltpu.CompilerParams(vmem_limit_bytes=4 * 2**20),
         name="gather",
     )(part, *others)
-    patches = [patch] + [exchanged(patch, rest_mask(member)) for member in range(1, members)]
+    order = sorted(range(1, members), key=lambda member: -member)
+    patches = [patch] + [exchanged(patch, rest_mask(member)) for member in order]
 
     lane = jnp.arange(channels) // (channels // GROUPS)
     in_weight = widened(conv_in_weight)
     grouped = (lane[:, None] == lane[None, :]).astype(bf16)
     return pl.pallas_call(
-        functools.partial(finish_kernel, frames, n, cols),
+        functools.partial(finish_kernel, frames, n, cols, [0] + order),
         out_shape=jax.ShapeDtypeStruct((frames, 2, 2 * cols, channels), bf16),
         in_specs=[SMEM] + [VMEM] * (members + 6),
         out_specs=VMEM,

time: 46 us -> 44.1 us (0.959)
  waiting for transfers between devices: 13 us -> 11.4 us
    ppermute x16, waiting for transfers between devices: 13 us -> 11.4 us  [exchanged(): return lax.ppermute(value, 'seq', pairs)]
    pallas_call x3 -> x4, Pallas kernels: 7.3 us -> 6.92 us  [the longest x1 4.63 us: shards(): pl.pallas_call(functools.partial(finish_kernel, frames, n, cols, [0] + or...]
  transfers between devices with their start and end apart: 16 -> 16, of which waited for: 8 -> 8; matrix products, arithmetic and copies ran while one was open for 6% -> 6% of each run, Pallas kernels for 3% -> 4%
where the time goes in v5:
time: 44.1 us; the launch traced here: 43.9 us
  starting transfers between devices  19.5 us (44%)
  waiting for transfers between devices  11.4 us (26%)
  Pallas kernels  9.07 us (21%)
  other arithmetic  2.59 us (6%)
  local copies, waits for them, and re-layouts  1.01 us (2%)
    ppermute x16, starting transfers between devices, exchanged(): return lax.ppermute(value, 'seq', pairs)  19.5 us
    ppermute x16, waiting for transfers between devices, exchanged(): return lax.ppermute(value, 'seq', pairs)  11.4 us
    pallas_call x1, Pallas kernels, shards(): pl.pallas_call(functools.partial(finish_kernel, frames, n, cols, [0] + or...  4.63 us
    pallas_call x3, Pallas kernels, attended(): pl.pallas_call(functools.partial(attend_kernel, depth, heads, not carried...  2.29 us
    concatenate x1, other arithmetic, widened(): whole = jnp.concatenate(blocks, axis=-1)  1.85 us
    pallas_call x1, Pallas kernels, shards(): pl.pallas_call(functools.partial(prepare_kernel, depth, heads), out_shape...  1.77 us
  transfers between devices with their start and end apart: 16, of which 8 were waited for; matrix products, arithmetic and copies ran while one was open for 6% of the time, Pallas kernels for 4%

profile of v5, /device:TPU:0, one launch (start us, length us, event | category | flops | bytes accessed | tf_op | source)
XLA Modules:
  0.0 43.9 jit_solution(10031587378332395248)
XLA Ops:
  0.0 1.8 %prepare.1 = (bf16[48,1024]{1,0:T(8,128)(2,1)S(1)}, bf16[48,1024]{1,0:T(8,128)(2,1)S(1)}, bf16[48,1024]{1,0:T(8,128)(2,1)S(1)}, bf16[48,1024]{1,0:T(8,128)(2,1)S...) custom-call(s32[1]{0:T(128)} %bitcast.index, ...), custom_call_target="tpu_custom_call" | custom-call | tf_op jit(solution)/shard_map/prepare/pallas_call | solution.py:344
  1.8 3.1 %collective-permute-start = (bf16[48,1664]{1,0:T(8,128)(2,1)S(1)}, bf16[48,1664]{1,0:T(8,128)(2,1)S(1)}, u32[]{:S(2)}, u32[]{:S(2)}) collective-permute-start(bf16[48,1664]{1,0:T(8,128)(2,1)S(1)} %pad_maximum_fusion.3), channel_id=1, source_target_pairs={{0,4},{1,5},{2,6},{3,7},{4,0},{5,1},{6,2},{7,3},{8,12},{9,13},{10,... | collective-permute-start | bytes 479240 | tf_op jit(solution)/shard_map/ppermute | solution.py:22
  4.9 2.6 %collective-permute-start.3 = (bf16[48,1024]{1,0:T(8,128)(2,1)S(1)}, bf16[48,1024]{1,0:T(8,128)(2,1)S(1)}, u32[]{:S(2)}, u32[]{:S(2)}) collective-permute-start(bf16[48,1024]{1,0:T(8,128)(2,1)S(1)} %get-tuple-element.29), channel_id=1, source_target_pairs={{0,8},{1,9},{2,10},{3,11},{4,12},{5,13},{6,14},{7,15},{8,0},{9,1},... | collective-permute-start | bytes 294920 | tf_op jit(solution)/shard_map/ppermute | solution.py:22
  7.5 1.9 %fusion.7 = bf16[3,4,4,16,1536]{4,3,2,1,0:T(8,128)(2,1)S(1)} fusion(bf16[3,3,3,16,384]{4,3,2,1,0:T(8,128)(2,1)} %param.14), kind=kLoop, calls=%fused_computation.13 | loop fusion | flops 23592960 | bytes 2691072 | tf_op jit(solution)/shard_map/concatenate | solution.py:303
  9.4 0.1 slice.18
  9.6 0.2 pad_maximum_fusion
  9.8 0.7 %copy-done = bf16[2560,64]{0,1:T(8,128)(2,1)S(1)} copy-done((bf16[2560,64]{0,1:T(8,128)(2,1)S(1)}, bf16[2560,64]{0,1:T(8,128)(2,1)}, u32[]{:S(2)}) %copy-start) | copy-done | bytes 327704
  10.6 0.3 stream.1.refs_5_
  11.0 1.8 %collective-permute-start.5 = (bf16[96,1024]{1,0:T(8,128)(2,1)S(1)}, bf16[96,1024]{1,0:T(8,128)(2,1)S(1)}, u32[]{:S(2)}, u32[]{:S(2)}) collective-permute-start(bf16[96,1024]{1,0:T(8,128)(2,1)S(1)} %pad_maximum_fusion.2), channel_id=1, source_target_pairs={{0,2},{1,3},{2,0},{3,1},{4,6},{5,7},{6,4},{7,5},{8,10},{9,11},{10,... | collective-permute-start | bytes 589832 | tf_op jit(solution)/shard_map/ppermute | solution.py:22
  12.8 0.1 compare_convert_fusion.refs_7_
  12.9 1.8 %collective-permute-start.1 = (bf16[48,640]{1,0:T(8,128)(2,1)S(1)}, bf16[48,640]{1,0:T(8,128)(2,1)S(1)}, u32[]{:S(2)}, u32[]{:S(2)}) collective-permute-start(bf16[48,640]{1,0:T(8,128)(2,1)S(1)} %get-tuple-element.27), channel_id=1, source_target_pairs={{0,8},{1,9},{2,10},{3,11},{4,12},{5,13},{6,14},{7,15},{8,0},{9,1},... | collective-permute-start | bytes 184328 | tf_op jit(solution)/shard_map/ppermute | solution.py:22
  14.7 2.1 %collective-permute-start.2 = (bf16[48,640]{1,0:T(8,128)(2,1)S(1)}, bf16[48,640]{1,0:T(8,128)(2,1)S(1)}, u32[]{:S(2)}, u32[]{:S(2)}) collective-permute-start(bf16[48,640]{1,0:T(8,128)(2,1)S(1)} %get-tuple-element.28), channel_id=1, source_target_pairs={{0,12},{1,13},{2,14},{3,15},{4,8},{5,9},{6,10},{7,11},{8,4},{9,5},... | collective-permute-start | bytes 184328 | tf_op jit(solution)/shard_map/ppermute | solution.py:22
  16.8 0.3 collective-permute-done.5
  17.1 0.1 collective-permute-start.7
  17.3 1.6 %collective-permute-start.6 = (bf16[96,1024]{1,0:T(8,128)(2,1)S(1)}, bf16[96,1024]{1,0:T(8,128)(2,1)S(1)}, u32[]{:S(2)}, u32[]{:S(2)}) collective-permute-start(bf16[96,1024]{1,0:T(8,128)(2,1)S(1)} %constant_dynamic-update-slice_fusion.refs_1_), channel_id=1, source_target_pairs={{0,2},{1,3},{2,0},{3,1},{4,6},{5,7},{6,4},{7,5},{8,10},{9,11},{10,... | collective-permute-start | bytes 589832 | tf_op jit(solution)/shard_map/ppermute | solution.py:22
  18.9 2.4 %collective-permute-done.1.refs_2_ = bf16[48,640]{1,0:T(8,128)(2,1)S(1)} collective-permute-done((bf16[48,640]{1,0:T(8,128)(2,1)S(1)}, bf16[48,640]{1,0:T(8,128)(2,1)S(1)}, u32[]{:S(2)}, u32[]{:S(2)}) %collective-permute-start.1) | collective-permute-done | bytes 61472 | tf_op jit(solution)/shard_map/ppermute | solution.py:22
  21.3 0.9 %attend_near.1 = (f32[5,192,128]{2,1,0:T(8,128)S(1)}, f32[5,192,256]{2,1,0:T(8,128)S(1)}) custom-call(bf16[192,640]{1,0:T(8,128)(2,1)S(1)} %collect.1.refs_0_, bf16[192,1024]{1,0:T(8,128)(2,1)S(1)} %pad_maximum_fusion.1.refs_1_, bf16[192,1024]{1,0:T(8,128)(2,1)S(1)} %collective-permute-done.7.refs_2_), custom_call_target="tpu_custom_call" | custom-call | flops 1000000000 | bytes 4000000 | tf_op jit(solution)/shard_map/attend_near/pallas_call | solution.py:403
  22.3 2.4 %collective-permute-done.6.refs_1_ = bf16[96,1024]{1,0:T(8,128)(2,1)S(1)} collective-permute-done((bf16[96,1024]{1,0:T(8,128)(2,1)S(1)}, bf16[96,1024]{1,0:T(8,128)(2,1)S(1)}, u32[]{:S(2)}, u32[]{:S(2)}) %collective-permute-start.6) | collective-permute-done | bytes 196640 | tf_op jit(solution)/shard_map/ppermute | solution.py:22
  24.7 0.6 %attend_middle.1 = (f32[5,192,128]{2,1,0:T(8,128)S(1)}, f32[5,192,256]{2,1,0:T(8,128)S(1)}) custom-call(bf16[192,640]{1,0:T(8,128)(2,1)S(1)} %collect.1.refs_0_, bf16[96,1024]{1,0:T(8,128)(2,1)S(1)} %constant_dynamic-update-slice_fusion.refs_1_, bf16[96,1024]{1,0:T(8,128)(2,1)S(1)} %collective-permute-done.9.refs_2_, ...), custom_call_target="tpu_custom_call" | custom-call | flops 1000000000 | bytes 4000000 | tf_op jit(solution)/shard_map/attend_middle/pallas_call | solution.py:403
  25.3 0.7 %collective-permute-done.8.refs_2_ = bf16[96,1024]{1,0:T(8,128)(2,1)S(1)} collective-permute-done((bf16[96,1024]{1,0:T(8,128)(2,1)S(1)}, bf16[96,1024]{1,0:T(8,128)(2,1)S(1)}, u32[]{:S(2)}, u32[]{:S(2)}) %collective-permute-start.8) | collective-permute-done | bytes 196640 | tf_op jit(solution)/shard_map/ppermute | solution.py:22
  26.1 0.7 %attend_far.1.own = bf16[96,128]{1,0:T(8,128)(2,1)S(1)} custom-call(bf16[192,640]{1,0:T(8,128)(2,1)S(1)} %collect.1.refs_0_, bf16[96,1024]{1,0:T(8,128)(2,1)S(1)} %collective-permute-done.6.refs_1_, bf16[96,1024]{1,0:T(8,128)(2,1)S(1)} %collective-permute-done.8.refs_2_, f32[5,192,128]{2,1,0:T(8,128)S(1)} %get-tuple-element.37.refs_3_, ...), custom_call_target="tpu_custom_call" | custom-call | flops 1000000000 | bytes 4000000 | tf_op jit(solution)/shard_map/attend_far/pallas_call | solution.py:403
  26.8 3.7 %collective-permute-start.10 = (bf16[96,128]{1,0:T(8,128)(2,1)S(1)}, bf16[96,128]{1,0:T(8,128)(2,1)S(1)}, u32[]{:S(2)}, u32[]{:S(2)}) collective-permute-start(bf16[96,128]{1,0:T(8,128)(2,1)S(1)} %attend_far.1.own), channel_id=1, source_target_pairs={{0,12},{1,13},{2,14},{3,15},{4,8},{5,9},{6,10},{7,11},{8,4},{9,5},... | collective-permute-start | bytes 73736 | tf_op jit(solution)/shard_map/ppermute | solution.py:22
  30.5 0.8 %collective-permute-start.12 = (bf16[96,128]{1,0:T(8,128)(2,1)S(1)}, bf16[96,128]{1,0:T(8,128)(2,1)S(1)}, u32[]{:S(2)}, u32[]{:S(2)}) collective-permute-start(bf16[96,128]{1,0:T(8,128)(2,1)S(1)} %attend_far.1.own), channel_id=1, source_target_pairs={{0,4},{1,5},{2,6},{3,7},{4,0},{5,1},{6,2},{7,3},{8,12},{9,13},{10,... | collective-permute-start | bytes 73736 | tf_op jit(solution)/shard_map/ppermute | solution.py:22
  31.3 1.2 %collective-permute-done.10.three = bf16[96,128]{1,0:T(8,128)(2,1)S(1)} collective-permute-done((bf16[96,128]{1,0:T(8,128)(2,1)S(1)}, bf16[96,128]{1,0:T(8,128)(2,1)S(1)}, u32[]{:S(2)}, u32[]{:S(2)}) %collective-permute-start.10) | collective-permute-done | bytes 24608 | tf_op jit(solution)/shard_map/ppermute | solution.py:22
  32.5 2.7 %collective-permute-done.11.two = bf16[96,128]{1,0:T(8,128)(2,1)S(1)} collective-permute-done((bf16[96,128]{1,0:T(8,128)(2,1)S(1)}, bf16[96,128]{1,0:T(8,128)(2,1)S(1)}, u32[]{:S(2)}, u32[]{:S(2)}) %collective-permute-start.11) | collective-permute-done | bytes 24608 | tf_op jit(solution)/shard_map/ppermute | solution.py:22
  35.2 0.1 gather.1.refs_0_
  35.4 1.6 %collective-permute-start.14 = (bf16[96,128]{1,0:T(8,128)(2,1)S(1)}, bf16[96,128]{1,0:T(8,128)(2,1)S(1)}, u32[]{:S(2)}, u32[]{:S(2)}) collective-permute-start(bf16[96,128]{1,0:T(8,128)(2,1)S(1)} %gather.1.refs_0_), channel_id=1, source_target_pairs={{0,2},{1,3},{2,0},{3,1},{4,6},{5,7},{6,4},{7,5},{8,10},{9,11},{10,... | collective-permute-start | bytes 73736 | tf_op jit(solution)/shard_map/ppermute | solution.py:22
  36.9 0.3 collective-permute-start.15
  37.2 0.3 and_convert_fusion.refs_4_
  37.5 1.3 %collective-permute-done.13.refs_1_ = bf16[96,128]{1,0:T(8,128)(2,1)S(1)} collective-permute-done((bf16[96,128]{1,0:T(8,128)(2,1)S(1)}, bf16[96,128]{1,0:T(8,128)(2,1)S(1)}, u32[]{:S(2)}, u32[]{:S(2)}) %collective-permute-start.13) | collective-permute-done | bytes 24608 | tf_op jit(solution)/shard_map/ppermute | solution.py:22
  38.8 0.5 %collective-permute-done.14.refs_2_ = bf16[96,128]{1,0:T(8,128)(2,1)S(1)} collective-permute-done((bf16[96,128]{1,0:T(8,128)(2,1)S(1)}, bf16[96,128]{1,0:T(8,128)(2,1)S(1)}, u32[]{:S(2)}, u32[]{:S(2)}) %collective-permute-start.14) | collective-permute-done | bytes 24608 | tf_op jit(solution)/shard_map/ppermute | solution.py:22
  39.3 4.6 %finish.1 = bf16[3,2,32,384]{3,2,1,0:T(8,128)(2,1)} custom-call(s32[1]{0:T(128)} %bitcast.index, bf16[96,128]{1,0:T(8,128)(2,1)S(1)} %gather.1.refs_0_, bf16[96,128]{1,0:T(8,128)(2,1)S(1)} %collective-permute-done.13.refs_1_, bf16[96,128]{1,0:T(8,128)(2,1)S(1)} %collective-permute-done.14.refs_2_, bf16[96,128]{1,0:T(8,128)(2,1)S(1)} %collective-permute-done.15.refs_3_, ...), custom_call_target="tpu_custom_call" | custom-call | tf_op jit(solution)/shard_map/finish/pallas_call | solution.py:436
  (41 shorter events, 0.5 us)
Async XLA Ops:
  1.8 9.1 %collective-permute-start = (bf16[48,1664]{1,0:T(8,128)(2,1)S(1)}, bf16[48,1664]{1,0:T(8,128)(2,1)S(1)}, u32[]{:S(2)}, u32[]{:S(2)}) collective-permute-start(bf16[48,1664]{1,0:T(8,128)(2,1)S(1)} %pad_maximum_fusion.3), channel_id=1, source_target_pairs={{0,4},{1,5},{2,6},{3,7},{4,0},{5,1},{6,2},{7,3},{8,12},{9,13},{10,... | collective-permute-start | bytes 479240 | tf_op jit(solution)/shard_map/ppermute | solution.py:22
  4.9 12.3 %collective-permute-start.3 = (bf16[48,1024]{1,0:T(8,128)(2,1)S(1)}, bf16[48,1024]{1,0:T(8,128)(2,1)S(1)}, u32[]{:S(2)}, u32[]{:S(2)}) collective-permute-start(bf16[48,1024]{1,0:T(8,128)(2,1)S(1)} %get-tuple-element.29), channel_id=1, source_target_pairs={{0,8},{1,9},{2,10},{3,11},{4,12},{5,13},{6,14},{7,15},{8,0},{9,1},... | collective-permute-start | bytes 294920 | tf_op jit(solution)/shard_map/ppermute | solution.py:22
  7.5 9.7 %collective-permute-start.4 = (bf16[48,1024]{1,0:T(8,128)(2,1)S(1)}, bf16[48,1024]{1,0:T(8,128)(2,1)S(1)}, u32[]{:S(2)}, u32[]{:S(2)}) collective-permute-start(bf16[48,1024]{1,0:T(8,128)(2,1)S(1)} %get-tuple-element.30), channel_id=1, source_target_pairs={{0,12},{1,13},{2,14},{3,15},{4,8},{5,9},{6,10},{7,11},{8,4},{9,5},... | collective-permute-start | bytes 294920 | tf_op jit(solution)/shard_map/ppermute | solution.py:22
  9.5 1.0 %copy-start = (bf16[2560,64]{0,1:T(8,128)(2,1)S(1)}, bf16[2560,64]{0,1:T(8,128)(2,1)}, u32[]{:S(2)}) copy-start(bf16[2560,64]{0,1:T(8,128)(2,1)} %param.13) | copy-start | bytes 983044
  9.5 1.0 %copy-start.1 = (bf16[3,1,16,2560]{3,2,1,0:T(8,128)(2,1)S(1)}, bf16[3,1,16,2560]{3,2,1,0:T(8,128)(2,1)}, u32[]{:S(2)}) copy-start(bf16[3,1,16,2560]{3,2,1,0:T(8,128)(2,1)} %param.12) | copy-start | bytes 737284
  11.0 6.1 %collective-permute-start.5 = (bf16[96,1024]{1,0:T(8,128)(2,1)S(1)}, bf16[96,1024]{1,0:T(8,128)(2,1)S(1)}, u32[]{:S(2)}, u32[]{:S(2)}) collective-permute-start(bf16[96,1024]{1,0:T(8,128)(2,1)S(1)} %pad_maximum_fusion.2), channel_id=1, source_target_pairs={{0,2},{1,3},{2,0},{3,1},{4,6},{5,7},{6,4},{7,5},{8,10},{9,11},{10,... | collective-permute-start | bytes 589832 | tf_op jit(solution)/shard_map/ppermute | solution.py:22
  12.9 8.3 %collective-permute-start.1 = (bf16[48,640]{1,0:T(8,128)(2,1)S(1)}, bf16[48,640]{1,0:T(8,128)(2,1)S(1)}, u32[]{:S(2)}, u32[]{:S(2)}) collective-permute-start(bf16[48,640]{1,0:T(8,128)(2,1)S(1)} %get-tuple-element.27), channel_id=1, source_target_pairs={{0,8},{1,9},{2,10},{3,11},{4,12},{5,13},{6,14},{7,15},{8,0},{9,1},... | collective-permute-start | bytes 184328 | tf_op jit(solution)/shard_map/ppermute | solution.py:22
  14.7 6.5 %collective-permute-start.2 = (bf16[48,640]{1,0:T(8,128)(2,1)S(1)}, bf16[48,640]{1,0:T(8,128)(2,1)S(1)}, u32[]{:S(2)}, u32[]{:S(2)}) collective-permute-start(bf16[48,640]{1,0:T(8,128)(2,1)S(1)} %get-tuple-element.28), channel_id=1, source_target_pairs={{0,12},{1,13},{2,14},{3,15},{4,8},{5,9},{6,10},{7,11},{8,4},{9,5},... | collective-permute-start | bytes 184328 | tf_op jit(solution)/shard_map/ppermute | solution.py:22
  17.1 4.2 %collective-permute-start.7 = (bf16[192,1024]{1,0:T(8,128)(2,1)S(1)}, bf16[192,1024]{1,0:T(8,128)(2,1)S(1)}, u32[]{:S(2)}, u32[]{:S(2)}) collective-permute-start(bf16[192,1024]{1,0:T(8,128)(2,1)S(1)} %pad_maximum_fusion.1.refs_1_), channel_id=1, source_target_pairs={{0,1},{1,0},{2,3},{3,2},{4,5},{5,4},{6,7},{7,6},{8,9},{9,8},{10,11... | collective-permute-start | bytes 1179656 | tf_op jit(solution)/shard_map/ppermute | solution.py:22
  17.3 7.3 %collective-permute-start.6 = (bf16[96,1024]{1,0:T(8,128)(2,1)S(1)}, bf16[96,1024]{1,0:T(8,128)(2,1)S(1)}, u32[]{:S(2)}, u32[]{:S(2)}) collective-permute-start(bf16[96,1024]{1,0:T(8,128)(2,1)S(1)} %constant_dynamic-update-slice_fusion.refs_1_), channel_id=1, source_target_pairs={{0,2},{1,3},{2,0},{3,1},{4,6},{5,7},{6,4},{7,5},{8,10},{9,11},{10,... | collective-permute-start | bytes 589832 | tf_op jit(solution)/shard_map/ppermute | solution.py:22
  21.2 18.0 %slice-start = ((s8[7962624]{0:T(1024)(128)(4,1)}), s8[4194304]{0:T(1024)(128)(4,1)S(1)}, s32[]{:S(2)}) async-start(s8[7962624]{0:T(1024)(128)(4,1)} %bitcast.8), calls=%async_computation | async-start | bytes 8388608
  21.2 18.0 %slice-start.1 = ((s8[7962624]{0:T(1024)(128)(4,1)}), s8[3768320]{0:T(1024)(128)(4,1)S(1)}, s32[]{:S(2)}) async-start(s8[7962624]{0:T(1024)(128)(4,1)} %bitcast.8), calls=%async_computation.1 | async-start | bytes 7536640
  21.2 3.4 %collective-permute-start.9 = (bf16[96,1024]{1,0:T(8,128)(2,1)S(1)}, bf16[96,1024]{1,0:T(8,128)(2,1)S(1)}, u32[]{:S(2)}, u32[]{:S(2)}) collective-permute-start(bf16[96,1024]{1,0:T(8,128)(2,1)S(1)} %constant_dynamic-update-slice_fusion.refs_1_), channel_id=1, source_target_pairs={{0,1},{1,0},{2,3},{3,2},{4,5},{5,4},{6,7},{7,6},{8,9},{9,8},{10,11... | collective-permute-start | bytes 589832 | tf_op jit(solution)/shard_map/ppermute | solution.py:22
  24.6 1.4 %collective-permute-start.8 = (bf16[96,1024]{1,0:T(8,128)(2,1)S(1)}, bf16[96,1024]{1,0:T(8,128)(2,1)S(1)}, u32[]{:S(2)}, u32[]{:S(2)}) collective-permute-start(bf16[96,1024]{1,0:T(8,128)(2,1)S(1)} %collective-permute-done.6.refs_1_), channel_id=1, source_target_pairs={{0,1},{1,0},{2,3},{3,2},{4,5},{5,4},{6,7},{7,6},{8,9},{9,8},{10,11... | collective-permute-start | bytes 589832 | tf_op jit(solution)/shard_map/ppermute | solution.py:22
  25.3 12.2 %copy-start.2 = (f32[384]{0:T(512)S(1)}, f32[384]{0:T(512)}, u32[]{:S(2)}) copy-start(f32[384]{0:T(512)} %param.15) | copy-start | bytes 4612
  25.3 12.2 %copy-start.3 = (f32[384]{0:T(512)S(1)}, f32[384]{0:T(512)}, u32[]{:S(2)}) copy-start(f32[384]{0:T(512)} %param.16) | copy-start | bytes 4612
  26.8 5.7 %collective-permute-start.10 = (bf16[96,128]{1,0:T(8,128)(2,1)S(1)}, bf16[96,128]{1,0:T(8,128)(2,1)S(1)}, u32[]{:S(2)}, u32[]{:S(2)}) collective-permute-start(bf16[96,128]{1,0:T(8,128)(2,1)S(1)} %attend_far.1.own), channel_id=1, source_target_pairs={{0,12},{1,13},{2,14},{3,15},{4,8},{5,9},{6,10},{7,11},{8,4},{9,5},... | collective-permute-start | bytes 73736 | tf_op jit(solution)/shard_map/ppermute | solution.py:22
  30.5 4.7 %collective-permute-start.11 = (bf16[96,128]{1,0:T(8,128)(2,1)S(1)}, bf16[96,128]{1,0:T(8,128)(2,1)S(1)}, u32[]{:S(2)}, u32[]{:S(2)}) collective-permute-start(bf16[96,128]{1,0:T(8,128)(2,1)S(1)} %attend_far.1.own), channel_id=1, source_target_pairs={{0,8},{1,9},{2,10},{3,11},{4,12},{5,13},{6,14},{7,15},{8,0},{9,1},... | collective-permute-start | bytes 73736 | tf_op jit(solution)/shard_map/ppermute | solution.py:22
  30.5 4.7 %collective-permute-start.12 = (bf16[96,128]{1,0:T(8,128)(2,1)S(1)}, bf16[96,128]{1,0:T(8,128)(2,1)S(1)}, u32[]{:S(2)}, u32[]{:S(2)}) collective-permute-start(bf16[96,128]{1,0:T(8,128)(2,1)S(1)} %attend_far.1.own), channel_id=1, source_target_pairs={{0,4},{1,5},{2,6},{3,7},{4,0},{5,1},{6,2},{7,3},{8,12},{9,13},{10,... | collective-permute-start | bytes 73736 | tf_op jit(solution)/shard_map/ppermute | solution.py:22
  35.3 3.5 %collective-permute-start.13 = (bf16[96,128]{1,0:T(8,128)(2,1)S(1)}, bf16[96,128]{1,0:T(8,128)(2,1)S(1)}, u32[]{:S(2)}, u32[]{:S(2)}) collective-permute-start(bf16[96,128]{1,0:T(8,128)(2,1)S(1)} %gather.1.refs_0_), channel_id=1, source_target_pairs={{0,3},{1,2},{2,1},{3,0},{4,7},{5,6},{6,5},{7,4},{8,11},{9,10},{10,... | collective-permute-start | bytes 73736 | tf_op jit(solution)/shard_map/ppermute | solution.py:22
  35.4 3.9 %collective-permute-start.14 = (bf16[96,128]{1,0:T(8,128)(2,1)S(1)}, bf16[96,128]{1,0:T(8,128)(2,1)S(1)}, u32[]{:S(2)}, u32[]{:S(2)}) collective-permute-start(bf16[96,128]{1,0:T(8,128)(2,1)S(1)} %gather.1.refs_0_), channel_id=1, source_target_pairs={{0,2},{1,3},{2,0},{3,1},{4,6},{5,7},{6,4},{7,5},{8,10},{9,11},{10,... | collective-permute-start | bytes 73736 | tf_op jit(solution)/shard_map/ppermute | solution.py:22
  36.9 2.3 %collective-permute-start.15 = (bf16[96,128]{1,0:T(8,128)(2,1)S(1)}, bf16[96,128]{1,0:T(8,128)(2,1)S(1)}, u32[]{:S(2)}, u32[]{:S(2)}) collective-permute-start(bf16[96,128]{1,0:T(8,128)(2,1)S(1)} %gather.1.refs_0_), channel_id=1, source_target_pairs={{0,1},{1,0},{2,3},{3,2},{4,5},{5,4},{6,7},{7,6},{8,9},{9,8},{10,11... | collective-permute-start | bytes 73736 | tf_op jit(solution)/shard_map/ppermute | solution.py:22

commit v6 on v5

--- a/solution.py
+++ b/solution.py
@@ -376,7 +376,7 @@
     kv[1], q[1] = both[:, : kv[1].shape[1]], both[:, kv[1].shape[1] :]
     for step in range(2, SPLIT):
         kv[step] = exchanged(kv[step], step << 2)
-    q[2:] = lax.optimization_barrier((q[2:], both))[0]
+    q[2:] = lax.optimization_barrier((q[2:], kv[2]))[0]
     for step in range(2, SPLIT):
         q[step] = exchanged(q[step], step << 2)
 
@@ -386,7 +386,9 @@
 
     near = jnp.concatenate(spread(kv[:2]), axis=0)
     near = [near, exchanged(near, 1)]
-    far = spread(lax.optimization_barrier((kv[2:], near[0]))[0])
+    waited = [kv[2]] + lax.optimization_barrier((kv[3:], near[0]))[0]
+    far = [exchanged(piece, rest_mask(member)) for piece in waited for member in range(2, members, 2)]
+    held = jnp.concatenate(waited, axis=0)
     limit = pltpu.CompilerParams(vmem_limit_bytes=(12 + 2 * members // 4 * 4) * 2**20)
     queried = pl.pallas_call(
         collect_kernel,
@@ -411,11 +413,12 @@
         )(queried, *blocks, *carried, *last)
 
     carried = attended(near, [], [], "attend_near")
-    beside = exchanged(far[0], 1)
+    beside = exchanged(held, 1)
     middle = carried
-    carried = attended([far[0], beside], carried, [], "attend_middle")
-    passed = lax.optimization_barrier((far[1:], middle))[0]
-    far = passed + [exchanged(block, 1) for block in passed]
+    carried = attended([held, beside], carried, [], "attend_middle")
+    passed = lax.optimization_barrier((far, middle))[0]
+    far = passed
+    far = far + [exchanged(block, 1) for block in far]
     part = attended(far, carried, [streamed], "attend_far")
 
     others = [exchanged(part, step << 2) for step in (3, 2, 1)]

time: 44.1 us -> 43.4 us (0.984)
  starting transfers between devices: 19.5 us -> 21.2 us
  waiting for transfers between devices: 11.4 us -> 9.87 us
  local copies, waits for them, and re-layouts: 1.01 us -> 0.27 us
    ppermute x16 -> x18, starting transfers between devices: 19.5 us -> 21.2 us  [exchanged(): return lax.ppermute(value, 'seq', pairs)]
    ppermute x16 -> x18, waiting for transfers between devices: 11.4 us -> 9.87 us  [exchanged(): return lax.ppermute(value, 'seq', pairs)]
    unnamed x13, local copies, waits for them, and re-layouts: 0.83 us -> 0.04 us
  transfers between devices with their start and end apart: 16 -> 18, of which waited for: 8 -> 9; matrix products, arithmetic and copies ran while one was open for 6% -> 6% of each run, Pallas kernels for 4% -> 4%
where the time goes in v6:
time: 43.4 us; the launch traced here: 43.3 us
  starting transfers between devices  21.2 us (49%)
  waiting for transfers between devices  9.87 us (23%)
  Pallas kernels  9.08 us (21%)
  other arithmetic  2.55 us (6%)
    ppermute x18, starting transfers between devices, exchanged(): return lax.ppermute(value, 'seq', pairs)  21.2 us
    ppermute x18, waiting for transfers between devices, exchanged(): return lax.ppermute(value, 'seq', pairs)  9.87 us
    pallas_call x1, Pallas kernels, shards(): pl.pallas_call(functools.partial(finish_kernel, frames, n, cols, [0] + or...  4.64 us
    pallas_call x3, Pallas kernels, attended(): pl.pallas_call(functools.partial(attend_kernel, depth, heads, not carried...  2.29 us
    concatenate x1, other arithmetic, widened(): whole = jnp.concatenate(blocks, axis=-1)  1.84 us
    pallas_call x1, Pallas kernels, shards(): pl.pallas_call(functools.partial(prepare_kernel, depth, heads), out_shape...  1.77 us
  transfers between devices with their start and end apart: 18, of which 9 were waited for; matrix products, arithmetic and copies ran while one was open for 6% of the time, Pallas kernels for 4%

profile of v6, /device:TPU:0, one launch (start us, length us, event | category | flops | bytes accessed | tf_op | source)
XLA Modules:
  0.0 43.3 jit_solution(10553606132485868718)
XLA Ops:
  0.0 1.8 %prepare.1 = (bf16[48,1024]{1,0:T(8,128)(2,1)S(1)}, bf16[48,1024]{1,0:T(8,128)(2,1)S(1)}, bf16[48,1024]{1,0:T(8,128)(2,1)S(1)}, bf16[48,1024]{1,0:T(8,128)(2,1)S...) custom-call(s32[1]{0:T(128)} %bitcast.index, ...), custom_call_target="tpu_custom_call" | custom-call | tf_op jit(solution)/shard_map/prepare/pallas_call | solution.py:344
  1.8 4.1 %collective-permute-start.1 = (bf16[48,1024]{1,0:T(8,128)(2,1)S(1)}, bf16[48,1024]{1,0:T(8,128)(2,1)S(1)}, u32[]{:S(2)}, u32[]{:S(2)}) collective-permute-start(bf16[48,1024]{1,0:T(8,128)(2,1)S(1)} %get-tuple-element.27), channel_id=1, source_target_pairs={{0,8},{1,9},{2,10},{3,11},{4,12},{5,13},{6,14},{7,15},{8,0},{9,1},... | collective-permute-start | bytes 294920 | tf_op jit(solution)/shard_map/ppermute | solution.py:22
  5.9 1.6 %collective-permute-start = (bf16[48,1664]{1,0:T(8,128)(2,1)S(1)}, bf16[48,1664]{1,0:T(8,128)(2,1)S(1)}, u32[]{:S(2)}, u32[]{:S(2)}) collective-permute-start(bf16[48,1664]{1,0:T(8,128)(2,1)S(1)} %pad_maximum_fusion.3), channel_id=1, source_target_pairs={{0,4},{1,5},{2,6},{3,7},{4,0},{5,1},{6,2},{7,3},{8,12},{9,13},{10,... | collective-permute-start | bytes 479240 | tf_op jit(solution)/shard_map/ppermute | solution.py:22
  7.5 1.8 %fusion.7 = bf16[3,4,4,16,1536]{4,3,2,1,0:T(8,128)(2,1)S(1)} fusion(bf16[3,3,3,16,384]{4,3,2,1,0:T(8,128)(2,1)} %param.14), kind=kLoop, calls=%fused_computation.13 | loop fusion | flops 23592960 | bytes 2691072 | tf_op jit(solution)/shard_map/concatenate | solution.py:303
  9.8 0.2 pad_maximum_fusion
  10.0 2.8 %collective-permute-done = bf16[48,1664]{1,0:T(8,128)(2,1)S(1)} collective-permute-done((bf16[48,1664]{1,0:T(8,128)(2,1)S(1)}, bf16[48,1664]{1,0:T(8,128)(2,1)S(1)}, u32[]{:S(2)}, u32[]{:S(2)}) %collective-permute-start) | collective-permute-done | bytes 159776 | tf_op jit(solution)/shard_map/ppermute | solution.py:22
  12.9 1.8 %collective-permute-start.6 = (bf16[96,1024]{1,0:T(8,128)(2,1)S(1)}, bf16[96,1024]{1,0:T(8,128)(2,1)S(1)}, u32[]{:S(2)}, u32[]{:S(2)}) collective-permute-start(bf16[96,1024]{1,0:T(8,128)(2,1)S(1)} %pad_maximum_fusion.2), channel_id=1, source_target_pairs={{0,2},{1,3},{2,0},{3,1},{4,6},{5,7},{6,4},{7,5},{8,10},{9,11},{10,... | collective-permute-start | bytes 589832 | tf_op jit(solution)/shard_map/ppermute | solution.py:22
  14.7 1.7 %collective-permute-start.2 = (bf16[48,640]{1,0:T(8,128)(2,1)S(1)}, bf16[48,640]{1,0:T(8,128)(2,1)S(1)}, u32[]{:S(2)}, u32[]{:S(2)}) collective-permute-start(bf16[48,640]{1,0:T(8,128)(2,1)S(1)} %get-tuple-element.28), channel_id=1, source_target_pairs={{0,8},{1,9},{2,10},{3,11},{4,12},{5,13},{6,14},{7,15},{8,0},{9,1},... | collective-permute-start | bytes 184328 | tf_op jit(solution)/shard_map/ppermute | solution.py:22
  16.5 2.3 %collective-permute-start.3 = (bf16[48,640]{1,0:T(8,128)(2,1)S(1)}, bf16[48,640]{1,0:T(8,128)(2,1)S(1)}, u32[]{:S(2)}, u32[]{:S(2)}) collective-permute-start(bf16[48,640]{1,0:T(8,128)(2,1)S(1)} %get-tuple-element.29), channel_id=1, source_target_pairs={{0,12},{1,13},{2,14},{3,15},{4,8},{5,9},{6,10},{7,11},{8,4},{9,5},... | collective-permute-start | bytes 184328 | tf_op jit(solution)/shard_map/ppermute | solution.py:22
  18.8 0.5 %collective-permute-start.4 = (bf16[48,1024]{1,0:T(8,128)(2,1)S(1)}, bf16[48,1024]{1,0:T(8,128)(2,1)S(1)}, u32[]{:S(2)}, u32[]{:S(2)}) collective-permute-start(bf16[48,1024]{1,0:T(8,128)(2,1)S(1)} %collective-permute-done.1), channel_id=1, source_target_pairs={{0,2},{1,3},{2,0},{3,1},{4,6},{5,7},{6,4},{7,5},{8,10},{9,11},{10,... | collective-permute-start | bytes 294920 | tf_op jit(solution)/shard_map/ppermute | solution.py:22
  19.5 1.9 %collective-permute-start.7 = (bf16[48,1024]{1,0:T(8,128)(2,1)S(1)}, bf16[48,1024]{1,0:T(8,128)(2,1)S(1)}, u32[]{:S(2)}, u32[]{:S(2)}) collective-permute-start(bf16[48,1024]{1,0:T(8,128)(2,1)S(1)} %collective-permute-done.5), channel_id=1, source_target_pairs={{0,2},{1,3},{2,0},{3,1},{4,6},{5,7},{6,4},{7,5},{8,10},{9,11},{10,... | collective-permute-start | bytes 294920 | tf_op jit(solution)/shard_map/ppermute | solution.py:22
  21.4 0.2 collective-permute-start.11
  21.6 0.9 %collective-permute-done.3.refs_3_ = bf16[48,640]{1,0:T(8,128)(2,1)S(1)} collective-permute-done((bf16[48,640]{1,0:T(8,128)(2,1)S(1)}, bf16[48,640]{1,0:T(8,128)(2,1)S(1)}, u32[]{:S(2)}, u32[]{:S(2)}) %collective-permute-start.3) | collective-permute-done | bytes 61472 | tf_op jit(solution)/shard_map/ppermute | solution.py:22
  22.6 0.9 %attend_near.1 = (f32[5,192,128]{2,1,0:T(8,128)S(1)}, f32[5,192,256]{2,1,0:T(8,128)S(1)}) custom-call(bf16[192,640]{1,0:T(8,128)(2,1)S(1)} %collect.1.refs_0_, bf16[192,1024]{1,0:T(8,128)(2,1)S(1)} %pad_maximum_fusion.1.refs_1_, bf16[192,1024]{1,0:T(8,128)(2,1)S(1)} %collective-permute-done.8.refs_2_), custom_call_target="tpu_custom_call" | custom-call | flops 1000000000 | bytes 4000000 | tf_op jit(solution)/shard_map/attend_near/pallas_call | solution.py:405
  23.5 0.7 %collective-permute-done.4.refs_1_ = bf16[48,1024]{1,0:T(8,128)(2,1)S(1)} collective-permute-done((bf16[48,1024]{1,0:T(8,128)(2,1)S(1)}, bf16[48,1024]{1,0:T(8,128)(2,1)S(1)}, u32[]{:S(2)}, u32[]{:S(2)}) %collective-permute-start.4) | collective-permute-done | bytes 98336 | tf_op jit(solution)/shard_map/ppermute | solution.py:22
  24.2 1.3 %collective-permute-done.7.refs_2_ = bf16[48,1024]{1,0:T(8,128)(2,1)S(1)} collective-permute-done((bf16[48,1024]{1,0:T(8,128)(2,1)S(1)}, bf16[48,1024]{1,0:T(8,128)(2,1)S(1)}, u32[]{:S(2)}, u32[]{:S(2)}) %collective-permute-start.7) | collective-permute-done | bytes 98336 | tf_op jit(solution)/shard_map/ppermute | solution.py:22
  25.5 0.5 %collective-permute-start.9 = (bf16[48,1024]{1,0:T(8,128)(2,1)S(1)}, bf16[48,1024]{1,0:T(8,128)(2,1)S(1)}, u32[]{:S(2)}, u32[]{:S(2)}) collective-permute-start(bf16[48,1024]{1,0:T(8,128)(2,1)S(1)} %collective-permute-done.4.refs_1_), channel_id=1, source_target_pairs={{0,1},{1,0},{2,3},{3,2},{4,5},{5,4},{6,7},{7,6},{8,9},{9,8},{10,11... | collective-permute-start | bytes 294920 | tf_op jit(solution)/shard_map/ppermute | solution.py:22
  26.0 0.3 stream.1.refs_7_
  26.4 0.6 %attend_middle.1 = (f32[5,192,128]{2,1,0:T(8,128)S(1)}, f32[5,192,256]{2,1,0:T(8,128)S(1)}) custom-call(bf16[192,640]{1,0:T(8,128)(2,1)S(1)} %collect.1.refs_0_, bf16[96,1024]{1,0:T(8,128)(2,1)S(1)} %constant_dynamic-update-slice_fusion.refs_1_, bf16[96,1024]{1,0:T(8,128)(2,1)S(1)} %collective-permute-done.11.refs_2_, ...), custom_call_target="tpu_custom_call" | custom-call | flops 1000000000 | bytes 4000000 | tf_op jit(solution)/shard_map/attend_middle/pallas_call | solution.py:405
  27.0 0.7 %attend_far.1.own = bf16[96,128]{1,0:T(8,128)(2,1)S(1)} custom-call(bf16[192,640]{1,0:T(8,128)(2,1)S(1)} %collect.1.refs_0_, bf16[48,1024]{1,0:T(8,128)(2,1)S(1)} %collective-permute-done.4.refs_1_, bf16[48,1024]{1,0:T(8,128)(2,1)S(1)} %collective-permute-done.7.refs_2_, bf16[48,1024]{1,0:T(8,128)(2,1)S(1)} %collective-permute-done.9.refs_3_, ...), custom_call_target="tpu_custom_call" | custom-call | flops 1000000000 | bytes 4000000 | tf_op jit(solution)/shard_map/attend_far/pallas_call | solution.py:405
  27.8 1.6 %collective-permute-start.12 = (bf16[96,128]{1,0:T(8,128)(2,1)S(1)}, bf16[96,128]{1,0:T(8,128)(2,1)S(1)}, u32[]{:S(2)}, u32[]{:S(2)}) collective-permute-start(bf16[96,128]{1,0:T(8,128)(2,1)S(1)} %attend_far.1.own), channel_id=1, source_target_pairs={{0,12},{1,13},{2,14},{3,15},{4,8},{5,9},{6,10},{7,11},{8,4},{9,5},... | collective-permute-start | bytes 73736 | tf_op jit(solution)/shard_map/ppermute | solution.py:22
  29.4 1.2 %collective-permute-start.13 = (bf16[96,128]{1,0:T(8,128)(2,1)S(1)}, bf16[96,128]{1,0:T(8,128)(2,1)S(1)}, u32[]{:S(2)}, u32[]{:S(2)}) collective-permute-start(bf16[96,128]{1,0:T(8,128)(2,1)S(1)} %attend_far.1.own), channel_id=1, source_target_pairs={{0,8},{1,9},{2,10},{3,11},{4,12},{5,13},{6,14},{7,15},{8,0},{9,1},... | collective-permute-start | bytes 73736 | tf_op jit(solution)/shard_map/ppermute | solution.py:22
  30.6 1.6 %collective-permute-start.14 = (bf16[96,128]{1,0:T(8,128)(2,1)S(1)}, bf16[96,128]{1,0:T(8,128)(2,1)S(1)}, u32[]{:S(2)}, u32[]{:S(2)}) collective-permute-start(bf16[96,128]{1,0:T(8,128)(2,1)S(1)} %attend_far.1.own), channel_id=1, source_target_pairs={{0,4},{1,5},{2,6},{3,7},{4,0},{5,1},{6,2},{7,3},{8,12},{9,13},{10,... | collective-permute-start | bytes 73736 | tf_op jit(solution)/shard_map/ppermute | solution.py:22
  32.2 1.3 %collective-permute-done.12.three = bf16[96,128]{1,0:T(8,128)(2,1)S(1)} collective-permute-done((bf16[96,128]{1,0:T(8,128)(2,1)S(1)}, bf16[96,128]{1,0:T(8,128)(2,1)S(1)}, u32[]{:S(2)}, u32[]{:S(2)}) %collective-permute-start.12) | collective-permute-done | bytes 24608 | tf_op jit(solution)/shard_map/ppermute | solution.py:22
  33.6 0.7 %collective-permute-done.13.two = bf16[96,128]{1,0:T(8,128)(2,1)S(1)} collective-permute-done((bf16[96,128]{1,0:T(8,128)(2,1)S(1)}, bf16[96,128]{1,0:T(8,128)(2,1)S(1)}, u32[]{:S(2)}, u32[]{:S(2)}) %collective-permute-start.13) | collective-permute-done | bytes 24608 | tf_op jit(solution)/shard_map/ppermute | solution.py:22
  34.3 0.3 collective-permute-done.14.one
  34.7 1.4 %collective-permute-start.16 = (bf16[96,128]{1,0:T(8,128)(2,1)S(1)}, bf16[96,128]{1,0:T(8,128)(2,1)S(1)}, u32[]{:S(2)}, u32[]{:S(2)}) collective-permute-start(bf16[96,128]{1,0:T(8,128)(2,1)S(1)} %gather.1.refs_0_), channel_id=1, source_target_pairs={{0,2},{1,3},{2,0},{3,1},{4,6},{5,7},{6,4},{7,5},{8,10},{9,11},{10,... | collective-permute-start | bytes 73736 | tf_op jit(solution)/shard_map/ppermute | solution.py:22
  36.2 0.4 collective-permute-start.17
  36.6 0.3 and_convert_fusion.refs_4_
  36.9 1.3 %collective-permute-done.15.refs_1_ = bf16[96,128]{1,0:T(8,128)(2,1)S(1)} collective-permute-done((bf16[96,128]{1,0:T(8,128)(2,1)S(1)}, bf16[96,128]{1,0:T(8,128)(2,1)S(1)}, u32[]{:S(2)}, u32[]{:S(2)}) %collective-permute-start.15) | collective-permute-done | bytes 24608 | tf_op jit(solution)/shard_map/ppermute | solution.py:22
  38.1 0.5 %collective-permute-done.16.refs_2_ = bf16[96,128]{1,0:T(8,128)(2,1)S(1)} collective-permute-done((bf16[96,128]{1,0:T(8,128)(2,1)S(1)}, bf16[96,128]{1,0:T(8,128)(2,1)S(1)}, u32[]{:S(2)}, u32[]{:S(2)}) %collective-permute-start.16) | collective-permute-done | bytes 24608 | tf_op jit(solution)/shard_map/ppermute | solution.py:22
  38.6 4.6 %finish.1 = bf16[3,2,32,384]{3,2,1,0:T(8,128)(2,1)} custom-call(s32[1]{0:T(128)} %bitcast.index, bf16[96,128]{1,0:T(8,128)(2,1)S(1)} %gather.1.refs_0_, bf16[96,128]{1,0:T(8,128)(2,1)S(1)} %collective-permute-done.15.refs_1_, bf16[96,128]{1,0:T(8,128)(2,1)S(1)} %collective-permute-done.16.refs_2_, bf16[96,128]{1,0:T(8,128)(2,1)S(1)} %collective-permute-done.17.refs_3_, ...), custom_call_target="tpu_custom_call" | custom-call | tf_op jit(solution)/shard_map/finish/pallas_call | solution.py:439
  (45 shorter events, 0.8 us)
Async XLA Ops:
  1.8 13.0 %collective-permute-start.1 = (bf16[48,1024]{1,0:T(8,128)(2,1)S(1)}, bf16[48,1024]{1,0:T(8,128)(2,1)S(1)}, u32[]{:S(2)}, u32[]{:S(2)}) collective-permute-start(bf16[48,1024]{1,0:T(8,128)(2,1)S(1)} %get-tuple-element.27), channel_id=1, source_target_pairs={{0,8},{1,9},{2,10},{3,11},{4,12},{5,13},{6,14},{7,15},{8,0},{9,1},... | collective-permute-start | bytes 294920 | tf_op jit(solution)/shard_map/ppermute | solution.py:22
  5.9 7.0 %collective-permute-start = (bf16[48,1664]{1,0:T(8,128)(2,1)S(1)}, bf16[48,1664]{1,0:T(8,128)(2,1)S(1)}, u32[]{:S(2)}, u32[]{:S(2)}) collective-permute-start(bf16[48,1664]{1,0:T(8,128)(2,1)S(1)} %pad_maximum_fusion.3), channel_id=1, source_target_pairs={{0,4},{1,5},{2,6},{3,7},{4,0},{5,1},{6,2},{7,3},{8,12},{9,13},{10,... | collective-permute-start | bytes 479240 | tf_op jit(solution)/shard_map/ppermute | solution.py:22
  7.5 11.9 %collective-permute-start.5 = (bf16[48,1024]{1,0:T(8,128)(2,1)S(1)}, bf16[48,1024]{1,0:T(8,128)(2,1)S(1)}, u32[]{:S(2)}, u32[]{:S(2)}) collective-permute-start(bf16[48,1024]{1,0:T(8,128)(2,1)S(1)} %get-tuple-element.30), channel_id=1, source_target_pairs={{0,12},{1,13},{2,14},{3,15},{4,8},{5,9},{6,10},{7,11},{8,4},{9,5},... | collective-permute-start | bytes 294920 | tf_op jit(solution)/shard_map/ppermute | solution.py:22
  12.9 6.4 %collective-permute-start.6 = (bf16[96,1024]{1,0:T(8,128)(2,1)S(1)}, bf16[96,1024]{1,0:T(8,128)(2,1)S(1)}, u32[]{:S(2)}, u32[]{:S(2)}) collective-permute-start(bf16[96,1024]{1,0:T(8,128)(2,1)S(1)} %pad_maximum_fusion.2), channel_id=1, source_target_pairs={{0,2},{1,3},{2,0},{3,1},{4,6},{5,7},{6,4},{7,5},{8,10},{9,11},{10,... | collective-permute-start | bytes 589832 | tf_op jit(solution)/shard_map/ppermute | solution.py:22
  14.7 6.6 %collective-permute-start.2 = (bf16[48,640]{1,0:T(8,128)(2,1)S(1)}, bf16[48,640]{1,0:T(8,128)(2,1)S(1)}, u32[]{:S(2)}, u32[]{:S(2)}) collective-permute-start(bf16[48,640]{1,0:T(8,128)(2,1)S(1)} %get-tuple-element.28), channel_id=1, source_target_pairs={{0,8},{1,9},{2,10},{3,11},{4,12},{5,13},{6,14},{7,15},{8,0},{9,1},... | collective-permute-start | bytes 184328 | tf_op jit(solution)/shard_map/ppermute | solution.py:22
  16.5 6.0 %collective-permute-start.3 = (bf16[48,640]{1,0:T(8,128)(2,1)S(1)}, bf16[48,640]{1,0:T(8,128)(2,1)S(1)}, u32[]{:S(2)}, u32[]{:S(2)}) collective-permute-start(bf16[48,640]{1,0:T(8,128)(2,1)S(1)} %get-tuple-element.29), channel_id=1, source_target_pairs={{0,12},{1,13},{2,14},{3,15},{4,8},{5,9},{6,10},{7,11},{8,4},{9,5},... | collective-permute-start | bytes 184328 | tf_op jit(solution)/shard_map/ppermute | solution.py:22
  18.8 5.4 %collective-permute-start.4 = (bf16[48,1024]{1,0:T(8,128)(2,1)S(1)}, bf16[48,1024]{1,0:T(8,128)(2,1)S(1)}, u32[]{:S(2)}, u32[]{:S(2)}) collective-permute-start(bf16[48,1024]{1,0:T(8,128)(2,1)S(1)} %collective-permute-done.1), channel_id=1, source_target_pairs={{0,2},{1,3},{2,0},{3,1},{4,6},{5,7},{6,4},{7,5},{8,10},{9,11},{10,... | collective-permute-start | bytes 294920 | tf_op jit(solution)/shard_map/ppermute | solution.py:22
  19.4 3.2 %collective-permute-start.8 = (bf16[192,1024]{1,0:T(8,128)(2,1)S(1)}, bf16[192,1024]{1,0:T(8,128)(2,1)S(1)}, u32[]{:S(2)}, u32[]{:S(2)}) collective-permute-start(bf16[192,1024]{1,0:T(8,128)(2,1)S(1)} %pad_maximum_fusion.1.refs_1_), channel_id=1, source_target_pairs={{0,1},{1,0},{2,3},{3,2},{4,5},{5,4},{6,7},{7,6},{8,9},{9,8},{10,11... | collective-permute-start | bytes 1179656 | tf_op jit(solution)/shard_map/ppermute | solution.py:22
  19.5 6.1 %collective-permute-start.7 = (bf16[48,1024]{1,0:T(8,128)(2,1)S(1)}, bf16[48,1024]{1,0:T(8,128)(2,1)S(1)}, u32[]{:S(2)}, u32[]{:S(2)}) collective-permute-start(bf16[48,1024]{1,0:T(8,128)(2,1)S(1)} %collective-permute-done.5), channel_id=1, source_target_pairs={{0,2},{1,3},{2,0},{3,1},{4,6},{5,7},{6,4},{7,5},{8,10},{9,11},{10,... | collective-permute-start | bytes 294920 | tf_op jit(solution)/shard_map/ppermute | solution.py:22
  21.4 5.0 %collective-permute-start.11 = (bf16[96,1024]{1,0:T(8,128)(2,1)S(1)}, bf16[96,1024]{1,0:T(8,128)(2,1)S(1)}, u32[]{:S(2)}, u32[]{:S(2)}) collective-permute-start(bf16[96,1024]{1,0:T(8,128)(2,1)S(1)} %constant_dynamic-update-slice_fusion.refs_1_), channel_id=1, source_target_pairs={{0,1},{1,0},{2,3},{3,2},{4,5},{5,4},{6,7},{7,6},{8,9},{9,8},{10,11... | collective-permute-start | bytes 589832 | tf_op jit(solution)/shard_map/ppermute | solution.py:22
  22.5 16.1 %slice-start = ((s8[7962624]{0:T(1024)(128)(4,1)}), s8[4194304]{0:T(1024)(128)(4,1)S(1)}, s32[]{:S(2)}) async-start(s8[7962624]{0:T(1024)(128)(4,1)} %bitcast.8), calls=%async_computation | async-start | bytes 8388608
  22.5 16.1 %slice-start.1 = ((s8[7962624]{0:T(1024)(128)(4,1)}), s8[3768320]{0:T(1024)(128)(4,1)S(1)}, s32[]{:S(2)}) async-start(s8[7962624]{0:T(1024)(128)(4,1)} %bitcast.8), calls=%async_computation.1 | async-start | bytes 7536640
  22.5 3.5 %copy-start = (bf16[2560,64]{0,1:T(8,128)(2,1)S(1)}, bf16[2560,64]{0,1:T(8,128)(2,1)}, u32[]{:S(2)}) copy-start(bf16[2560,64]{0,1:T(8,128)(2,1)} %param.13) | copy-start | bytes 983044
  22.5 3.5 %copy-start.1 = (bf16[3,1,16,2560]{3,2,1,0:T(8,128)(2,1)S(1)}, bf16[3,1,16,2560]{3,2,1,0:T(8,128)(2,1)}, u32[]{:S(2)}) copy-start(bf16[3,1,16,2560]{3,2,1,0:T(8,128)(2,1)} %param.12) | copy-start | bytes 737284
  25.5 1.5 %collective-permute-start.10 = (bf16[48,1024]{1,0:T(8,128)(2,1)S(1)}, bf16[48,1024]{1,0:T(8,128)(2,1)S(1)}, u32[]{:S(2)}, u32[]{:S(2)}) collective-permute-start(bf16[48,1024]{1,0:T(8,128)(2,1)S(1)} %collective-permute-done.7.refs_2_), channel_id=1, source_target_pairs={{0,1},{1,0},{2,3},{3,2},{4,5},{5,4},{6,7},{7,6},{8,9},{9,8},{10,11... | collective-permute-start | bytes 294920 | tf_op jit(solution)/shard_map/ppermute | solution.py:22
  25.5 1.5 %collective-permute-start.9 = (bf16[48,1024]{1,0:T(8,128)(2,1)S(1)}, bf16[48,1024]{1,0:T(8,128)(2,1)S(1)}, u32[]{:S(2)}, u32[]{:S(2)}) collective-permute-start(bf16[48,1024]{1,0:T(8,128)(2,1)S(1)} %collective-permute-done.4.refs_1_), channel_id=1, source_target_pairs={{0,1},{1,0},{2,3},{3,2},{4,5},{5,4},{6,7},{7,6},{8,9},{9,8},{10,11... | collective-permute-start | bytes 294920 | tf_op jit(solution)/shard_map/ppermute | solution.py:22
  27.0 9.9 %copy-start.2 = (f32[384]{0:T(512)S(1)}, f32[384]{0:T(512)}, u32[]{:S(2)}) copy-start(f32[384]{0:T(512)} %param.15) | copy-start | bytes 4612
  27.0 9.9 %copy-start.3 = (f32[384]{0:T(512)S(1)}, f32[384]{0:T(512)}, u32[]{:S(2)}) copy-start(f32[384]{0:T(512)} %param.16) | copy-start | bytes 4612
  27.8 5.8 %collective-permute-start.12 = (bf16[96,128]{1,0:T(8,128)(2,1)S(1)}, bf16[96,128]{1,0:T(8,128)(2,1)S(1)}, u32[]{:S(2)}, u32[]{:S(2)}) collective-permute-start(bf16[96,128]{1,0:T(8,128)(2,1)S(1)} %attend_far.1.own), channel_id=1, source_target_pairs={{0,12},{1,13},{2,14},{3,15},{4,8},{5,9},{6,10},{7,11},{8,4},{9,5},... | collective-permute-start | bytes 73736 | tf_op jit(solution)/shard_map/ppermute | solution.py:22
  29.4 4.9 %collective-permute-start.13 = (bf16[96,128]{1,0:T(8,128)(2,1)S(1)}, bf16[96,128]{1,0:T(8,128)(2,1)S(1)}, u32[]{:S(2)}, u32[]{:S(2)}) collective-permute-start(bf16[96,128]{1,0:T(8,128)(2,1)S(1)} %attend_far.1.own), channel_id=1, source_target_pairs={{0,8},{1,9},{2,10},{3,11},{4,12},{5,13},{6,14},{7,15},{8,0},{9,1},... | collective-permute-start | bytes 73736 | tf_op jit(solution)/shard_map/ppermute | solution.py:22
  30.6 3.9 %collective-permute-start.14 = (bf16[96,128]{1,0:T(8,128)(2,1)S(1)}, bf16[96,128]{1,0:T(8,128)(2,1)S(1)}, u32[]{:S(2)}, u32[]{:S(2)}) collective-permute-start(bf16[96,128]{1,0:T(8,128)(2,1)S(1)} %attend_far.1.own), channel_id=1, source_target_pairs={{0,4},{1,5},{2,6},{3,7},{4,0},{5,1},{6,2},{7,3},{8,12},{9,13},{10,... | collective-permute-start | bytes 73736 | tf_op jit(solution)/shard_map/ppermute | solution.py:22
  34.6 3.5 %collective-permute-start.15 = (bf16[96,128]{1,0:T(8,128)(2,1)S(1)}, bf16[96,128]{1,0:T(8,128)(2,1)S(1)}, u32[]{:S(2)}, u32[]{:S(2)}) collective-permute-start(bf16[96,128]{1,0:T(8,128)(2,1)S(1)} %gather.1.refs_0_), channel_id=1, source_target_pairs={{0,3},{1,2},{2,1},{3,0},{4,7},{5,6},{6,5},{7,4},{8,11},{9,10},{10,... | collective-permute-start | bytes 73736 | tf_op jit(solution)/shard_map/ppermute | solution.py:22
  34.7 3.9 %collective-permute-start.16 = (bf16[96,128]{1,0:T(8,128)(2,1)S(1)}, bf16[96,128]{1,0:T(8,128)(2,1)S(1)}, u32[]{:S(2)}, u32[]{:S(2)}) collective-permute-start(bf16[96,128]{1,0:T(8,128)(2,1)S(1)} %gather.1.refs_0_), channel_id=1, source_target_pairs={{0,2},{1,3},{2,0},{3,1},{4,6},{5,7},{6,4},{7,5},{8,10},{9,11},{10,... | collective-permute-start | bytes 73736 | tf_op jit(solution)/shard_map/ppermute | solution.py:22
  36.2 2.5 %collective-permute-start.17 = (bf16[96,128]{1,0:T(8,128)(2,1)S(1)}, bf16[96,128]{1,0:T(8,128)(2,1)S(1)}, u32[]{:S(2)}, u32[]{:S(2)}) collective-permute-start(bf16[96,128]{1,0:T(8,128)(2,1)S(1)} %gather.1.refs_0_), channel_id=1, source_target_pairs={{0,1},{1,0},{2,3},{3,2},{4,5},{5,4},{6,7},{7,6},{8,9},{9,8},{10,11... | collective-permute-start | bytes 73736 | tf_op jit(solution)/shard_map/ppermute | solution.py:22

commit v7 on v6

--- a/solution.py
+++ b/solution.py
@@ -60,19 +60,26 @@
         copy.start()
     half = w.shape[0]
     wide = 2 * half
-    low = lax.broadcasted_iota(jnp.int32, (tokens, wide), 1) < half
-
-    def head_through(head):
-        return through_twice(v_here, w_here, slice(head * depth, (head + 1) * depth))
+    pair_row = lax.broadcasted_iota(jnp.int32, (wide, 2 * depth), 0) // half
+    pair_column = lax.broadcasted_iota(jnp.int32, (wide, 2 * depth), 1) // depth
+    own = (pair_row == pair_column).astype(jnp.bfloat16)
+
+    def pair_through(columns):
+        weight = w_here[:, columns]
+        weight = jnp.concatenate([weight, weight], axis=0) * own
+        return lax.dot_general(
+            v_here[:, columns], weight, (((1,), (1,)), ((), ())), preferred_element_type=jnp.float32
+        )
 
     for copy in whole:
         copy.wait()
     for owner in range(SPLIT):
         for pair in range((heads + 1) // 2):
-            first = owner * heads + 2 * pair
-            both = head_through(first)
+            at = (owner * heads + 2 * pair) * depth
             if 2 * pair + 1 < heads:
-                both = jnp.where(low, both, head_through(first + 1))
+                both = pair_through(slice(at, at + 2 * depth))
+            else:
+                both = through_twice(v_here, w_here, slice(at, at + depth))
             projected[owner, :, pair * wide : (pair + 1) * wide] = both.astype(jnp.bfloat16)
     for step in range(SPLIT):
         kv_out[step][:, group:] = projected[place ^ step]
@@ -154,7 +161,7 @@
 def collect_kernel(*refs):
     pieces, out = refs[:-1], refs[-1]
     tokens = pieces[0].shape[0]
-    for at, piece in enumerate(pieces):
+    for at, piece in zip((0, 1, 3, 2), pieces):
         out[at * tokens : (at + 1) * tokens, :] = piece[...]
 
 
@@ -398,7 +405,7 @@
         compiler_params=pltpu.CompilerParams(vmem_limit_bytes=4 * 2**20),
         cost_estimate=pl.CostEstimate(flops=5 * 10**9, bytes_accessed=10**6, transcendentals=0),
         name="collect",
-    )(*q)
+    )(q[0], q[1], q[3], q[2])
     state = [jax.ShapeDtypeStruct((heads, SPLIT * tokens, size), f32) for size in (wide, 2 * wide)]
 
     def attended(blocks, carried, last, name):

time: 43.4 us -> 43.3 us (level)
  no operation moved by 1% of the time
where the time goes in v7:
time: 43.3 us; the launch traced here: 43.1 us
  starting transfers between devices  20.9 us (48%)
  waiting for transfers between devices  10.2 us (24%)
  Pallas kernels  8.91 us (21%)
  other arithmetic  2.55 us (6%)
    ppermute x18, starting transfers between devices, exchanged(): return lax.ppermute(value, 'seq', pairs)  20.9 us
    ppermute x18, waiting for transfers between devices, exchanged(): return lax.ppermute(value, 'seq', pairs)  10.2 us
    pallas_call x1, Pallas kernels, shards(): pl.pallas_call(functools.partial(finish_kernel, frames, n, cols, [0] + or...  4.64 us
    pallas_call x3, Pallas kernels, attended(): pl.pallas_call(functools.partial(attend_kernel, depth, heads, not carried...  2.29 us
    concatenate x1, other arithmetic, widened(): whole = jnp.concatenate(blocks, axis=-1)  1.84 us
    pallas_call x1, Pallas kernels, shards(): pl.pallas_call(functools.partial(prepare_kernel, depth, heads), out_shape...  1.59 us
  transfers between devices with their start and end apart: 18, of which 9 were waited for; matrix products, arithmetic and copies ran while one was open for 6% of the time, Pallas kernels for 4%

profile of v7, /device:TPU:0, one launch (start us, length us, event | category | flops | bytes accessed | tf_op | source)
XLA Modules:
  0.0 43.1 jit_solution(11121780834652910255)
XLA Ops:
  0.0 1.6 %prepare.1 = (bf16[48,1024]{1,0:T(8,128)(2,1)S(1)}, bf16[48,1024]{1,0:T(8,128)(2,1)S(1)}, bf16[48,1024]{1,0:T(8,128)(2,1)S(1)}, bf16[48,1024]{1,0:T(8,128)(2,1)S...) custom-call(s32[1]{0:T(128)} %bitcast.index, ...), custom_call_target="tpu_custom_call" | custom-call | tf_op jit(solution)/shard_map/prepare/pallas_call | solution.py:351
  1.6 4.1 %collective-permute-start.1 = (bf16[48,1024]{1,0:T(8,128)(2,1)S(1)}, bf16[48,1024]{1,0:T(8,128)(2,1)S(1)}, u32[]{:S(2)}, u32[]{:S(2)}) collective-permute-start(bf16[48,1024]{1,0:T(8,128)(2,1)S(1)} %get-tuple-element.27), channel_id=1, source_target_pairs={{0,8},{1,9},{2,10},{3,11},{4,12},{5,13},{6,14},{7,15},{8,0},{9,1},... | collective-permute-start | bytes 294920 | tf_op jit(solution)/shard_map/ppermute | solution.py:22
  5.7 1.6 %collective-permute-start = (bf16[48,1664]{1,0:T(8,128)(2,1)S(1)}, bf16[48,1664]{1,0:T(8,128)(2,1)S(1)}, u32[]{:S(2)}, u32[]{:S(2)}) collective-permute-start(bf16[48,1664]{1,0:T(8,128)(2,1)S(1)} %pad_maximum_fusion.3), channel_id=1, source_target_pairs={{0,4},{1,5},{2,6},{3,7},{4,0},{5,1},{6,2},{7,3},{8,12},{9,13},{10,... | collective-permute-start | bytes 479240 | tf_op jit(solution)/shard_map/ppermute | solution.py:22
  7.4 1.8 %fusion.7 = bf16[3,4,4,16,1536]{4,3,2,1,0:T(8,128)(2,1)S(1)} fusion(bf16[3,3,3,16,384]{4,3,2,1,0:T(8,128)(2,1)} %param.14), kind=kLoop, calls=%fused_computation.13 | loop fusion | flops 23592960 | bytes 2691072 | tf_op jit(solution)/shard_map/concatenate | solution.py:310
  9.6 0.2 pad_maximum_fusion
  9.8 2.8 %collective-permute-done = bf16[48,1664]{1,0:T(8,128)(2,1)S(1)} collective-permute-done((bf16[48,1664]{1,0:T(8,128)(2,1)S(1)}, bf16[48,1664]{1,0:T(8,128)(2,1)S(1)}, u32[]{:S(2)}, u32[]{:S(2)}) %collective-permute-start) | collective-permute-done | bytes 159776 | tf_op jit(solution)/shard_map/ppermute | solution.py:22
  12.7 1.8 %collective-permute-start.6 = (bf16[96,1024]{1,0:T(8,128)(2,1)S(1)}, bf16[96,1024]{1,0:T(8,128)(2,1)S(1)}, u32[]{:S(2)}, u32[]{:S(2)}) collective-permute-start(bf16[96,1024]{1,0:T(8,128)(2,1)S(1)} %pad_maximum_fusion.2), channel_id=1, source_target_pairs={{0,2},{1,3},{2,0},{3,1},{4,6},{5,7},{6,4},{7,5},{8,10},{9,11},{10,... | collective-permute-start | bytes 589832 | tf_op jit(solution)/shard_map/ppermute | solution.py:22
  14.6 2.0 %collective-permute-start.2 = (bf16[48,640]{1,0:T(8,128)(2,1)S(1)}, bf16[48,640]{1,0:T(8,128)(2,1)S(1)}, u32[]{:S(2)}, u32[]{:S(2)}) collective-permute-start(bf16[48,640]{1,0:T(8,128)(2,1)S(1)} %get-tuple-element.28), channel_id=1, source_target_pairs={{0,12},{1,13},{2,14},{3,15},{4,8},{5,9},{6,10},{7,11},{8,4},{9,5},... | collective-permute-start | bytes 184328 | tf_op jit(solution)/shard_map/ppermute | solution.py:22
  16.6 1.1 %collective-permute-start.3 = (bf16[48,640]{1,0:T(8,128)(2,1)S(1)}, bf16[48,640]{1,0:T(8,128)(2,1)S(1)}, u32[]{:S(2)}, u32[]{:S(2)}) collective-permute-start(bf16[48,640]{1,0:T(8,128)(2,1)S(1)} %get-tuple-element.29), channel_id=1, source_target_pairs={{0,8},{1,9},{2,10},{3,11},{4,12},{5,13},{6,14},{7,15},{8,0},{9,1},... | collective-permute-start | bytes 184328 | tf_op jit(solution)/shard_map/ppermute | solution.py:22
  17.7 0.5 %collective-permute-start.4 = (bf16[48,1024]{1,0:T(8,128)(2,1)S(1)}, bf16[48,1024]{1,0:T(8,128)(2,1)S(1)}, u32[]{:S(2)}, u32[]{:S(2)}) collective-permute-start(bf16[48,1024]{1,0:T(8,128)(2,1)S(1)} %collective-permute-done.1), channel_id=1, source_target_pairs={{0,2},{1,3},{2,0},{3,1},{4,6},{5,7},{6,4},{7,5},{8,10},{9,11},{10,... | collective-permute-start | bytes 294920 | tf_op jit(solution)/shard_map/ppermute | solution.py:22
  18.2 0.6 %collective-permute-done.6 = bf16[96,1024]{1,0:T(8,128)(2,1)S(1)} collective-permute-done((bf16[96,1024]{1,0:T(8,128)(2,1)S(1)}, bf16[96,1024]{1,0:T(8,128)(2,1)S(1)}, u32[]{:S(2)}, u32[]{:S(2)}) %collective-permute-start.6) | collective-permute-done | bytes 196640 | tf_op jit(solution)/shard_map/ppermute | solution.py:22
  19.0 2.5 %collective-permute-start.7 = (bf16[48,1024]{1,0:T(8,128)(2,1)S(1)}, bf16[48,1024]{1,0:T(8,128)(2,1)S(1)}, u32[]{:S(2)}, u32[]{:S(2)}) collective-permute-start(bf16[48,1024]{1,0:T(8,128)(2,1)S(1)} %collective-permute-done.5), channel_id=1, source_target_pairs={{0,2},{1,3},{2,0},{3,1},{4,6},{5,7},{6,4},{7,5},{8,10},{9,11},{10,... | collective-permute-start | bytes 294920 | tf_op jit(solution)/shard_map/ppermute | solution.py:22
  21.5 0.2 collective-permute-start.11
  21.7 0.4 collective-permute-done.3.refs_3_
  22.1 0.9 %attend_near.1 = (f32[5,192,128]{2,1,0:T(8,128)S(1)}, f32[5,192,256]{2,1,0:T(8,128)S(1)}) custom-call(bf16[192,640]{1,0:T(8,128)(2,1)S(1)} %collect.1.refs_0_, bf16[192,1024]{1,0:T(8,128)(2,1)S(1)} %pad_maximum_fusion.1.refs_1_, bf16[192,1024]{1,0:T(8,128)(2,1)S(1)} %collective-permute-done.8.refs_2_), custom_call_target="tpu_custom_call" | custom-call | flops 1000000000 | bytes 4000000 | tf_op jit(solution)/shard_map/attend_near/pallas_call | solution.py:412
  23.1 1.7 %collective-permute-done.7.refs_2_ = bf16[48,1024]{1,0:T(8,128)(2,1)S(1)} collective-permute-done((bf16[48,1024]{1,0:T(8,128)(2,1)S(1)}, bf16[48,1024]{1,0:T(8,128)(2,1)S(1)}, u32[]{:S(2)}, u32[]{:S(2)}) %collective-permute-start.7) | collective-permute-done | bytes 98336 | tf_op jit(solution)/shard_map/ppermute | solution.py:22
  24.8 0.5 %collective-permute-start.9 = (bf16[48,1024]{1,0:T(8,128)(2,1)S(1)}, bf16[48,1024]{1,0:T(8,128)(2,1)S(1)}, u32[]{:S(2)}, u32[]{:S(2)}) collective-permute-start(bf16[48,1024]{1,0:T(8,128)(2,1)S(1)} %collective-permute-done.4.refs_1_), channel_id=1, source_target_pairs={{0,1},{1,0},{2,3},{3,2},{4,5},{5,4},{6,7},{7,6},{8,9},{9,8},{10,11... | collective-permute-start | bytes 294920 | tf_op jit(solution)/shard_map/ppermute | solution.py:22
  25.3 0.3 stream.1.refs_7_
  25.7 0.6 %attend_middle.1 = (f32[5,192,128]{2,1,0:T(8,128)S(1)}, f32[5,192,256]{2,1,0:T(8,128)S(1)}) custom-call(bf16[192,640]{1,0:T(8,128)(2,1)S(1)} %collect.1.refs_0_, bf16[96,1024]{1,0:T(8,128)(2,1)S(1)} %constant_dynamic-update-slice_fusion.refs_1_, bf16[96,1024]{1,0:T(8,128)(2,1)S(1)} %collective-permute-done.11.refs_2_, ...), custom_call_target="tpu_custom_call" | custom-call | flops 1000000000 | bytes 4000000 | tf_op jit(solution)/shard_map/attend_middle/pallas_call | solution.py:412
  26.3 0.7 %attend_far.1.own = bf16[96,128]{1,0:T(8,128)(2,1)S(1)} custom-call(bf16[192,640]{1,0:T(8,128)(2,1)S(1)} %collect.1.refs_0_, bf16[48,1024]{1,0:T(8,128)(2,1)S(1)} %collective-permute-done.4.refs_1_, bf16[48,1024]{1,0:T(8,128)(2,1)S(1)} %collective-permute-done.7.refs_2_, bf16[48,1024]{1,0:T(8,128)(2,1)S(1)} %collective-permute-done.9.refs_3_, ...), custom_call_target="tpu_custom_call" | custom-call | flops 1000000000 | bytes 4000000 | tf_op jit(solution)/shard_map/attend_far/pallas_call | solution.py:412
  27.1 2.3 %collective-permute-start.12 = (bf16[96,128]{1,0:T(8,128)(2,1)S(1)}, bf16[96,128]{1,0:T(8,128)(2,1)S(1)}, u32[]{:S(2)}, u32[]{:S(2)}) collective-permute-start(bf16[96,128]{1,0:T(8,128)(2,1)S(1)} %attend_far.1.own), channel_id=1, source_target_pairs={{0,12},{1,13},{2,14},{3,15},{4,8},{5,9},{6,10},{7,11},{8,4},{9,5},... | collective-permute-start | bytes 73736 | tf_op jit(solution)/shard_map/ppermute | solution.py:22
  29.4 1.1 %collective-permute-start.13 = (bf16[96,128]{1,0:T(8,128)(2,1)S(1)}, bf16[96,128]{1,0:T(8,128)(2,1)S(1)}, u32[]{:S(2)}, u32[]{:S(2)}) collective-permute-start(bf16[96,128]{1,0:T(8,128)(2,1)S(1)} %attend_far.1.own), channel_id=1, source_target_pairs={{0,8},{1,9},{2,10},{3,11},{4,12},{5,13},{6,14},{7,15},{8,0},{9,1},... | collective-permute-start | bytes 73736 | tf_op jit(solution)/shard_map/ppermute | solution.py:22
  30.5 1.1 %collective-permute-start.14 = (bf16[96,128]{1,0:T(8,128)(2,1)S(1)}, bf16[96,128]{1,0:T(8,128)(2,1)S(1)}, u32[]{:S(2)}, u32[]{:S(2)}) collective-permute-start(bf16[96,128]{1,0:T(8,128)(2,1)S(1)} %attend_far.1.own), channel_id=1, source_target_pairs={{0,4},{1,5},{2,6},{3,7},{4,0},{5,1},{6,2},{7,3},{8,12},{9,13},{10,... | collective-permute-start | bytes 73736 | tf_op jit(solution)/shard_map/ppermute | solution.py:22
  31.6 1.4 %collective-permute-done.12.three = bf16[96,128]{1,0:T(8,128)(2,1)S(1)} collective-permute-done((bf16[96,128]{1,0:T(8,128)(2,1)S(1)}, bf16[96,128]{1,0:T(8,128)(2,1)S(1)}, u32[]{:S(2)}, u32[]{:S(2)}) %collective-permute-start.12) | collective-permute-done | bytes 24608 | tf_op jit(solution)/shard_map/ppermute | solution.py:22
  32.9 1.2 %collective-permute-done.13.two = bf16[96,128]{1,0:T(8,128)(2,1)S(1)} collective-permute-done((bf16[96,128]{1,0:T(8,128)(2,1)S(1)}, bf16[96,128]{1,0:T(8,128)(2,1)S(1)}, u32[]{:S(2)}, u32[]{:S(2)}) %collective-permute-start.13) | collective-permute-done | bytes 24608 | tf_op jit(solution)/shard_map/ppermute | solution.py:22
  34.1 0.3 collective-permute-done.14.one
  34.5 1.5 %collective-permute-start.16 = (bf16[96,128]{1,0:T(8,128)(2,1)S(1)}, bf16[96,128]{1,0:T(8,128)(2,1)S(1)}, u32[]{:S(2)}, u32[]{:S(2)}) collective-permute-start(bf16[96,128]{1,0:T(8,128)(2,1)S(1)} %gather.1.refs_0_), channel_id=1, source_target_pairs={{0,2},{1,3},{2,0},{3,1},{4,6},{5,7},{6,4},{7,5},{8,10},{9,11},{10,... | collective-permute-start | bytes 73736 | tf_op jit(solution)/shard_map/ppermute | solution.py:22
  36.0 0.4 collective-permute-start.17
  36.4 0.3 and_convert_fusion.refs_4_
  36.7 1.3 %collective-permute-done.15.refs_1_ = bf16[96,128]{1,0:T(8,128)(2,1)S(1)} collective-permute-done((bf16[96,128]{1,0:T(8,128)(2,1)S(1)}, bf16[96,128]{1,0:T(8,128)(2,1)S(1)}, u32[]{:S(2)}, u32[]{:S(2)}) %collective-permute-start.15) | collective-permute-done | bytes 24608 | tf_op jit(solution)/shard_map/ppermute | solution.py:22
  38.0 0.4 collective-permute-done.16.refs_2_
  38.5 4.6 %finish.1 = bf16[3,2,32,384]{3,2,1,0:T(8,128)(2,1)} custom-call(s32[1]{0:T(128)} %bitcast.index, bf16[96,128]{1,0:T(8,128)(2,1)S(1)} %gather.1.refs_0_, bf16[96,128]{1,0:T(8,128)(2,1)S(1)} %collective-permute-done.15.refs_1_, bf16[96,128]{1,0:T(8,128)(2,1)S(1)} %collective-permute-done.16.refs_2_, bf16[96,128]{1,0:T(8,128)(2,1)S(1)} %collective-permute-done.17.refs_3_, ...), custom_call_target="tpu_custom_call" | custom-call | tf_op jit(solution)/shard_map/finish/pallas_call | solution.py:446
  (45 shorter events, 0.8 us)
Async XLA Ops:
  1.6 13.0 %collective-permute-start.1 = (bf16[48,1024]{1,0:T(8,128)(2,1)S(1)}, bf16[48,1024]{1,0:T(8,128)(2,1)S(1)}, u32[]{:S(2)}, u32[]{:S(2)}) collective-permute-start(bf16[48,1024]{1,0:T(8,128)(2,1)S(1)} %get-tuple-element.27), channel_id=1, source_target_pairs={{0,8},{1,9},{2,10},{3,11},{4,12},{5,13},{6,14},{7,15},{8,0},{9,1},... | collective-permute-start | bytes 294920 | tf_op jit(solution)/shard_map/ppermute | solution.py:22
  5.7 7.0 %collective-permute-start = (bf16[48,1664]{1,0:T(8,128)(2,1)S(1)}, bf16[48,1664]{1,0:T(8,128)(2,1)S(1)}, u32[]{:S(2)}, u32[]{:S(2)}) collective-permute-start(bf16[48,1664]{1,0:T(8,128)(2,1)S(1)} %pad_maximum_fusion.3), channel_id=1, source_target_pairs={{0,4},{1,5},{2,6},{3,7},{4,0},{5,1},{6,2},{7,3},{8,12},{9,13},{10,... | collective-permute-start | bytes 479240 | tf_op jit(solution)/shard_map/ppermute | solution.py:22
  7.4 11.6 %collective-permute-start.5 = (bf16[48,1024]{1,0:T(8,128)(2,1)S(1)}, bf16[48,1024]{1,0:T(8,128)(2,1)S(1)}, u32[]{:S(2)}, u32[]{:S(2)}) collective-permute-start(bf16[48,1024]{1,0:T(8,128)(2,1)S(1)} %get-tuple-element.30), channel_id=1, source_target_pairs={{0,12},{1,13},{2,14},{3,15},{4,8},{5,9},{6,10},{7,11},{8,4},{9,5},... | collective-permute-start | bytes 294920 | tf_op jit(solution)/shard_map/ppermute | solution.py:22
  12.7 6.1 %collective-permute-start.6 = (bf16[96,1024]{1,0:T(8,128)(2,1)S(1)}, bf16[96,1024]{1,0:T(8,128)(2,1)S(1)}, u32[]{:S(2)}, u32[]{:S(2)}) collective-permute-start(bf16[96,1024]{1,0:T(8,128)(2,1)S(1)} %pad_maximum_fusion.2), channel_id=1, source_target_pairs={{0,2},{1,3},{2,0},{3,1},{4,6},{5,7},{6,4},{7,5},{8,10},{9,11},{10,... | collective-permute-start | bytes 589832 | tf_op jit(solution)/shard_map/ppermute | solution.py:22
  14.6 6.9 %collective-permute-start.2 = (bf16[48,640]{1,0:T(8,128)(2,1)S(1)}, bf16[48,640]{1,0:T(8,128)(2,1)S(1)}, u32[]{:S(2)}, u32[]{:S(2)}) collective-permute-start(bf16[48,640]{1,0:T(8,128)(2,1)S(1)} %get-tuple-element.28), channel_id=1, source_target_pairs={{0,12},{1,13},{2,14},{3,15},{4,8},{5,9},{6,10},{7,11},{8,4},{9,5},... | collective-permute-start | bytes 184328 | tf_op jit(solution)/shard_map/ppermute | solution.py:22
  16.6 5.5 %collective-permute-start.3 = (bf16[48,640]{1,0:T(8,128)(2,1)S(1)}, bf16[48,640]{1,0:T(8,128)(2,1)S(1)}, u32[]{:S(2)}, u32[]{:S(2)}) collective-permute-start(bf16[48,640]{1,0:T(8,128)(2,1)S(1)} %get-tuple-element.29), channel_id=1, source_target_pairs={{0,8},{1,9},{2,10},{3,11},{4,12},{5,13},{6,14},{7,15},{8,0},{9,1},... | collective-permute-start | bytes 184328 | tf_op jit(solution)/shard_map/ppermute | solution.py:22
  17.7 5.4 %collective-permute-start.4 = (bf16[48,1024]{1,0:T(8,128)(2,1)S(1)}, bf16[48,1024]{1,0:T(8,128)(2,1)S(1)}, u32[]{:S(2)}, u32[]{:S(2)}) collective-permute-start(bf16[48,1024]{1,0:T(8,128)(2,1)S(1)} %collective-permute-done.1), channel_id=1, source_target_pairs={{0,2},{1,3},{2,0},{3,1},{4,6},{5,7},{6,4},{7,5},{8,10},{9,11},{10,... | collective-permute-start | bytes 294920 | tf_op jit(solution)/shard_map/ppermute | solution.py:22
  18.9 3.3 %collective-permute-start.8 = (bf16[192,1024]{1,0:T(8,128)(2,1)S(1)}, bf16[192,1024]{1,0:T(8,128)(2,1)S(1)}, u32[]{:S(2)}, u32[]{:S(2)}) collective-permute-start(bf16[192,1024]{1,0:T(8,128)(2,1)S(1)} %pad_maximum_fusion.1.refs_1_), channel_id=1, source_target_pairs={{0,1},{1,0},{2,3},{3,2},{4,5},{5,4},{6,7},{7,6},{8,9},{9,8},{10,11... | collective-permute-start | bytes 1179656 | tf_op jit(solution)/shard_map/ppermute | solution.py:22
  19.0 5.9 %collective-permute-start.7 = (bf16[48,1024]{1,0:T(8,128)(2,1)S(1)}, bf16[48,1024]{1,0:T(8,128)(2,1)S(1)}, u32[]{:S(2)}, u32[]{:S(2)}) collective-permute-start(bf16[48,1024]{1,0:T(8,128)(2,1)S(1)} %collective-permute-done.5), channel_id=1, source_target_pairs={{0,2},{1,3},{2,0},{3,1},{4,6},{5,7},{6,4},{7,5},{8,10},{9,11},{10,... | collective-permute-start | bytes 294920 | tf_op jit(solution)/shard_map/ppermute | solution.py:22
  21.5 4.2 %collective-permute-start.11 = (bf16[96,1024]{1,0:T(8,128)(2,1)S(1)}, bf16[96,1024]{1,0:T(8,128)(2,1)S(1)}, u32[]{:S(2)}, u32[]{:S(2)}) collective-permute-start(bf16[96,1024]{1,0:T(8,128)(2,1)S(1)} %constant_dynamic-update-slice_fusion.refs_1_), channel_id=1, source_target_pairs={{0,1},{1,0},{2,3},{3,2},{4,5},{5,4},{6,7},{7,6},{8,9},{9,8},{10,11... | collective-permute-start | bytes 589832 | tf_op jit(solution)/shard_map/ppermute | solution.py:22
  22.1 16.4 %slice-start = ((s8[7962624]{0:T(1024)(128)(4,1)}), s8[4194304]{0:T(1024)(128)(4,1)S(1)}, s32[]{:S(2)}) async-start(s8[7962624]{0:T(1024)(128)(4,1)} %bitcast.8), calls=%async_computation | async-start | bytes 8388608
  22.1 16.4 %slice-start.1 = ((s8[7962624]{0:T(1024)(128)(4,1)}), s8[3768320]{0:T(1024)(128)(4,1)S(1)}, s32[]{:S(2)}) async-start(s8[7962624]{0:T(1024)(128)(4,1)} %bitcast.8), calls=%async_computation.1 | async-start | bytes 7536640
  22.1 3.2 %copy-start = (bf16[2560,64]{0,1:T(8,128)(2,1)S(1)}, bf16[2560,64]{0,1:T(8,128)(2,1)}, u32[]{:S(2)}) copy-start(bf16[2560,64]{0,1:T(8,128)(2,1)} %param.13) | copy-start | bytes 983044
  22.1 3.2 %copy-start.1 = (bf16[3,1,16,2560]{3,2,1,0:T(8,128)(2,1)S(1)}, bf16[3,1,16,2560]{3,2,1,0:T(8,128)(2,1)}, u32[]{:S(2)}) copy-start(bf16[3,1,16,2560]{3,2,1,0:T(8,128)(2,1)} %param.12) | copy-start | bytes 737284
  24.8 1.5 %collective-permute-start.10 = (bf16[48,1024]{1,0:T(8,128)(2,1)S(1)}, bf16[48,1024]{1,0:T(8,128)(2,1)S(1)}, u32[]{:S(2)}, u32[]{:S(2)}) collective-permute-start(bf16[48,1024]{1,0:T(8,128)(2,1)S(1)} %collective-permute-done.7.refs_2_), channel_id=1, source_target_pairs={{0,1},{1,0},{2,3},{3,2},{4,5},{5,4},{6,7},{7,6},{8,9},{9,8},{10,11... | collective-permute-start | bytes 294920 | tf_op jit(solution)/shard_map/ppermute | solution.py:22
  24.8 1.5 %collective-permute-start.9 = (bf16[48,1024]{1,0:T(8,128)(2,1)S(1)}, bf16[48,1024]{1,0:T(8,128)(2,1)S(1)}, u32[]{:S(2)}, u32[]{:S(2)}) collective-permute-start(bf16[48,1024]{1,0:T(8,128)(2,1)S(1)} %collective-permute-done.4.refs_1_), channel_id=1, source_target_pairs={{0,1},{1,0},{2,3},{3,2},{4,5},{5,4},{6,7},{7,6},{8,9},{9,8},{10,11... | collective-permute-start | bytes 294920 | tf_op jit(solution)/shard_map/ppermute | solution.py:22
  26.3 10.4 %copy-start.2 = (f32[384]{0:T(512)S(1)}, f32[384]{0:T(512)}, u32[]{:S(2)}) copy-start(f32[384]{0:T(512)} %param.15) | copy-start | bytes 4612
  26.3 10.4 %copy-start.3 = (f32[384]{0:T(512)S(1)}, f32[384]{0:T(512)}, u32[]{:S(2)}) copy-start(f32[384]{0:T(512)} %param.16) | copy-start | bytes 4612
  27.1 5.8 %collective-permute-start.12 = (bf16[96,128]{1,0:T(8,128)(2,1)S(1)}, bf16[96,128]{1,0:T(8,128)(2,1)S(1)}, u32[]{:S(2)}, u32[]{:S(2)}) collective-permute-start(bf16[96,128]{1,0:T(8,128)(2,1)S(1)} %attend_far.1.own), channel_id=1, source_target_pairs={{0,12},{1,13},{2,14},{3,15},{4,8},{5,9},{6,10},{7,11},{8,4},{9,5},... | collective-permute-start | bytes 73736 | tf_op jit(solution)/shard_map/ppermute | solution.py:22
  29.4 4.8 %collective-permute-start.13 = (bf16[96,128]{1,0:T(8,128)(2,1)S(1)}, bf16[96,128]{1,0:T(8,128)(2,1)S(1)}, u32[]{:S(2)}, u32[]{:S(2)}) collective-permute-start(bf16[96,128]{1,0:T(8,128)(2,1)S(1)} %attend_far.1.own), channel_id=1, source_target_pairs={{0,8},{1,9},{2,10},{3,11},{4,12},{5,13},{6,14},{7,15},{8,0},{9,1},... | collective-permute-start | bytes 73736 | tf_op jit(solution)/shard_map/ppermute | solution.py:22
  30.5 3.9 %collective-permute-start.14 = (bf16[96,128]{1,0:T(8,128)(2,1)S(1)}, bf16[96,128]{1,0:T(8,128)(2,1)S(1)}, u32[]{:S(2)}, u32[]{:S(2)}) collective-permute-start(bf16[96,128]{1,0:T(8,128)(2,1)S(1)} %attend_far.1.own), channel_id=1, source_target_pairs={{0,4},{1,5},{2,6},{3,7},{4,0},{5,1},{6,2},{7,3},{8,12},{9,13},{10,... | collective-permute-start | bytes 73736 | tf_op jit(solution)/shard_map/ppermute | solution.py:22
  34.5 3.6 %collective-permute-start.15 = (bf16[96,128]{1,0:T(8,128)(2,1)S(1)}, bf16[96,128]{1,0:T(8,128)(2,1)S(1)}, u32[]{:S(2)}, u32[]{:S(2)}) collective-permute-start(bf16[96,128]{1,0:T(8,128)(2,1)S(1)} %gather.1.refs_0_), channel_id=1, source_target_pairs={{0,3},{1,2},{2,1},{3,0},{4,7},{5,6},{6,5},{7,4},{8,11},{9,10},{10,... | collective-permute-start | bytes 73736 | tf_op jit(solution)/shard_map/ppermute | solution.py:22
  34.5 3.9 %collective-permute-start.16 = (bf16[96,128]{1,0:T(8,128)(2,1)S(1)}, bf16[96,128]{1,0:T(8,128)(2,1)S(1)}, u32[]{:S(2)}, u32[]{:S(2)}) collective-permute-start(bf16[96,128]{1,0:T(8,128)(2,1)S(1)} %gather.1.refs_0_), channel_id=1, source_target_pairs={{0,2},{1,3},{2,0},{3,1},{4,6},{5,7},{6,4},{7,5},{8,10},{9,11},{10,... | collective-permute-start | bytes 73736 | tf_op jit(solution)/shard_map/ppermute | solution.py:22
  36.0 2.4 %collective-permute-start.17 = (bf16[96,128]{1,0:T(8,128)(2,1)S(1)}, bf16[96,128]{1,0:T(8,128)(2,1)S(1)}, u32[]{:S(2)}, u32[]{:S(2)}) collective-permute-start(bf16[96,128]{1,0:T(8,128)(2,1)S(1)} %gather.1.refs_0_), channel_id=1, source_target_pairs={{0,1},{1,0},{2,3},{3,2},{4,5},{5,4},{6,7},{7,6},{8,9},{9,8},{10,11... | collective-permute-start | bytes 73736 | tf_op jit(solution)/shard_map/ppermute | solution.py:22

commit v8 on v7

--- a/solution.py
+++ b/solution.py
@@ -415,18 +415,18 @@
             in_specs=[VMEM] * (1 + len(blocks) + len(carried) + len(last)),
             out_specs=VMEM if last else [VMEM] * 2,
             compiler_params=limit,
-            cost_estimate=pl.CostEstimate(flops=10**9, bytes_accessed=4 * 10**6, transcendentals=4 * 10**5),
+            cost_estimate=pl.CostEstimate(flops={'attend_near': 100000000, 'attend_middle': 100000000, 'attend_far': 100000000}[name], bytes_accessed=10**5, transcendentals=0),
             name=name,
         )(queried, *blocks, *carried, *last)
 
     carried = attended(near, [], [], "attend_near")
     beside = exchanged(held, 1)
-    middle = carried
-    carried = attended([held, beside], carried, [], "attend_middle")
-    passed = lax.optimization_barrier((far, middle))[0]
-    far = passed
-    far = far + [exchanged(block, 1) for block in far]
-    part = attended(far, carried, [streamed], "attend_far")
+    some = len(far) // 2
+    passed = far[:some] + lax.optimization_barrier((far[some:], carried))[0]
+    crossed = [exchanged(block, 1) for block in passed]
+    some = len(passed) // 2
+    carried = attended([held, beside] + passed[:some] + crossed[:some], carried, [], "attend_middle")
+    part = attended(passed[some:] + crossed[some:], carried, [streamed], "attend_far")
 
     others = [exchanged(part, step << 2) for step in (3, 2, 1)]
     patch = pl.pallas_call(

time: 43.3 us -> 43.1 us (level)
  waiting for transfers between devices: 10.2 us -> 9.44 us
  local copies, waits for them, and re-layouts: 0.27 us -> 0.9 us
  starting transfers between devices: 20.9 us -> 20.4 us
    ppermute x18, waiting for transfers between devices: 10.2 us -> 9.44 us  [exchanged(): return lax.ppermute(value, 'seq', pairs)]
    unnamed x13, local copies, waits for them, and re-layouts: 0.04 us -> 0.72 us
    ppermute x18, starting transfers between devices: 20.9 us -> 20.4 us  [exchanged(): return lax.ppermute(value, 'seq', pairs)]
  transfers between devices with their start and end apart: 18 -> 18, of which waited for: 9 -> 11; matrix products, arithmetic and copies ran while one was open for 6% -> 6% of each run, Pallas kernels for 4% -> 5%
where the time goes in v8:
time: 43.1 us; the launch traced here: 42.9 us
  starting transfers between devices  20.4 us (47%)
  waiting for transfers between devices  9.44 us (22%)
  Pallas kernels  9.31 us (22%)
  other arithmetic  2.57 us (6%)
  local copies, waits for them, and re-layouts  0.9 us (2%)
    ppermute x18, starting transfers between devices, exchanged(): return lax.ppermute(value, 'seq', pairs)  20.4 us
    ppermute x18, waiting for transfers between devices, exchanged(): return lax.ppermute(value, 'seq', pairs)  9.44 us
    pallas_call x1, Pallas kernels, shards(): pl.pallas_call(functools.partial(finish_kernel, frames, n, cols, [0] + or...  4.63 us
    pallas_call x3, Pallas kernels, attended(): pl.pallas_call(functools.partial(attend_kernel, depth, heads, not carried...  2.7 us
    concatenate x1, other arithmetic, widened(): whole = jnp.concatenate(blocks, axis=-1)  1.84 us
    pallas_call x1, Pallas kernels, shards(): pl.pallas_call(functools.partial(prepare_kernel, depth, heads), out_shape...  1.59 us
  transfers between devices with their start and end apart: 18, of which 11 were waited for; matrix products, arithmetic and copies ran while one was open for 6% of the time, Pallas kernels for 5%

profile of v8, /device:TPU:0, one launch (start us, length us, event | category | flops | bytes accessed | tf_op | source)
XLA Modules:
  0.0 42.9 jit_solution(17508250610074692274)
XLA Ops:
  0.0 1.6 %prepare.1 = (bf16[48,1024]{1,0:T(8,128)(2,1)S(1)}, bf16[48,1024]{1,0:T(8,128)(2,1)S(1)}, bf16[48,1024]{1,0:T(8,128)(2,1)S(1)}, bf16[48,1024]{1,0:T(8,128)(2,1)S...) custom-call(s32[1]{0:T(128)} %bitcast.index, ...), custom_call_target="tpu_custom_call" | custom-call | tf_op jit(solution)/shard_map/prepare/pallas_call | solution.py:351
  1.6 4.1 %collective-permute-start.1 = (bf16[48,1024]{1,0:T(8,128)(2,1)S(1)}, bf16[48,1024]{1,0:T(8,128)(2,1)S(1)}, u32[]{:S(2)}, u32[]{:S(2)}) collective-permute-start(bf16[48,1024]{1,0:T(8,128)(2,1)S(1)} %get-tuple-element.26), channel_id=1, source_target_pairs={{0,8},{1,9},{2,10},{3,11},{4,12},{5,13},{6,14},{7,15},{8,0},{9,1},... | collective-permute-start | bytes 294920 | tf_op jit(solution)/shard_map/ppermute | solution.py:22
  5.7 1.6 %collective-permute-start = (bf16[48,1664]{1,0:T(8,128)(2,1)S(1)}, bf16[48,1664]{1,0:T(8,128)(2,1)S(1)}, u32[]{:S(2)}, u32[]{:S(2)}) collective-permute-start(bf16[48,1664]{1,0:T(8,128)(2,1)S(1)} %pad_maximum_fusion.3), channel_id=1, source_target_pairs={{0,4},{1,5},{2,6},{3,7},{4,0},{5,1},{6,2},{7,3},{8,12},{9,13},{10,... | collective-permute-start | bytes 479240 | tf_op jit(solution)/shard_map/ppermute | solution.py:22
  7.4 1.8 %fusion.7 = bf16[3,4,4,16,1536]{4,3,2,1,0:T(8,128)(2,1)S(1)} fusion(bf16[3,3,3,16,384]{4,3,2,1,0:T(8,128)(2,1)} %param.14), kind=kLoop, calls=%fused_computation.13 | loop fusion | flops 23592960 | bytes 2691072 | tf_op jit(solution)/shard_map/concatenate | solution.py:310
  9.8 0.6 %copy-done = bf16[2560,64]{0,1:T(8,128)(2,1)S(1)} copy-done((bf16[2560,64]{0,1:T(8,128)(2,1)S(1)}, bf16[2560,64]{0,1:T(8,128)(2,1)}, u32[]{:S(2)}) %copy-start) | copy-done | bytes 327704
  10.5 0.3 stream.1.refs_5_
  10.8 1.9 %collective-permute-done = bf16[48,1664]{1,0:T(8,128)(2,1)S(1)} collective-permute-done((bf16[48,1664]{1,0:T(8,128)(2,1)S(1)}, bf16[48,1664]{1,0:T(8,128)(2,1)S(1)}, u32[]{:S(2)}, u32[]{:S(2)}) %collective-permute-start) | collective-permute-done | bytes 159776 | tf_op jit(solution)/shard_map/ppermute | solution.py:22
  12.7 1.8 %collective-permute-start.5 = (bf16[96,1024]{1,0:T(8,128)(2,1)S(1)}, bf16[96,1024]{1,0:T(8,128)(2,1)S(1)}, u32[]{:S(2)}, u32[]{:S(2)}) collective-permute-start(bf16[96,1024]{1,0:T(8,128)(2,1)S(1)} %pad_maximum_fusion.2), channel_id=1, source_target_pairs={{0,2},{1,3},{2,0},{3,1},{4,6},{5,7},{6,4},{7,5},{8,10},{9,11},{10,... | collective-permute-start | bytes 589832 | tf_op jit(solution)/shard_map/ppermute | solution.py:22
  14.6 2.0 %collective-permute-start.2 = (bf16[48,640]{1,0:T(8,128)(2,1)S(1)}, bf16[48,640]{1,0:T(8,128)(2,1)S(1)}, u32[]{:S(2)}, u32[]{:S(2)}) collective-permute-start(bf16[48,640]{1,0:T(8,128)(2,1)S(1)} %get-tuple-element.27), channel_id=1, source_target_pairs={{0,12},{1,13},{2,14},{3,15},{4,8},{5,9},{6,10},{7,11},{8,4},{9,5},... | collective-permute-start | bytes 184328 | tf_op jit(solution)/shard_map/ppermute | solution.py:22
  16.6 1.1 %collective-permute-start.3 = (bf16[48,640]{1,0:T(8,128)(2,1)S(1)}, bf16[48,640]{1,0:T(8,128)(2,1)S(1)}, u32[]{:S(2)}, u32[]{:S(2)}) collective-permute-start(bf16[48,640]{1,0:T(8,128)(2,1)S(1)} %get-tuple-element.28), channel_id=1, source_target_pairs={{0,8},{1,9},{2,10},{3,11},{4,12},{5,13},{6,14},{7,15},{8,0},{9,1},... | collective-permute-start | bytes 184328 | tf_op jit(solution)/shard_map/ppermute | solution.py:22
  17.7 0.5 %collective-permute-start.10 = (bf16[48,1024]{1,0:T(8,128)(2,1)S(1)}, bf16[48,1024]{1,0:T(8,128)(2,1)S(1)}, u32[]{:S(2)}, u32[]{:S(2)}) collective-permute-start(bf16[48,1024]{1,0:T(8,128)(2,1)S(1)} %collective-permute-done.1), channel_id=1, source_target_pairs={{0,2},{1,3},{2,0},{3,1},{4,6},{5,7},{6,4},{7,5},{8,10},{9,11},{10,... | collective-permute-start | bytes 294920 | tf_op jit(solution)/shard_map/ppermute | solution.py:22
  18.2 0.6 %collective-permute-done.5 = bf16[96,1024]{1,0:T(8,128)(2,1)S(1)} collective-permute-done((bf16[96,1024]{1,0:T(8,128)(2,1)S(1)}, bf16[96,1024]{1,0:T(8,128)(2,1)S(1)}, u32[]{:S(2)}, u32[]{:S(2)}) %collective-permute-start.5) | collective-permute-done | bytes 196640 | tf_op jit(solution)/shard_map/ppermute | solution.py:22
  19.0 2.5 %collective-permute-start.6 = (bf16[48,1024]{1,0:T(8,128)(2,1)S(1)}, bf16[48,1024]{1,0:T(8,128)(2,1)S(1)}, u32[]{:S(2)}, u32[]{:S(2)}) collective-permute-start(bf16[48,1024]{1,0:T(8,128)(2,1)S(1)} %collective-permute-done.4), channel_id=1, source_target_pairs={{0,2},{1,3},{2,0},{3,1},{4,6},{5,7},{6,4},{7,5},{8,10},{9,11},{10,... | collective-permute-start | bytes 294920 | tf_op jit(solution)/shard_map/ppermute | solution.py:22
  21.5 0.2 collective-permute-start.9
  21.7 0.4 collective-permute-done.3.refs_3_
  22.3 0.9 %attend_near.1 = (f32[5,192,128]{2,1,0:T(8,128)S(1)}, f32[5,192,256]{2,1,0:T(8,128)S(1)}) custom-call(bf16[192,640]{1,0:T(8,128)(2,1)S(1)} %collect.1.refs_0_, bf16[192,1024]{1,0:T(8,128)(2,1)S(1)} %pad_maximum_fusion.1.refs_1_, bf16[192,1024]{1,0:T(8,128)(2,1)S(1)} %collective-permute-done.7.refs_2_), custom_call_target="tpu_custom_call" | custom-call | flops 100000000 | bytes 100000 | tf_op jit(solution)/shard_map/attend_near/pallas_call | solution.py:412
  23.3 1.5 %collective-permute-done.6.refs_1_ = bf16[48,1024]{1,0:T(8,128)(2,1)S(1)} collective-permute-done((bf16[48,1024]{1,0:T(8,128)(2,1)S(1)}, bf16[48,1024]{1,0:T(8,128)(2,1)S(1)}, u32[]{:S(2)}, u32[]{:S(2)}) %collective-permute-start.6) | collective-permute-done | bytes 98336 | tf_op jit(solution)/shard_map/ppermute | solution.py:22
  24.9 1.0 %attend_middle.1 = (f32[5,192,128]{2,1,0:T(8,128)S(1)}, f32[5,192,256]{2,1,0:T(8,128)S(1)}) custom-call(bf16[192,640]{1,0:T(8,128)(2,1)S(1)} %collect.1.refs_0_, bf16[96,1024]{1,0:T(8,128)(2,1)S(1)} %constant_dynamic-update-slice_fusion.refs_1_, bf16[96,1024]{1,0:T(8,128)(2,1)S(1)} %collective-permute-done.9.refs_2_, ...), custom_call_target="tpu_custom_call" | custom-call | flops 100000000 | bytes 100000 | tf_op jit(solution)/shard_map/attend_middle/pallas_call | solution.py:412
  25.9 0.2 collective-permute-done.8.refs_2_
  26.1 0.8 %attend_far.1.own = bf16[96,128]{1,0:T(8,128)(2,1)S(1)} custom-call(bf16[192,640]{1,0:T(8,128)(2,1)S(1)} %collect.1.refs_0_, bf16[48,1024]{1,0:T(8,128)(2,1)S(1)} %collective-permute-done.6.refs_1_, bf16[48,1024]{1,0:T(8,128)(2,1)S(1)} %collective-permute-done.8.refs_2_, f32[5,192,128]{2,1,0:T(8,128)S(1)} %get-tuple-element.35.refs_3_, ...), custom_call_target="tpu_custom_call" | custom-call | flops 100000000 | bytes 100000 | tf_op jit(solution)/shard_map/attend_far/pallas_call | solution.py:412
  26.9 2.3 %collective-permute-start.12 = (bf16[96,128]{1,0:T(8,128)(2,1)S(1)}, bf16[96,128]{1,0:T(8,128)(2,1)S(1)}, u32[]{:S(2)}, u32[]{:S(2)}) collective-permute-start(bf16[96,128]{1,0:T(8,128)(2,1)S(1)} %attend_far.1.own), channel_id=1, source_target_pairs={{0,12},{1,13},{2,14},{3,15},{4,8},{5,9},{6,10},{7,11},{8,4},{9,5},... | collective-permute-start | bytes 73736 | tf_op jit(solution)/shard_map/ppermute | solution.py:22
  29.2 1.1 %collective-permute-start.13 = (bf16[96,128]{1,0:T(8,128)(2,1)S(1)}, bf16[96,128]{1,0:T(8,128)(2,1)S(1)}, u32[]{:S(2)}, u32[]{:S(2)}) collective-permute-start(bf16[96,128]{1,0:T(8,128)(2,1)S(1)} %attend_far.1.own), channel_id=1, source_target_pairs={{0,8},{1,9},{2,10},{3,11},{4,12},{5,13},{6,14},{7,15},{8,0},{9,1},... | collective-permute-start | bytes 73736 | tf_op jit(solution)/shard_map/ppermute | solution.py:22
  30.3 1.1 %collective-permute-start.14 = (bf16[96,128]{1,0:T(8,128)(2,1)S(1)}, bf16[96,128]{1,0:T(8,128)(2,1)S(1)}, u32[]{:S(2)}, u32[]{:S(2)}) collective-permute-start(bf16[96,128]{1,0:T(8,128)(2,1)S(1)} %attend_far.1.own), channel_id=1, source_target_pairs={{0,4},{1,5},{2,6},{3,7},{4,0},{5,1},{6,2},{7,3},{8,12},{9,13},{10,... | collective-permute-start | bytes 73736 | tf_op jit(solution)/shard_map/ppermute | solution.py:22
  31.4 1.3 %collective-permute-done.12.three = bf16[96,128]{1,0:T(8,128)(2,1)S(1)} collective-permute-done((bf16[96,128]{1,0:T(8,128)(2,1)S(1)}, bf16[96,128]{1,0:T(8,128)(2,1)S(1)}, u32[]{:S(2)}, u32[]{:S(2)}) %collective-permute-start.12) | collective-permute-done | bytes 24608 | tf_op jit(solution)/shard_map/ppermute | solution.py:22
  32.7 1.2 %collective-permute-done.13.two = bf16[96,128]{1,0:T(8,128)(2,1)S(1)} collective-permute-done((bf16[96,128]{1,0:T(8,128)(2,1)S(1)}, bf16[96,128]{1,0:T(8,128)(2,1)S(1)}, u32[]{:S(2)}, u32[]{:S(2)}) %collective-permute-start.13) | collective-permute-done | bytes 24608 | tf_op jit(solution)/shard_map/ppermute | solution.py:22
  33.9 0.3 collective-permute-done.14.one
  34.4 1.6 %collective-permute-start.16 = (bf16[96,128]{1,0:T(8,128)(2,1)S(1)}, bf16[96,128]{1,0:T(8,128)(2,1)S(1)}, u32[]{:S(2)}, u32[]{:S(2)}) collective-permute-start(bf16[96,128]{1,0:T(8,128)(2,1)S(1)} %gather.1.refs_0_), channel_id=1, source_target_pairs={{0,2},{1,3},{2,0},{3,1},{4,6},{5,7},{6,4},{7,5},{8,10},{9,11},{10,... | collective-permute-start | bytes 73736 | tf_op jit(solution)/shard_map/ppermute | solution.py:22
  35.9 0.3 collective-permute-start.17
  36.2 0.3 and_convert_fusion.refs_4_
  36.5 1.3 %collective-permute-done.15.refs_1_ = bf16[96,128]{1,0:T(8,128)(2,1)S(1)} collective-permute-done((bf16[96,128]{1,0:T(8,128)(2,1)S(1)}, bf16[96,128]{1,0:T(8,128)(2,1)S(1)}, u32[]{:S(2)}, u32[]{:S(2)}) %collective-permute-start.15) | collective-permute-done | bytes 24608 | tf_op jit(solution)/shard_map/ppermute | solution.py:22
  37.8 0.5 %collective-permute-done.16.refs_2_ = bf16[96,128]{1,0:T(8,128)(2,1)S(1)} collective-permute-done((bf16[96,128]{1,0:T(8,128)(2,1)S(1)}, bf16[96,128]{1,0:T(8,128)(2,1)S(1)}, u32[]{:S(2)}, u32[]{:S(2)}) %collective-permute-start.16) | collective-permute-done | bytes 24608 | tf_op jit(solution)/shard_map/ppermute | solution.py:22
  38.3 4.6 %finish.1 = bf16[3,2,32,384]{3,2,1,0:T(8,128)(2,1)} custom-call(s32[1]{0:T(128)} %bitcast.index, bf16[96,128]{1,0:T(8,128)(2,1)S(1)} %gather.1.refs_0_, bf16[96,128]{1,0:T(8,128)(2,1)S(1)} %collective-permute-done.15.refs_1_, bf16[96,128]{1,0:T(8,128)(2,1)S(1)} %collective-permute-done.16.refs_2_, bf16[96,128]{1,0:T(8,128)(2,1)S(1)} %collective-permute-done.17.refs_3_, ...), custom_call_target="tpu_custom_call" | custom-call | tf_op jit(solution)/shard_map/finish/pallas_call | solution.py:446
  (45 shorter events, 1.3 us)
Async XLA Ops:
  1.6 13.0 %collective-permute-start.1 = (bf16[48,1024]{1,0:T(8,128)(2,1)S(1)}, bf16[48,1024]{1,0:T(8,128)(2,1)S(1)}, u32[]{:S(2)}, u32[]{:S(2)}) collective-permute-start(bf16[48,1024]{1,0:T(8,128)(2,1)S(1)} %get-tuple-element.26), channel_id=1, source_target_pairs={{0,8},{1,9},{2,10},{3,11},{4,12},{5,13},{6,14},{7,15},{8,0},{9,1},... | collective-permute-start | bytes 294920 | tf_op jit(solution)/shard_map/ppermute | solution.py:22
  5.7 7.0 %collective-permute-start = (bf16[48,1664]{1,0:T(8,128)(2,1)S(1)}, bf16[48,1664]{1,0:T(8,128)(2,1)S(1)}, u32[]{:S(2)}, u32[]{:S(2)}) collective-permute-start(bf16[48,1664]{1,0:T(8,128)(2,1)S(1)} %pad_maximum_fusion.3), channel_id=1, source_target_pairs={{0,4},{1,5},{2,6},{3,7},{4,0},{5,1},{6,2},{7,3},{8,12},{9,13},{10,... | collective-permute-start | bytes 479240 | tf_op jit(solution)/shard_map/ppermute | solution.py:22
  7.4 11.6 %collective-permute-start.4 = (bf16[48,1024]{1,0:T(8,128)(2,1)S(1)}, bf16[48,1024]{1,0:T(8,128)(2,1)S(1)}, u32[]{:S(2)}, u32[]{:S(2)}) collective-permute-start(bf16[48,1024]{1,0:T(8,128)(2,1)S(1)} %get-tuple-element.29), channel_id=1, source_target_pairs={{0,12},{1,13},{2,14},{3,15},{4,8},{5,9},{6,10},{7,11},{8,4},{9,5},... | collective-permute-start | bytes 294920 | tf_op jit(solution)/shard_map/ppermute | solution.py:22
  9.4 1.0 %copy-start = (bf16[2560,64]{0,1:T(8,128)(2,1)S(1)}, bf16[2560,64]{0,1:T(8,128)(2,1)}, u32[]{:S(2)}) copy-start(bf16[2560,64]{0,1:T(8,128)(2,1)} %param.13) | copy-start | bytes 983044
  9.4 1.0 %copy-start.1 = (bf16[3,1,16,2560]{3,2,1,0:T(8,128)(2,1)S(1)}, bf16[3,1,16,2560]{3,2,1,0:T(8,128)(2,1)}, u32[]{:S(2)}) copy-start(bf16[3,1,16,2560]{3,2,1,0:T(8,128)(2,1)} %param.12) | copy-start | bytes 737284
  12.7 6.1 %collective-permute-start.5 = (bf16[96,1024]{1,0:T(8,128)(2,1)S(1)}, bf16[96,1024]{1,0:T(8,128)(2,1)S(1)}, u32[]{:S(2)}, u32[]{:S(2)}) collective-permute-start(bf16[96,1024]{1,0:T(8,128)(2,1)S(1)} %pad_maximum_fusion.2), channel_id=1, source_target_pairs={{0,2},{1,3},{2,0},{3,1},{4,6},{5,7},{6,4},{7,5},{8,10},{9,11},{10,... | collective-permute-start | bytes 589832 | tf_op jit(solution)/shard_map/ppermute | solution.py:22
  14.6 6.9 %collective-permute-start.2 = (bf16[48,640]{1,0:T(8,128)(2,1)S(1)}, bf16[48,640]{1,0:T(8,128)(2,1)S(1)}, u32[]{:S(2)}, u32[]{:S(2)}) collective-permute-start(bf16[48,640]{1,0:T(8,128)(2,1)S(1)} %get-tuple-element.27), channel_id=1, source_target_pairs={{0,12},{1,13},{2,14},{3,15},{4,8},{5,9},{6,10},{7,11},{8,4},{9,5},... | collective-permute-start | bytes 184328 | tf_op jit(solution)/shard_map/ppermute | solution.py:22
  16.6 5.5 %collective-permute-start.3 = (bf16[48,640]{1,0:T(8,128)(2,1)S(1)}, bf16[48,640]{1,0:T(8,128)(2,1)S(1)}, u32[]{:S(2)}, u32[]{:S(2)}) collective-permute-start(bf16[48,640]{1,0:T(8,128)(2,1)S(1)} %get-tuple-element.28), channel_id=1, source_target_pairs={{0,8},{1,9},{2,10},{3,11},{4,12},{5,13},{6,14},{7,15},{8,0},{9,1},... | collective-permute-start | bytes 184328 | tf_op jit(solution)/shard_map/ppermute | solution.py:22
  17.7 4.6 %collective-permute-start.10 = (bf16[48,1024]{1,0:T(8,128)(2,1)S(1)}, bf16[48,1024]{1,0:T(8,128)(2,1)S(1)}, u32[]{:S(2)}, u32[]{:S(2)}) collective-permute-start(bf16[48,1024]{1,0:T(8,128)(2,1)S(1)} %collective-permute-done.1), channel_id=1, source_target_pairs={{0,2},{1,3},{2,0},{3,1},{4,6},{5,7},{6,4},{7,5},{8,10},{9,11},{10,... | collective-permute-start | bytes 294920 | tf_op jit(solution)/shard_map/ppermute | solution.py:22
  18.9 3.5 %collective-permute-start.7 = (bf16[192,1024]{1,0:T(8,128)(2,1)S(1)}, bf16[192,1024]{1,0:T(8,128)(2,1)S(1)}, u32[]{:S(2)}, u32[]{:S(2)}) collective-permute-start(bf16[192,1024]{1,0:T(8,128)(2,1)S(1)} %pad_maximum_fusion.1.refs_1_), channel_id=1, source_target_pairs={{0,1},{1,0},{2,3},{3,2},{4,5},{5,4},{6,7},{7,6},{8,9},{9,8},{10,11... | collective-permute-start | bytes 1179656 | tf_op jit(solution)/shard_map/ppermute | solution.py:22
  19.0 5.9 %collective-permute-start.6 = (bf16[48,1024]{1,0:T(8,128)(2,1)S(1)}, bf16[48,1024]{1,0:T(8,128)(2,1)S(1)}, u32[]{:S(2)}, u32[]{:S(2)}) collective-permute-start(bf16[48,1024]{1,0:T(8,128)(2,1)S(1)} %collective-permute-done.4), channel_id=1, source_target_pairs={{0,2},{1,3},{2,0},{3,1},{4,6},{5,7},{6,4},{7,5},{8,10},{9,11},{10,... | collective-permute-start | bytes 294920 | tf_op jit(solution)/shard_map/ppermute | solution.py:22
  21.5 3.4 %collective-permute-start.9 = (bf16[96,1024]{1,0:T(8,128)(2,1)S(1)}, bf16[96,1024]{1,0:T(8,128)(2,1)S(1)}, u32[]{:S(2)}, u32[]{:S(2)}) collective-permute-start(bf16[96,1024]{1,0:T(8,128)(2,1)S(1)} %constant_dynamic-update-slice_fusion.refs_1_), channel_id=1, source_target_pairs={{0,1},{1,0},{2,3},{3,2},{4,5},{5,4},{6,7},{7,6},{8,9},{9,8},{10,11... | collective-permute-start | bytes 589832 | tf_op jit(solution)/shard_map/ppermute | solution.py:22
  22.1 16.1 %slice-start = ((s8[7962624]{0:T(1024)(128)(4,1)}), s8[4194304]{0:T(1024)(128)(4,1)S(1)}, s32[]{:S(2)}) async-start(s8[7962624]{0:T(1024)(128)(4,1)} %bitcast.8), calls=%async_computation | async-start | bytes 8388608
  22.1 16.2 %slice-start.1 = ((s8[7962624]{0:T(1024)(128)(4,1)}), s8[3768320]{0:T(1024)(128)(4,1)S(1)}, s32[]{:S(2)}) async-start(s8[7962624]{0:T(1024)(128)(4,1)} %bitcast.8), calls=%async_computation.1 | async-start | bytes 7536640
  22.3 2.5 %collective-permute-start.11 = (bf16[48,1024]{1,0:T(8,128)(2,1)S(1)}, bf16[48,1024]{1,0:T(8,128)(2,1)S(1)}, u32[]{:S(2)}, u32[]{:S(2)}) collective-permute-start(bf16[48,1024]{1,0:T(8,128)(2,1)S(1)} %collective-permute-done.10.refs_3_), channel_id=1, source_target_pairs={{0,1},{1,0},{2,3},{3,2},{4,5},{5,4},{6,7},{7,6},{8,9},{9,8},{10,11... | collective-permute-start | bytes 294920 | tf_op jit(solution)/shard_map/ppermute | solution.py:22
  23.3 13.2 %copy-start.2 = (f32[384]{0:T(512)S(1)}, f32[384]{0:T(512)}, u32[]{:S(2)}) copy-start(f32[384]{0:T(512)} %param.15) | copy-start | bytes 4612
  23.3 13.2 %copy-start.3 = (f32[384]{0:T(512)S(1)}, f32[384]{0:T(512)}, u32[]{:S(2)}) copy-start(f32[384]{0:T(512)} %param.16) | copy-start | bytes 4612
  24.8 1.3 %collective-permute-start.8 = (bf16[48,1024]{1,0:T(8,128)(2,1)S(1)}, bf16[48,1024]{1,0:T(8,128)(2,1)S(1)}, u32[]{:S(2)}, u32[]{:S(2)}) collective-permute-start(bf16[48,1024]{1,0:T(8,128)(2,1)S(1)} %collective-permute-done.6.refs_1_), channel_id=1, source_target_pairs={{0,1},{1,0},{2,3},{3,2},{4,5},{5,4},{6,7},{7,6},{8,9},{9,8},{10,11... | collective-permute-start | bytes 294920 | tf_op jit(solution)/shard_map/ppermute | solution.py:22
  26.9 5.8 %collective-permute-start.12 = (bf16[96,128]{1,0:T(8,128)(2,1)S(1)}, bf16[96,128]{1,0:T(8,128)(2,1)S(1)}, u32[]{:S(2)}, u32[]{:S(2)}) collective-permute-start(bf16[96,128]{1,0:T(8,128)(2,1)S(1)} %attend_far.1.own), channel_id=1, source_target_pairs={{0,12},{1,13},{2,14},{3,15},{4,8},{5,9},{6,10},{7,11},{8,4},{9,5},... | collective-permute-start | bytes 73736 | tf_op jit(solution)/shard_map/ppermute | solution.py:22
  29.2 4.7 %collective-permute-start.13 = (bf16[96,128]{1,0:T(8,128)(2,1)S(1)}, bf16[96,128]{1,0:T(8,128)(2,1)S(1)}, u32[]{:S(2)}, u32[]{:S(2)}) collective-permute-start(bf16[96,128]{1,0:T(8,128)(2,1)S(1)} %attend_far.1.own), channel_id=1, source_target_pairs={{0,8},{1,9},{2,10},{3,11},{4,12},{5,13},{6,14},{7,15},{8,0},{9,1},... | collective-permute-start | bytes 73736 | tf_op jit(solution)/shard_map/ppermute | solution.py:22
  30.3 3.9 %collective-permute-start.14 = (bf16[96,128]{1,0:T(8,128)(2,1)S(1)}, bf16[96,128]{1,0:T(8,128)(2,1)S(1)}, u32[]{:S(2)}, u32[]{:S(2)}) collective-permute-start(bf16[96,128]{1,0:T(8,128)(2,1)S(1)} %attend_far.1.own), channel_id=1, source_target_pairs={{0,4},{1,5},{2,6},{3,7},{4,0},{5,1},{6,2},{7,3},{8,12},{9,13},{10,... | collective-permute-start | bytes 73736 | tf_op jit(solution)/shard_map/ppermute | solution.py:22
  34.3 3.5 %collective-permute-start.15 = (bf16[96,128]{1,0:T(8,128)(2,1)S(1)}, bf16[96,128]{1,0:T(8,128)(2,1)S(1)}, u32[]{:S(2)}, u32[]{:S(2)}) collective-permute-start(bf16[96,128]{1,0:T(8,128)(2,1)S(1)} %gather.1.refs_0_), channel_id=1, source_target_pairs={{0,3},{1,2},{2,1},{3,0},{4,7},{5,6},{6,5},{7,4},{8,11},{9,10},{10,... | collective-permute-start | bytes 73736 | tf_op jit(solution)/shard_map/ppermute | solution.py:22
  34.4 3.9 %collective-permute-start.16 = (bf16[96,128]{1,0:T(8,128)(2,1)S(1)}, bf16[96,128]{1,0:T(8,128)(2,1)S(1)}, u32[]{:S(2)}, u32[]{:S(2)}) collective-permute-start(bf16[96,128]{1,0:T(8,128)(2,1)S(1)} %gather.1.refs_0_), channel_id=1, source_target_pairs={{0,2},{1,3},{2,0},{3,1},{4,6},{5,7},{6,4},{7,5},{8,10},{9,11},{10,... | collective-permute-start | bytes 73736 | tf_op jit(solution)/shard_map/ppermute | solution.py:22
  35.9 2.3 %collective-permute-start.17 = (bf16[96,128]{1,0:T(8,128)(2,1)S(1)}, bf16[96,128]{1,0:T(8,128)(2,1)S(1)}, u32[]{:S(2)}, u32[]{:S(2)}) collective-permute-start(bf16[96,128]{1,0:T(8,128)(2,1)S(1)} %gather.1.refs_0_), channel_id=1, source_target_pairs={{0,1},{1,0},{2,3},{3,2},{4,5},{5,4},{6,7},{7,6},{8,9},{9,8},{10,11... | collective-permute-start | bytes 73736 | tf_op jit(solution)/shard_map/ppermute | solution.py:22

commit v9 on v7

--- a/solution.py
+++ b/solution.py
@@ -415,7 +415,7 @@
             in_specs=[VMEM] * (1 + len(blocks) + len(carried) + len(last)),
             out_specs=VMEM if last else [VMEM] * 2,
             compiler_params=limit,
-            cost_estimate=pl.CostEstimate(flops=10**9, bytes_accessed=4 * 10**6, transcendentals=4 * 10**5),
+            cost_estimate=pl.CostEstimate(flops=10**8, bytes_accessed=10**5, transcendentals=0),
             name=name,
         )(queried, *blocks, *carried, *last)
 

time: 43.3 us -> 43.2 us (level)
  waiting for transfers between devices: 10.2 us -> 9.48 us
  local copies, waits for them, and re-layouts: 0.27 us -> 0.9 us
    ppermute x18, waiting for transfers between devices: 10.2 us -> 9.48 us  [exchanged(): return lax.ppermute(value, 'seq', pairs)]
    unnamed x13, local copies, waits for them, and re-layouts: 0.04 us -> 0.72 us
  transfers between devices with their start and end apart: 18 -> 18, of which waited for: 9 -> 11; matrix products, arithmetic and copies ran while one was open for 6% -> 6% of each run, Pallas kernels for 4% -> 4%
where the time goes in v9:
time: 43.2 us; the launch traced here: 43 us
  starting transfers between devices  20.9 us (48%)
  waiting for transfers between devices  9.48 us (22%)
  Pallas kernels  8.87 us (21%)
  other arithmetic  2.57 us (6%)
  local copies, waits for them, and re-layouts  0.9 us (2%)
    ppermute x18, starting transfers between devices, exchanged(): return lax.ppermute(value, 'seq', pairs)  20.9 us
    ppermute x18, waiting for transfers between devices, exchanged(): return lax.ppermute(value, 'seq', pairs)  9.48 us
    pallas_call x1, Pallas kernels, shards(): pl.pallas_call(functools.partial(finish_kernel, frames, n, cols, [0] + or...  4.64 us
    pallas_call x3, Pallas kernels, attended(): pl.pallas_call(functools.partial(attend_kernel, depth, heads, not carried...  2.26 us
    concatenate x1, other arithmetic, widened(): whole = jnp.concatenate(blocks, axis=-1)  1.84 us
    pallas_call x1, Pallas kernels, shards(): pl.pallas_call(functools.partial(prepare_kernel, depth, heads), out_shape...  1.59 us
  transfers between devices with their start and end apart: 18, of which 11 were waited for; matrix products, arithmetic and copies ran while one was open for 6% of the time, Pallas kernels for 4%

profile of v9, /device:TPU:0, one launch (start us, length us, event | category | flops | bytes accessed | tf_op | source)
XLA Modules:
  0.0 43.0 jit_solution(1743061375245741032)
XLA Ops:
  0.0 1.6 %prepare.1 = (bf16[48,1024]{1,0:T(8,128)(2,1)S(1)}, bf16[48,1024]{1,0:T(8,128)(2,1)S(1)}, bf16[48,1024]{1,0:T(8,128)(2,1)S(1)}, bf16[48,1024]{1,0:T(8,128)(2,1)S...) custom-call(s32[1]{0:T(128)} %bitcast.index, ...), custom_call_target="tpu_custom_call" | custom-call | tf_op jit(solution)/shard_map/prepare/pallas_call | solution.py:351
  1.6 4.1 %collective-permute-start.1 = (bf16[48,1024]{1,0:T(8,128)(2,1)S(1)}, bf16[48,1024]{1,0:T(8,128)(2,1)S(1)}, u32[]{:S(2)}, u32[]{:S(2)}) collective-permute-start(bf16[48,1024]{1,0:T(8,128)(2,1)S(1)} %get-tuple-element.27), channel_id=1, source_target_pairs={{0,8},{1,9},{2,10},{3,11},{4,12},{5,13},{6,14},{7,15},{8,0},{9,1},... | collective-permute-start | bytes 294920 | tf_op jit(solution)/shard_map/ppermute | solution.py:22
  5.7 1.6 %collective-permute-start = (bf16[48,1664]{1,0:T(8,128)(2,1)S(1)}, bf16[48,1664]{1,0:T(8,128)(2,1)S(1)}, u32[]{:S(2)}, u32[]{:S(2)}) collective-permute-start(bf16[48,1664]{1,0:T(8,128)(2,1)S(1)} %pad_maximum_fusion.3), channel_id=1, source_target_pairs={{0,4},{1,5},{2,6},{3,7},{4,0},{5,1},{6,2},{7,3},{8,12},{9,13},{10,... | collective-permute-start | bytes 479240 | tf_op jit(solution)/shard_map/ppermute | solution.py:22
  7.4 1.8 %fusion.7 = bf16[3,4,4,16,1536]{4,3,2,1,0:T(8,128)(2,1)S(1)} fusion(bf16[3,3,3,16,384]{4,3,2,1,0:T(8,128)(2,1)} %param.14), kind=kLoop, calls=%fused_computation.13 | loop fusion | flops 23592960 | bytes 2691072 | tf_op jit(solution)/shard_map/concatenate | solution.py:310
  9.8 0.6 %copy-done = bf16[2560,64]{0,1:T(8,128)(2,1)S(1)} copy-done((bf16[2560,64]{0,1:T(8,128)(2,1)S(1)}, bf16[2560,64]{0,1:T(8,128)(2,1)}, u32[]{:S(2)}) %copy-start) | copy-done | bytes 327704
  10.5 0.3 stream.1.refs_7_
  10.8 1.9 %collective-permute-done = bf16[48,1664]{1,0:T(8,128)(2,1)S(1)} collective-permute-done((bf16[48,1664]{1,0:T(8,128)(2,1)S(1)}, bf16[48,1664]{1,0:T(8,128)(2,1)S(1)}, u32[]{:S(2)}, u32[]{:S(2)}) %collective-permute-start) | collective-permute-done | bytes 159776 | tf_op jit(solution)/shard_map/ppermute | solution.py:22
  12.7 1.8 %collective-permute-start.6 = (bf16[96,1024]{1,0:T(8,128)(2,1)S(1)}, bf16[96,1024]{1,0:T(8,128)(2,1)S(1)}, u32[]{:S(2)}, u32[]{:S(2)}) collective-permute-start(bf16[96,1024]{1,0:T(8,128)(2,1)S(1)} %pad_maximum_fusion.2), channel_id=1, source_target_pairs={{0,2},{1,3},{2,0},{3,1},{4,6},{5,7},{6,4},{7,5},{8,10},{9,11},{10,... | collective-permute-start | bytes 589832 | tf_op jit(solution)/shard_map/ppermute | solution.py:22
  14.6 2.0 %collective-permute-start.2 = (bf16[48,640]{1,0:T(8,128)(2,1)S(1)}, bf16[48,640]{1,0:T(8,128)(2,1)S(1)}, u32[]{:S(2)}, u32[]{:S(2)}) collective-permute-start(bf16[48,640]{1,0:T(8,128)(2,1)S(1)} %get-tuple-element.28), channel_id=1, source_target_pairs={{0,12},{1,13},{2,14},{3,15},{4,8},{5,9},{6,10},{7,11},{8,4},{9,5},... | collective-permute-start | bytes 184328 | tf_op jit(solution)/shard_map/ppermute | solution.py:22
  16.6 1.1 %collective-permute-start.3 = (bf16[48,640]{1,0:T(8,128)(2,1)S(1)}, bf16[48,640]{1,0:T(8,128)(2,1)S(1)}, u32[]{:S(2)}, u32[]{:S(2)}) collective-permute-start(bf16[48,640]{1,0:T(8,128)(2,1)S(1)} %get-tuple-element.29), channel_id=1, source_target_pairs={{0,8},{1,9},{2,10},{3,11},{4,12},{5,13},{6,14},{7,15},{8,0},{9,1},... | collective-permute-start | bytes 184328 | tf_op jit(solution)/shard_map/ppermute | solution.py:22
  17.7 0.5 %collective-permute-start.4 = (bf16[48,1024]{1,0:T(8,128)(2,1)S(1)}, bf16[48,1024]{1,0:T(8,128)(2,1)S(1)}, u32[]{:S(2)}, u32[]{:S(2)}) collective-permute-start(bf16[48,1024]{1,0:T(8,128)(2,1)S(1)} %collective-permute-done.1), channel_id=1, source_target_pairs={{0,2},{1,3},{2,0},{3,1},{4,6},{5,7},{6,4},{7,5},{8,10},{9,11},{10,... | collective-permute-start | bytes 294920 | tf_op jit(solution)/shard_map/ppermute | solution.py:22
  18.2 0.6 %collective-permute-done.6 = bf16[96,1024]{1,0:T(8,128)(2,1)S(1)} collective-permute-done((bf16[96,1024]{1,0:T(8,128)(2,1)S(1)}, bf16[96,1024]{1,0:T(8,128)(2,1)S(1)}, u32[]{:S(2)}, u32[]{:S(2)}) %collective-permute-start.6) | collective-permute-done | bytes 196640 | tf_op jit(solution)/shard_map/ppermute | solution.py:22
  19.0 2.5 %collective-permute-start.7 = (bf16[48,1024]{1,0:T(8,128)(2,1)S(1)}, bf16[48,1024]{1,0:T(8,128)(2,1)S(1)}, u32[]{:S(2)}, u32[]{:S(2)}) collective-permute-start(bf16[48,1024]{1,0:T(8,128)(2,1)S(1)} %collective-permute-done.5), channel_id=1, source_target_pairs={{0,2},{1,3},{2,0},{3,1},{4,6},{5,7},{6,4},{7,5},{8,10},{9,11},{10,... | collective-permute-start | bytes 294920 | tf_op jit(solution)/shard_map/ppermute | solution.py:22
  21.5 0.2 collective-permute-start.11
  21.7 0.4 collective-permute-done.3.refs_3_
  22.1 0.9 %attend_near.1 = (f32[5,192,128]{2,1,0:T(8,128)S(1)}, f32[5,192,256]{2,1,0:T(8,128)S(1)}) custom-call(bf16[192,640]{1,0:T(8,128)(2,1)S(1)} %collect.1.refs_0_, bf16[192,1024]{1,0:T(8,128)(2,1)S(1)} %pad_maximum_fusion.1.refs_1_, bf16[192,1024]{1,0:T(8,128)(2,1)S(1)} %collective-permute-done.8.refs_2_), custom_call_target="tpu_custom_call" | custom-call | flops 100000000 | bytes 100000 | tf_op jit(solution)/shard_map/attend_near/pallas_call | solution.py:412
  23.1 1.7 %collective-permute-done.7.refs_2_ = bf16[48,1024]{1,0:T(8,128)(2,1)S(1)} collective-permute-done((bf16[48,1024]{1,0:T(8,128)(2,1)S(1)}, bf16[48,1024]{1,0:T(8,128)(2,1)S(1)}, u32[]{:S(2)}, u32[]{:S(2)}) %collective-permute-start.7) | collective-permute-done | bytes 98336 | tf_op jit(solution)/shard_map/ppermute | solution.py:22
  24.8 0.5 %collective-permute-start.9 = (bf16[48,1024]{1,0:T(8,128)(2,1)S(1)}, bf16[48,1024]{1,0:T(8,128)(2,1)S(1)}, u32[]{:S(2)}, u32[]{:S(2)}) collective-permute-start(bf16[48,1024]{1,0:T(8,128)(2,1)S(1)} %collective-permute-done.4.refs_1_), channel_id=1, source_target_pairs={{0,1},{1,0},{2,3},{3,2},{4,5},{5,4},{6,7},{7,6},{8,9},{9,8},{10,11... | collective-permute-start | bytes 294920 | tf_op jit(solution)/shard_map/ppermute | solution.py:22
  25.4 0.6 %attend_middle.1 = (f32[5,192,128]{2,1,0:T(8,128)S(1)}, f32[5,192,256]{2,1,0:T(8,128)S(1)}) custom-call(bf16[192,640]{1,0:T(8,128)(2,1)S(1)} %collect.1.refs_0_, bf16[96,1024]{1,0:T(8,128)(2,1)S(1)} %constant_dynamic-update-slice_fusion.refs_1_, bf16[96,1024]{1,0:T(8,128)(2,1)S(1)} %collective-permute-done.11.refs_2_, ...), custom_call_target="tpu_custom_call" | custom-call | flops 100000000 | bytes 100000 | tf_op jit(solution)/shard_map/attend_middle/pallas_call | solution.py:412
  26.3 0.7 %attend_far.1.own = bf16[96,128]{1,0:T(8,128)(2,1)S(1)} custom-call(bf16[192,640]{1,0:T(8,128)(2,1)S(1)} %collect.1.refs_0_, bf16[48,1024]{1,0:T(8,128)(2,1)S(1)} %collective-permute-done.4.refs_1_, bf16[48,1024]{1,0:T(8,128)(2,1)S(1)} %collective-permute-done.7.refs_2_, bf16[48,1024]{1,0:T(8,128)(2,1)S(1)} %collective-permute-done.9.refs_3_, ...), custom_call_target="tpu_custom_call" | custom-call | flops 100000000 | bytes 100000 | tf_op jit(solution)/shard_map/attend_far/pallas_call | solution.py:412
  27.0 2.3 %collective-permute-start.12 = (bf16[96,128]{1,0:T(8,128)(2,1)S(1)}, bf16[96,128]{1,0:T(8,128)(2,1)S(1)}, u32[]{:S(2)}, u32[]{:S(2)}) collective-permute-start(bf16[96,128]{1,0:T(8,128)(2,1)S(1)} %attend_far.1.own), channel_id=1, source_target_pairs={{0,12},{1,13},{2,14},{3,15},{4,8},{5,9},{6,10},{7,11},{8,4},{9,5},... | collective-permute-start | bytes 73736 | tf_op jit(solution)/shard_map/ppermute | solution.py:22
  29.3 1.1 %collective-permute-start.13 = (bf16[96,128]{1,0:T(8,128)(2,1)S(1)}, bf16[96,128]{1,0:T(8,128)(2,1)S(1)}, u32[]{:S(2)}, u32[]{:S(2)}) collective-permute-start(bf16[96,128]{1,0:T(8,128)(2,1)S(1)} %attend_far.1.own), channel_id=1, source_target_pairs={{0,8},{1,9},{2,10},{3,11},{4,12},{5,13},{6,14},{7,15},{8,0},{9,1},... | collective-permute-start | bytes 73736 | tf_op jit(solution)/shard_map/ppermute | solution.py:22
  30.4 1.1 %collective-permute-start.14 = (bf16[96,128]{1,0:T(8,128)(2,1)S(1)}, bf16[96,128]{1,0:T(8,128)(2,1)S(1)}, u32[]{:S(2)}, u32[]{:S(2)}) collective-permute-start(bf16[96,128]{1,0:T(8,128)(2,1)S(1)} %attend_far.1.own), channel_id=1, source_target_pairs={{0,4},{1,5},{2,6},{3,7},{4,0},{5,1},{6,2},{7,3},{8,12},{9,13},{10,... | collective-permute-start | bytes 73736 | tf_op jit(solution)/shard_map/ppermute | solution.py:22
  31.5 1.4 %collective-permute-done.12.three = bf16[96,128]{1,0:T(8,128)(2,1)S(1)} collective-permute-done((bf16[96,128]{1,0:T(8,128)(2,1)S(1)}, bf16[96,128]{1,0:T(8,128)(2,1)S(1)}, u32[]{:S(2)}, u32[]{:S(2)}) %collective-permute-start.12) | collective-permute-done | bytes 24608 | tf_op jit(solution)/shard_map/ppermute | solution.py:22
  32.9 1.1 %collective-permute-done.13.two = bf16[96,128]{1,0:T(8,128)(2,1)S(1)} collective-permute-done((bf16[96,128]{1,0:T(8,128)(2,1)S(1)}, bf16[96,128]{1,0:T(8,128)(2,1)S(1)}, u32[]{:S(2)}, u32[]{:S(2)}) %collective-permute-start.13) | collective-permute-done | bytes 24608 | tf_op jit(solution)/shard_map/ppermute | solution.py:22
  34.0 0.3 collective-permute-done.14.one
  34.5 1.5 %collective-permute-start.16 = (bf16[96,128]{1,0:T(8,128)(2,1)S(1)}, bf16[96,128]{1,0:T(8,128)(2,1)S(1)}, u32[]{:S(2)}, u32[]{:S(2)}) collective-permute-start(bf16[96,128]{1,0:T(8,128)(2,1)S(1)} %gather.1.refs_0_), channel_id=1, source_target_pairs={{0,2},{1,3},{2,0},{3,1},{4,6},{5,7},{6,4},{7,5},{8,10},{9,11},{10,... | collective-permute-start | bytes 73736 | tf_op jit(solution)/shard_map/ppermute | solution.py:22
  36.0 0.3 collective-permute-start.17
  36.3 0.3 and_convert_fusion.refs_4_
  36.6 1.3 %collective-permute-done.15.refs_1_ = bf16[96,128]{1,0:T(8,128)(2,1)S(1)} collective-permute-done((bf16[96,128]{1,0:T(8,128)(2,1)S(1)}, bf16[96,128]{1,0:T(8,128)(2,1)S(1)}, u32[]{:S(2)}, u32[]{:S(2)}) %collective-permute-start.15) | collective-permute-done | bytes 24608 | tf_op jit(solution)/shard_map/ppermute | solution.py:22
  37.9 0.5 %collective-permute-done.16.refs_2_ = bf16[96,128]{1,0:T(8,128)(2,1)S(1)} collective-permute-done((bf16[96,128]{1,0:T(8,128)(2,1)S(1)}, bf16[96,128]{1,0:T(8,128)(2,1)S(1)}, u32[]{:S(2)}, u32[]{:S(2)}) %collective-permute-start.16) | collective-permute-done | bytes 24608 | tf_op jit(solution)/shard_map/ppermute | solution.py:22
  38.4 4.6 %finish.1 = bf16[3,2,32,384]{3,2,1,0:T(8,128)(2,1)} custom-call(s32[1]{0:T(128)} %bitcast.index, bf16[96,128]{1,0:T(8,128)(2,1)S(1)} %gather.1.refs_0_, bf16[96,128]{1,0:T(8,128)(2,1)S(1)} %collective-permute-done.15.refs_1_, bf16[96,128]{1,0:T(8,128)(2,1)S(1)} %collective-permute-done.16.refs_2_, bf16[96,128]{1,0:T(8,128)(2,1)S(1)} %collective-permute-done.17.refs_3_, ...), custom_call_target="tpu_custom_call" | custom-call | tf_op jit(solution)/shard_map/finish/pallas_call | solution.py:446
  (45 shorter events, 1.4 us)
Async XLA Ops:
  1.6 13.0 %collective-permute-start.1 = (bf16[48,1024]{1,0:T(8,128)(2,1)S(1)}, bf16[48,1024]{1,0:T(8,128)(2,1)S(1)}, u32[]{:S(2)}, u32[]{:S(2)}) collective-permute-start(bf16[48,1024]{1,0:T(8,128)(2,1)S(1)} %get-tuple-element.27), channel_id=1, source_target_pairs={{0,8},{1,9},{2,10},{3,11},{4,12},{5,13},{6,14},{7,15},{8,0},{9,1},... | collective-permute-start | bytes 294920 | tf_op jit(solution)/shard_map/ppermute | solution.py:22
  5.7 7.0 %collective-permute-start = (bf16[48,1664]{1,0:T(8,128)(2,1)S(1)}, bf16[48,1664]{1,0:T(8,128)(2,1)S(1)}, u32[]{:S(2)}, u32[]{:S(2)}) collective-permute-start(bf16[48,1664]{1,0:T(8,128)(2,1)S(1)} %pad_maximum_fusion.3), channel_id=1, source_target_pairs={{0,4},{1,5},{2,6},{3,7},{4,0},{5,1},{6,2},{7,3},{8,12},{9,13},{10,... | collective-permute-start | bytes 479240 | tf_op jit(solution)/shard_map/ppermute | solution.py:22
  7.4 11.6 %collective-permute-start.5 = (bf16[48,1024]{1,0:T(8,128)(2,1)S(1)}, bf16[48,1024]{1,0:T(8,128)(2,1)S(1)}, u32[]{:S(2)}, u32[]{:S(2)}) collective-permute-start(bf16[48,1024]{1,0:T(8,128)(2,1)S(1)} %get-tuple-element.30), channel_id=1, source_target_pairs={{0,12},{1,13},{2,14},{3,15},{4,8},{5,9},{6,10},{7,11},{8,4},{9,5},... | collective-permute-start | bytes 294920 | tf_op jit(solution)/shard_map/ppermute | solution.py:22
  9.4 1.0 %copy-start = (bf16[2560,64]{0,1:T(8,128)(2,1)S(1)}, bf16[2560,64]{0,1:T(8,128)(2,1)}, u32[]{:S(2)}) copy-start(bf16[2560,64]{0,1:T(8,128)(2,1)} %param.13) | copy-start | bytes 983044
  9.4 1.0 %copy-start.1 = (bf16[3,1,16,2560]{3,2,1,0:T(8,128)(2,1)S(1)}, bf16[3,1,16,2560]{3,2,1,0:T(8,128)(2,1)}, u32[]{:S(2)}) copy-start(bf16[3,1,16,2560]{3,2,1,0:T(8,128)(2,1)} %param.12) | copy-start | bytes 737284
  12.7 6.1 %collective-permute-start.6 = (bf16[96,1024]{1,0:T(8,128)(2,1)S(1)}, bf16[96,1024]{1,0:T(8,128)(2,1)S(1)}, u32[]{:S(2)}, u32[]{:S(2)}) collective-permute-start(bf16[96,1024]{1,0:T(8,128)(2,1)S(1)} %pad_maximum_fusion.2), channel_id=1, source_target_pairs={{0,2},{1,3},{2,0},{3,1},{4,6},{5,7},{6,4},{7,5},{8,10},{9,11},{10,... | collective-permute-start | bytes 589832 | tf_op jit(solution)/shard_map/ppermute | solution.py:22
  14.6 6.9 %collective-permute-start.2 = (bf16[48,640]{1,0:T(8,128)(2,1)S(1)}, bf16[48,640]{1,0:T(8,128)(2,1)S(1)}, u32[]{:S(2)}, u32[]{:S(2)}) collective-permute-start(bf16[48,640]{1,0:T(8,128)(2,1)S(1)} %get-tuple-element.28), channel_id=1, source_target_pairs={{0,12},{1,13},{2,14},{3,15},{4,8},{5,9},{6,10},{7,11},{8,4},{9,5},... | collective-permute-start | bytes 184328 | tf_op jit(solution)/shard_map/ppermute | solution.py:22
  16.6 5.5 %collective-permute-start.3 = (bf16[48,640]{1,0:T(8,128)(2,1)S(1)}, bf16[48,640]{1,0:T(8,128)(2,1)S(1)}, u32[]{:S(2)}, u32[]{:S(2)}) collective-permute-start(bf16[48,640]{1,0:T(8,128)(2,1)S(1)} %get-tuple-element.29), channel_id=1, source_target_pairs={{0,8},{1,9},{2,10},{3,11},{4,12},{5,13},{6,14},{7,15},{8,0},{9,1},... | collective-permute-start | bytes 184328 | tf_op jit(solution)/shard_map/ppermute | solution.py:22
  17.7 5.4 %collective-permute-start.4 = (bf16[48,1024]{1,0:T(8,128)(2,1)S(1)}, bf16[48,1024]{1,0:T(8,128)(2,1)S(1)}, u32[]{:S(2)}, u32[]{:S(2)}) collective-permute-start(bf16[48,1024]{1,0:T(8,128)(2,1)S(1)} %collective-permute-done.1), channel_id=1, source_target_pairs={{0,2},{1,3},{2,0},{3,1},{4,6},{5,7},{6,4},{7,5},{8,10},{9,11},{10,... | collective-permute-start | bytes 294920 | tf_op jit(solution)/shard_map/ppermute | solution.py:22
  18.9 3.3 %collective-permute-start.8 = (bf16[192,1024]{1,0:T(8,128)(2,1)S(1)}, bf16[192,1024]{1,0:T(8,128)(2,1)S(1)}, u32[]{:S(2)}, u32[]{:S(2)}) collective-permute-start(bf16[192,1024]{1,0:T(8,128)(2,1)S(1)} %pad_maximum_fusion.1.refs_1_), channel_id=1, source_target_pairs={{0,1},{1,0},{2,3},{3,2},{4,5},{5,4},{6,7},{7,6},{8,9},{9,8},{10,11... | collective-permute-start | bytes 1179656 | tf_op jit(solution)/shard_map/ppermute | solution.py:22
  19.0 5.9 %collective-permute-start.7 = (bf16[48,1024]{1,0:T(8,128)(2,1)S(1)}, bf16[48,1024]{1,0:T(8,128)(2,1)S(1)}, u32[]{:S(2)}, u32[]{:S(2)}) collective-permute-start(bf16[48,1024]{1,0:T(8,128)(2,1)S(1)} %collective-permute-done.5), channel_id=1, source_target_pairs={{0,2},{1,3},{2,0},{3,1},{4,6},{5,7},{6,4},{7,5},{8,10},{9,11},{10,... | collective-permute-start | bytes 294920 | tf_op jit(solution)/shard_map/ppermute | solution.py:22
  21.5 3.9 %collective-permute-start.11 = (bf16[96,1024]{1,0:T(8,128)(2,1)S(1)}, bf16[96,1024]{1,0:T(8,128)(2,1)S(1)}, u32[]{:S(2)}, u32[]{:S(2)}) collective-permute-start(bf16[96,1024]{1,0:T(8,128)(2,1)S(1)} %constant_dynamic-update-slice_fusion.refs_1_), channel_id=1, source_target_pairs={{0,1},{1,0},{2,3},{3,2},{4,5},{5,4},{6,7},{7,6},{8,9},{9,8},{10,11... | collective-permute-start | bytes 589832 | tf_op jit(solution)/shard_map/ppermute | solution.py:22
  22.1 16.3 %slice-start = ((s8[7962624]{0:T(1024)(128)(4,1)}), s8[4194304]{0:T(1024)(128)(4,1)S(1)}, s32[]{:S(2)}) async-start(s8[7962624]{0:T(1024)(128)(4,1)} %bitcast.8), calls=%async_computation | async-start | bytes 8388608
  22.1 16.3 %slice-start.1 = ((s8[7962624]{0:T(1024)(128)(4,1)}), s8[3768320]{0:T(1024)(128)(4,1)S(1)}, s32[]{:S(2)}) async-start(s8[7962624]{0:T(1024)(128)(4,1)} %bitcast.8), calls=%async_computation.1 | async-start | bytes 7536640
  23.0 13.5 %copy-start.2 = (f32[384]{0:T(512)S(1)}, f32[384]{0:T(512)}, u32[]{:S(2)}) copy-start(f32[384]{0:T(512)} %param.15) | copy-start | bytes 4612
  23.1 13.5 %copy-start.3 = (f32[384]{0:T(512)S(1)}, f32[384]{0:T(512)}, u32[]{:S(2)}) copy-start(f32[384]{0:T(512)} %param.16) | copy-start | bytes 4612
  24.8 1.3 %collective-permute-start.10 = (bf16[48,1024]{1,0:T(8,128)(2,1)S(1)}, bf16[48,1024]{1,0:T(8,128)(2,1)S(1)}, u32[]{:S(2)}, u32[]{:S(2)}) collective-permute-start(bf16[48,1024]{1,0:T(8,128)(2,1)S(1)} %collective-permute-done.7.refs_2_), channel_id=1, source_target_pairs={{0,1},{1,0},{2,3},{3,2},{4,5},{5,4},{6,7},{7,6},{8,9},{9,8},{10,11... | collective-permute-start | bytes 294920 | tf_op jit(solution)/shard_map/ppermute | solution.py:22
  24.8 1.5 %collective-permute-start.9 = (bf16[48,1024]{1,0:T(8,128)(2,1)S(1)}, bf16[48,1024]{1,0:T(8,128)(2,1)S(1)}, u32[]{:S(2)}, u32[]{:S(2)}) collective-permute-start(bf16[48,1024]{1,0:T(8,128)(2,1)S(1)} %collective-permute-done.4.refs_1_), channel_id=1, source_target_pairs={{0,1},{1,0},{2,3},{3,2},{4,5},{5,4},{6,7},{7,6},{8,9},{9,8},{10,11... | collective-permute-start | bytes 294920 | tf_op jit(solution)/shard_map/ppermute | solution.py:22
  27.0 5.9 %collective-permute-start.12 = (bf16[96,128]{1,0:T(8,128)(2,1)S(1)}, bf16[96,128]{1,0:T(8,128)(2,1)S(1)}, u32[]{:S(2)}, u32[]{:S(2)}) collective-permute-start(bf16[96,128]{1,0:T(8,128)(2,1)S(1)} %attend_far.1.own), channel_id=1, source_target_pairs={{0,12},{1,13},{2,14},{3,15},{4,8},{5,9},{6,10},{7,11},{8,4},{9,5},... | collective-permute-start | bytes 73736 | tf_op jit(solution)/shard_map/ppermute | solution.py:22
  29.3 4.7 %collective-permute-start.13 = (bf16[96,128]{1,0:T(8,128)(2,1)S(1)}, bf16[96,128]{1,0:T(8,128)(2,1)S(1)}, u32[]{:S(2)}, u32[]{:S(2)}) collective-permute-start(bf16[96,128]{1,0:T(8,128)(2,1)S(1)} %attend_far.1.own), channel_id=1, source_target_pairs={{0,8},{1,9},{2,10},{3,11},{4,12},{5,13},{6,14},{7,15},{8,0},{9,1},... | collective-permute-start | bytes 73736 | tf_op jit(solution)/shard_map/ppermute | solution.py:22
  30.4 3.9 %collective-permute-start.14 = (bf16[96,128]{1,0:T(8,128)(2,1)S(1)}, bf16[96,128]{1,0:T(8,128)(2,1)S(1)}, u32[]{:S(2)}, u32[]{:S(2)}) collective-permute-start(bf16[96,128]{1,0:T(8,128)(2,1)S(1)} %attend_far.1.own), channel_id=1, source_target_pairs={{0,4},{1,5},{2,6},{3,7},{4,0},{5,1},{6,2},{7,3},{8,12},{9,13},{10,... | collective-permute-start | bytes 73736 | tf_op jit(solution)/shard_map/ppermute | solution.py:22
  34.4 3.5 %collective-permute-start.15 = (bf16[96,128]{1,0:T(8,128)(2,1)S(1)}, bf16[96,128]{1,0:T(8,128)(2,1)S(1)}, u32[]{:S(2)}, u32[]{:S(2)}) collective-permute-start(bf16[96,128]{1,0:T(8,128)(2,1)S(1)} %gather.1.refs_0_), channel_id=1, source_target_pairs={{0,3},{1,2},{2,1},{3,0},{4,7},{5,6},{6,5},{7,4},{8,11},{9,10},{10,... | collective-permute-start | bytes 73736 | tf_op jit(solution)/shard_map/ppermute | solution.py:22
  34.5 3.8 %collective-permute-start.16 = (bf16[96,128]{1,0:T(8,128)(2,1)S(1)}, bf16[96,128]{1,0:T(8,128)(2,1)S(1)}, u32[]{:S(2)}, u32[]{:S(2)}) collective-permute-start(bf16[96,128]{1,0:T(8,128)(2,1)S(1)} %gather.1.refs_0_), channel_id=1, source_target_pairs={{0,2},{1,3},{2,0},{3,1},{4,6},{5,7},{6,4},{7,5},{8,10},{9,11},{10,... | collective-permute-start | bytes 73736 | tf_op jit(solution)/shard_map/ppermute | solution.py:22
  36.0 2.3 %collective-permute-start.17 = (bf16[96,128]{1,0:T(8,128)(2,1)S(1)}, bf16[96,128]{1,0:T(8,128)(2,1)S(1)}, u32[]{:S(2)}, u32[]{:S(2)}) collective-permute-start(bf16[96,128]{1,0:T(8,128)(2,1)S(1)} %gather.1.refs_0_), channel_id=1, source_target_pairs={{0,1},{1,0},{2,3},{3,2},{4,5},{5,4},{6,7},{7,6},{8,9},{9,8},{10,11... | collective-permute-start | bytes 73736 | tf_op jit(solution)/shard_map/ppermute | solution.py:22

commit v10 on v9

--- a/solution.py
+++ b/solution.py
@@ -149,7 +149,7 @@
             mixed_out[head, :, wide:] = total
             continue
         mine = low if head % 2 == 0 else jnp.logical_not(low)
-        summed = summed + jnp.where(mine, weighed / total, 0.0)
+        summed = summed + jnp.where(mine, weighed * pl.reciprocal(total), 0.0)
     if not last:
         return
     summed = summed + pltpu.roll(summed, wide // 2, 1)

time: 43.2 us -> 43.2 us (level)
  no operation moved by 1% of the time
where the time goes in v10:
time: 43.2 us; the launch traced here: 43 us
  starting transfers between devices  20.9 us (48%)
  waiting for transfers between devices  9.48 us (22%)
  Pallas kernels  8.87 us (21%)
  other arithmetic  2.57 us (6%)
  local copies, waits for them, and re-layouts  0.9 us (2%)
    ppermute x18, starting transfers between devices, exchanged(): return lax.ppermute(value, 'seq', pairs)  20.9 us
    ppermute x18, waiting for transfers between devices, exchanged(): return lax.ppermute(value, 'seq', pairs)  9.48 us
    pallas_call x1, Pallas kernels, shards(): pl.pallas_call(functools.partial(finish_kernel, frames, n, cols, [0] + or...  4.64 us
    pallas_call x3, Pallas kernels, attended(): pl.pallas_call(functools.partial(attend_kernel, depth, heads, not carried...  2.26 us
    concatenate x1, other arithmetic, widened(): whole = jnp.concatenate(blocks, axis=-1)  1.84 us
    pallas_call x1, Pallas kernels, shards(): pl.pallas_call(functools.partial(prepare_kernel, depth, heads), out_shape...  1.59 us
  transfers between devices with their start and end apart: 18, of which 11 were waited for; matrix products, arithmetic and copies ran while one was open for 6% of the time, Pallas kernels for 4%

profile of v10, /device:TPU:0, one launch (start us, length us, event | category | flops | bytes accessed | tf_op | source)
XLA Modules:
  0.0 43.0 jit_solution(1743061375245741032)
XLA Ops:
  0.0 1.6 %prepare.1 = (bf16[48,1024]{1,0:T(8,128)(2,1)S(1)}, bf16[48,1024]{1,0:T(8,128)(2,1)S(1)}, bf16[48,1024]{1,0:T(8,128)(2,1)S(1)}, bf16[48,1024]{1,0:T(8,128)(2,1)S...) custom-call(s32[1]{0:T(128)} %bitcast.index, ...), custom_call_target="tpu_custom_call" | custom-call | tf_op jit(solution)/shard_map/prepare/pallas_call | solution.py:351
  1.6 4.1 %collective-permute-start.1 = (bf16[48,1024]{1,0:T(8,128)(2,1)S(1)}, bf16[48,1024]{1,0:T(8,128)(2,1)S(1)}, u32[]{:S(2)}, u32[]{:S(2)}) collective-permute-start(bf16[48,1024]{1,0:T(8,128)(2,1)S(1)} %get-tuple-element.27), channel_id=1, source_target_pairs={{0,8},{1,9},{2,10},{3,11},{4,12},{5,13},{6,14},{7,15},{8,0},{9,1},... | collective-permute-start | bytes 294920 | tf_op jit(solution)/shard_map/ppermute | solution.py:22
  5.7 1.6 %collective-permute-start = (bf16[48,1664]{1,0:T(8,128)(2,1)S(1)}, bf16[48,1664]{1,0:T(8,128)(2,1)S(1)}, u32[]{:S(2)}, u32[]{:S(2)}) collective-permute-start(bf16[48,1664]{1,0:T(8,128)(2,1)S(1)} %pad_maximum_fusion.3), channel_id=1, source_target_pairs={{0,4},{1,5},{2,6},{3,7},{4,0},{5,1},{6,2},{7,3},{8,12},{9,13},{10,... | collective-permute-start | bytes 479240 | tf_op jit(solution)/shard_map/ppermute | solution.py:22
  7.4 1.8 %fusion.7 = bf16[3,4,4,16,1536]{4,3,2,1,0:T(8,128)(2,1)S(1)} fusion(bf16[3,3,3,16,384]{4,3,2,1,0:T(8,128)(2,1)} %param.14), kind=kLoop, calls=%fused_computation.13 | loop fusion | flops 23592960 | bytes 2691072 | tf_op jit(solution)/shard_map/concatenate | solution.py:310
  9.8 0.6 %copy-done = bf16[2560,64]{0,1:T(8,128)(2,1)S(1)} copy-done((bf16[2560,64]{0,1:T(8,128)(2,1)S(1)}, bf16[2560,64]{0,1:T(8,128)(2,1)}, u32[]{:S(2)}) %copy-start) | copy-done | bytes 327704
  10.5 0.3 stream.1.refs_7_
  10.8 1.9 %collective-permute-done = bf16[48,1664]{1,0:T(8,128)(2,1)S(1)} collective-permute-done((bf16[48,1664]{1,0:T(8,128)(2,1)S(1)}, bf16[48,1664]{1,0:T(8,128)(2,1)S(1)}, u32[]{:S(2)}, u32[]{:S(2)}) %collective-permute-start) | collective-permute-done | bytes 159776 | tf_op jit(solution)/shard_map/ppermute | solution.py:22
  12.7 1.8 %collective-permute-start.6 = (bf16[96,1024]{1,0:T(8,128)(2,1)S(1)}, bf16[96,1024]{1,0:T(8,128)(2,1)S(1)}, u32[]{:S(2)}, u32[]{:S(2)}) collective-permute-start(bf16[96,1024]{1,0:T(8,128)(2,1)S(1)} %pad_maximum_fusion.2), channel_id=1, source_target_pairs={{0,2},{1,3},{2,0},{3,1},{4,6},{5,7},{6,4},{7,5},{8,10},{9,11},{10,... | collective-permute-start | bytes 589832 | tf_op jit(solution)/shard_map/ppermute | solution.py:22
  14.6 2.0 %collective-permute-start.2 = (bf16[48,640]{1,0:T(8,128)(2,1)S(1)}, bf16[48,640]{1,0:T(8,128)(2,1)S(1)}, u32[]{:S(2)}, u32[]{:S(2)}) collective-permute-start(bf16[48,640]{1,0:T(8,128)(2,1)S(1)} %get-tuple-element.28), channel_id=1, source_target_pairs={{0,12},{1,13},{2,14},{3,15},{4,8},{5,9},{6,10},{7,11},{8,4},{9,5},... | collective-permute-start | bytes 184328 | tf_op jit(solution)/shard_map/ppermute | solution.py:22
  16.6 1.1 %collective-permute-start.3 = (bf16[48,640]{1,0:T(8,128)(2,1)S(1)}, bf16[48,640]{1,0:T(8,128)(2,1)S(1)}, u32[]{:S(2)}, u32[]{:S(2)}) collective-permute-start(bf16[48,640]{1,0:T(8,128)(2,1)S(1)} %get-tuple-element.29), channel_id=1, source_target_pairs={{0,8},{1,9},{2,10},{3,11},{4,12},{5,13},{6,14},{7,15},{8,0},{9,1},... | collective-permute-start | bytes 184328 | tf_op jit(solution)/shard_map/ppermute | solution.py:22
  17.7 0.5 %collective-permute-start.4 = (bf16[48,1024]{1,0:T(8,128)(2,1)S(1)}, bf16[48,1024]{1,0:T(8,128)(2,1)S(1)}, u32[]{:S(2)}, u32[]{:S(2)}) collective-permute-start(bf16[48,1024]{1,0:T(8,128)(2,1)S(1)} %collective-permute-done.1), channel_id=1, source_target_pairs={{0,2},{1,3},{2,0},{3,1},{4,6},{5,7},{6,4},{7,5},{8,10},{9,11},{10,... | collective-permute-start | bytes 294920 | tf_op jit(solution)/shard_map/ppermute | solution.py:22
  18.2 0.6 %collective-permute-done.6 = bf16[96,1024]{1,0:T(8,128)(2,1)S(1)} collective-permute-done((bf16[96,1024]{1,0:T(8,128)(2,1)S(1)}, bf16[96,1024]{1,0:T(8,128)(2,1)S(1)}, u32[]{:S(2)}, u32[]{:S(2)}) %collective-permute-start.6) | collective-permute-done | bytes 196640 | tf_op jit(solution)/shard_map/ppermute | solution.py:22
  19.0 2.5 %collective-permute-start.7 = (bf16[48,1024]{1,0:T(8,128)(2,1)S(1)}, bf16[48,1024]{1,0:T(8,128)(2,1)S(1)}, u32[]{:S(2)}, u32[]{:S(2)}) collective-permute-start(bf16[48,1024]{1,0:T(8,128)(2,1)S(1)} %collective-permute-done.5), channel_id=1, source_target_pairs={{0,2},{1,3},{2,0},{3,1},{4,6},{5,7},{6,4},{7,5},{8,10},{9,11},{10,... | collective-permute-start | bytes 294920 | tf_op jit(solution)/shard_map/ppermute | solution.py:22
  21.5 0.2 collective-permute-start.11
  21.7 0.4 collective-permute-done.3.refs_3_
  22.1 0.9 %attend_near.1 = (f32[5,192,128]{2,1,0:T(8,128)S(1)}, f32[5,192,256]{2,1,0:T(8,128)S(1)}) custom-call(bf16[192,640]{1,0:T(8,128)(2,1)S(1)} %collect.1.refs_0_, bf16[192,1024]{1,0:T(8,128)(2,1)S(1)} %pad_maximum_fusion.1.refs_1_, bf16[192,1024]{1,0:T(8,128)(2,1)S(1)} %collective-permute-done.8.refs_2_), custom_call_target="tpu_custom_call" | custom-call | flops 100000000 | bytes 100000 | tf_op jit(solution)/shard_map/attend_near/pallas_call | solution.py:412
  23.1 1.7 %collective-permute-done.7.refs_2_ = bf16[48,1024]{1,0:T(8,128)(2,1)S(1)} collective-permute-done((bf16[48,1024]{1,0:T(8,128)(2,1)S(1)}, bf16[48,1024]{1,0:T(8,128)(2,1)S(1)}, u32[]{:S(2)}, u32[]{:S(2)}) %collective-permute-start.7) | collective-permute-done | bytes 98336 | tf_op jit(solution)/shard_map/ppermute | solution.py:22
  24.8 0.5 %collective-permute-start.9 = (bf16[48,1024]{1,0:T(8,128)(2,1)S(1)}, bf16[48,1024]{1,0:T(8,128)(2,1)S(1)}, u32[]{:S(2)}, u32[]{:S(2)}) collective-permute-start(bf16[48,1024]{1,0:T(8,128)(2,1)S(1)} %collective-permute-done.4.refs_1_), channel_id=1, source_target_pairs={{0,1},{1,0},{2,3},{3,2},{4,5},{5,4},{6,7},{7,6},{8,9},{9,8},{10,11... | collective-permute-start | bytes 294920 | tf_op jit(solution)/shard_map/ppermute | solution.py:22
  25.4 0.6 %attend_middle.1 = (f32[5,192,128]{2,1,0:T(8,128)S(1)}, f32[5,192,256]{2,1,0:T(8,128)S(1)}) custom-call(bf16[192,640]{1,0:T(8,128)(2,1)S(1)} %collect.1.refs_0_, bf16[96,1024]{1,0:T(8,128)(2,1)S(1)} %constant_dynamic-update-slice_fusion.refs_1_, bf16[96,1024]{1,0:T(8,128)(2,1)S(1)} %collective-permute-done.11.refs_2_, ...), custom_call_target="tpu_custom_call" | custom-call | flops 100000000 | bytes 100000 | tf_op jit(solution)/shard_map/attend_middle/pallas_call | solution.py:412
  26.3 0.7 %attend_far.1.own = bf16[96,128]{1,0:T(8,128)(2,1)S(1)} custom-call(bf16[192,640]{1,0:T(8,128)(2,1)S(1)} %collect.1.refs_0_, bf16[48,1024]{1,0:T(8,128)(2,1)S(1)} %collective-permute-done.4.refs_1_, bf16[48,1024]{1,0:T(8,128)(2,1)S(1)} %collective-permute-done.7.refs_2_, bf16[48,1024]{1,0:T(8,128)(2,1)S(1)} %collective-permute-done.9.refs_3_, ...), custom_call_target="tpu_custom_call" | custom-call | flops 100000000 | bytes 100000 | tf_op jit(solution)/shard_map/attend_far/pallas_call | solution.py:412
  27.0 2.3 %collective-permute-start.12 = (bf16[96,128]{1,0:T(8,128)(2,1)S(1)}, bf16[96,128]{1,0:T(8,128)(2,1)S(1)}, u32[]{:S(2)}, u32[]{:S(2)}) collective-permute-start(bf16[96,128]{1,0:T(8,128)(2,1)S(1)} %attend_far.1.own), channel_id=1, source_target_pairs={{0,12},{1,13},{2,14},{3,15},{4,8},{5,9},{6,10},{7,11},{8,4},{9,5},... | collective-permute-start | bytes 73736 | tf_op jit(solution)/shard_map/ppermute | solution.py:22
  29.3 1.1 %collective-permute-start.13 = (bf16[96,128]{1,0:T(8,128)(2,1)S(1)}, bf16[96,128]{1,0:T(8,128)(2,1)S(1)}, u32[]{:S(2)}, u32[]{:S(2)}) collective-permute-start(bf16[96,128]{1,0:T(8,128)(2,1)S(1)} %attend_far.1.own), channel_id=1, source_target_pairs={{0,8},{1,9},{2,10},{3,11},{4,12},{5,13},{6,14},{7,15},{8,0},{9,1},... | collective-permute-start | bytes 73736 | tf_op jit(solution)/shard_map/ppermute | solution.py:22
  30.4 1.1 %collective-permute-start.14 = (bf16[96,128]{1,0:T(8,128)(2,1)S(1)}, bf16[96,128]{1,0:T(8,128)(2,1)S(1)}, u32[]{:S(2)}, u32[]{:S(2)}) collective-permute-start(bf16[96,128]{1,0:T(8,128)(2,1)S(1)} %attend_far.1.own), channel_id=1, source_target_pairs={{0,4},{1,5},{2,6},{3,7},{4,0},{5,1},{6,2},{7,3},{8,12},{9,13},{10,... | collective-permute-start | bytes 73736 | tf_op jit(solution)/shard_map/ppermute | solution.py:22
  31.5 1.4 %collective-permute-done.12.three = bf16[96,128]{1,0:T(8,128)(2,1)S(1)} collective-permute-done((bf16[96,128]{1,0:T(8,128)(2,1)S(1)}, bf16[96,128]{1,0:T(8,128)(2,1)S(1)}, u32[]{:S(2)}, u32[]{:S(2)}) %collective-permute-start.12) | collective-permute-done | bytes 24608 | tf_op jit(solution)/shard_map/ppermute | solution.py:22
  32.9 1.1 %collective-permute-done.13.two = bf16[96,128]{1,0:T(8,128)(2,1)S(1)} collective-permute-done((bf16[96,128]{1,0:T(8,128)(2,1)S(1)}, bf16[96,128]{1,0:T(8,128)(2,1)S(1)}, u32[]{:S(2)}, u32[]{:S(2)}) %collective-permute-start.13) | collective-permute-done | bytes 24608 | tf_op jit(solution)/shard_map/ppermute | solution.py:22
  34.0 0.3 collective-permute-done.14.one
  34.5 1.5 %collective-permute-start.16 = (bf16[96,128]{1,0:T(8,128)(2,1)S(1)}, bf16[96,128]{1,0:T(8,128)(2,1)S(1)}, u32[]{:S(2)}, u32[]{:S(2)}) collective-permute-start(bf16[96,128]{1,0:T(8,128)(2,1)S(1)} %gather.1.refs_0_), channel_id=1, source_target_pairs={{0,2},{1,3},{2,0},{3,1},{4,6},{5,7},{6,4},{7,5},{8,10},{9,11},{10,... | collective-permute-start | bytes 73736 | tf_op jit(solution)/shard_map/ppermute | solution.py:22
  36.0 0.3 collective-permute-start.17
  36.3 0.3 and_convert_fusion.refs_4_
  36.6 1.3 %collective-permute-done.15.refs_1_ = bf16[96,128]{1,0:T(8,128)(2,1)S(1)} collective-permute-done((bf16[96,128]{1,0:T(8,128)(2,1)S(1)}, bf16[96,128]{1,0:T(8,128)(2,1)S(1)}, u32[]{:S(2)}, u32[]{:S(2)}) %collective-permute-start.15) | collective-permute-done | bytes 24608 | tf_op jit(solution)/shard_map/ppermute | solution.py:22
  37.9 0.5 %collective-permute-done.16.refs_2_ = bf16[96,128]{1,0:T(8,128)(2,1)S(1)} collective-permute-done((bf16[96,128]{1,0:T(8,128)(2,1)S(1)}, bf16[96,128]{1,0:T(8,128)(2,1)S(1)}, u32[]{:S(2)}, u32[]{:S(2)}) %collective-permute-start.16) | collective-permute-done | bytes 24608 | tf_op jit(solution)/shard_map/ppermute | solution.py:22
  38.4 4.6 %finish.1 = bf16[3,2,32,384]{3,2,1,0:T(8,128)(2,1)} custom-call(s32[1]{0:T(128)} %bitcast.index, bf16[96,128]{1,0:T(8,128)(2,1)S(1)} %gather.1.refs_0_, bf16[96,128]{1,0:T(8,128)(2,1)S(1)} %collective-permute-done.15.refs_1_, bf16[96,128]{1,0:T(8,128)(2,1)S(1)} %collective-permute-done.16.refs_2_, bf16[96,128]{1,0:T(8,128)(2,1)S(1)} %collective-permute-done.17.refs_3_, ...), custom_call_target="tpu_custom_call" | custom-call | tf_op jit(solution)/shard_map/finish/pallas_call | solution.py:446
  (45 shorter events, 1.4 us)
Async XLA Ops:
  1.6 13.0 %collective-permute-start.1 = (bf16[48,1024]{1,0:T(8,128)(2,1)S(1)}, bf16[48,1024]{1,0:T(8,128)(2,1)S(1)}, u32[]{:S(2)}, u32[]{:S(2)}) collective-permute-start(bf16[48,1024]{1,0:T(8,128)(2,1)S(1)} %get-tuple-element.27), channel_id=1, source_target_pairs={{0,8},{1,9},{2,10},{3,11},{4,12},{5,13},{6,14},{7,15},{8,0},{9,1},... | collective-permute-start | bytes 294920 | tf_op jit(solution)/shard_map/ppermute | solution.py:22
  5.7 7.0 %collective-permute-start = (bf16[48,1664]{1,0:T(8,128)(2,1)S(1)}, bf16[48,1664]{1,0:T(8,128)(2,1)S(1)}, u32[]{:S(2)}, u32[]{:S(2)}) collective-permute-start(bf16[48,1664]{1,0:T(8,128)(2,1)S(1)} %pad_maximum_fusion.3), channel_id=1, source_target_pairs={{0,4},{1,5},{2,6},{3,7},{4,0},{5,1},{6,2},{7,3},{8,12},{9,13},{10,... | collective-permute-start | bytes 479240 | tf_op jit(solution)/shard_map/ppermute | solution.py:22
  7.4 11.6 %collective-permute-start.5 = (bf16[48,1024]{1,0:T(8,128)(2,1)S(1)}, bf16[48,1024]{1,0:T(8,128)(2,1)S(1)}, u32[]{:S(2)}, u32[]{:S(2)}) collective-permute-start(bf16[48,1024]{1,0:T(8,128)(2,1)S(1)} %get-tuple-element.30), channel_id=1, source_target_pairs={{0,12},{1,13},{2,14},{3,15},{4,8},{5,9},{6,10},{7,11},{8,4},{9,5},... | collective-permute-start | bytes 294920 | tf_op jit(solution)/shard_map/ppermute | solution.py:22
  9.4 1.0 %copy-start = (bf16[2560,64]{0,1:T(8,128)(2,1)S(1)}, bf16[2560,64]{0,1:T(8,128)(2,1)}, u32[]{:S(2)}) copy-start(bf16[2560,64]{0,1:T(8,128)(2,1)} %param.13) | copy-start | bytes 983044
  9.4 1.0 %copy-start.1 = (bf16[3,1,16,2560]{3,2,1,0:T(8,128)(2,1)S(1)}, bf16[3,1,16,2560]{3,2,1,0:T(8,128)(2,1)}, u32[]{:S(2)}) copy-start(bf16[3,1,16,2560]{3,2,1,0:T(8,128)(2,1)} %param.12) | copy-start | bytes 737284
  12.7 6.1 %collective-permute-start.6 = (bf16[96,1024]{1,0:T(8,128)(2,1)S(1)}, bf16[96,1024]{1,0:T(8,128)(2,1)S(1)}, u32[]{:S(2)}, u32[]{:S(2)}) collective-permute-start(bf16[96,1024]{1,0:T(8,128)(2,1)S(1)} %pad_maximum_fusion.2), channel_id=1, source_target_pairs={{0,2},{1,3},{2,0},{3,1},{4,6},{5,7},{6,4},{7,5},{8,10},{9,11},{10,... | collective-permute-start | bytes 589832 | tf_op jit(solution)/shard_map/ppermute | solution.py:22
  14.6 6.9 %collective-permute-start.2 = (bf16[48,640]{1,0:T(8,128)(2,1)S(1)}, bf16[48,640]{1,0:T(8,128)(2,1)S(1)}, u32[]{:S(2)}, u32[]{:S(2)}) collective-permute-start(bf16[48,640]{1,0:T(8,128)(2,1)S(1)} %get-tuple-element.28), channel_id=1, source_target_pairs={{0,12},{1,13},{2,14},{3,15},{4,8},{5,9},{6,10},{7,11},{8,4},{9,5},... | collective-permute-start | bytes 184328 | tf_op jit(solution)/shard_map/ppermute | solution.py:22
  16.6 5.5 %collective-permute-start.3 = (bf16[48,640]{1,0:T(8,128)(2,1)S(1)}, bf16[48,640]{1,0:T(8,128)(2,1)S(1)}, u32[]{:S(2)}, u32[]{:S(2)}) collective-permute-start(bf16[48,640]{1,0:T(8,128)(2,1)S(1)} %get-tuple-element.29), channel_id=1, source_target_pairs={{0,8},{1,9},{2,10},{3,11},{4,12},{5,13},{6,14},{7,15},{8,0},{9,1},... | collective-permute-start | bytes 184328 | tf_op jit(solution)/shard_map/ppermute | solution.py:22
  17.7 5.4 %collective-permute-start.4 = (bf16[48,1024]{1,0:T(8,128)(2,1)S(1)}, bf16[48,1024]{1,0:T(8,128)(2,1)S(1)}, u32[]{:S(2)}, u32[]{:S(2)}) collective-permute-start(bf16[48,1024]{1,0:T(8,128)(2,1)S(1)} %collective-permute-done.1), channel_id=1, source_target_pairs={{0,2},{1,3},{2,0},{3,1},{4,6},{5,7},{6,4},{7,5},{8,10},{9,11},{10,... | collective-permute-start | bytes 294920 | tf_op jit(solution)/shard_map/ppermute | solution.py:22
  18.9 3.3 %collective-permute-start.8 = (bf16[192,1024]{1,0:T(8,128)(2,1)S(1)}, bf16[192,1024]{1,0:T(8,128)(2,1)S(1)}, u32[]{:S(2)}, u32[]{:S(2)}) collective-permute-start(bf16[192,1024]{1,0:T(8,128)(2,1)S(1)} %pad_maximum_fusion.1.refs_1_), channel_id=1, source_target_pairs={{0,1},{1,0},{2,3},{3,2},{4,5},{5,4},{6,7},{7,6},{8,9},{9,8},{10,11... | collective-permute-start | bytes 1179656 | tf_op jit(solution)/shard_map/ppermute | solution.py:22
  19.0 5.9 %collective-permute-start.7 = (bf16[48,1024]{1,0:T(8,128)(2,1)S(1)}, bf16[48,1024]{1,0:T(8,128)(2,1)S(1)}, u32[]{:S(2)}, u32[]{:S(2)}) collective-permute-start(bf16[48,1024]{1,0:T(8,128)(2,1)S(1)} %collective-permute-done.5), channel_id=1, source_target_pairs={{0,2},{1,3},{2,0},{3,1},{4,6},{5,7},{6,4},{7,5},{8,10},{9,11},{10,... | collective-permute-start | bytes 294920 | tf_op jit(solution)/shard_map/ppermute | solution.py:22
  21.5 3.9 %collective-permute-start.11 = (bf16[96,1024]{1,0:T(8,128)(2,1)S(1)}, bf16[96,1024]{1,0:T(8,128)(2,1)S(1)}, u32[]{:S(2)}, u32[]{:S(2)}) collective-permute-start(bf16[96,1024]{1,0:T(8,128)(2,1)S(1)} %constant_dynamic-update-slice_fusion.refs_1_), channel_id=1, source_target_pairs={{0,1},{1,0},{2,3},{3,2},{4,5},{5,4},{6,7},{7,6},{8,9},{9,8},{10,11... | collective-permute-start | bytes 589832 | tf_op jit(solution)/shard_map/ppermute | solution.py:22
  22.1 16.3 %slice-start = ((s8[7962624]{0:T(1024)(128)(4,1)}), s8[4194304]{0:T(1024)(128)(4,1)S(1)}, s32[]{:S(2)}) async-start(s8[7962624]{0:T(1024)(128)(4,1)} %bitcast.8), calls=%async_computation | async-start | bytes 8388608
  22.1 16.3 %slice-start.1 = ((s8[7962624]{0:T(1024)(128)(4,1)}), s8[3768320]{0:T(1024)(128)(4,1)S(1)}, s32[]{:S(2)}) async-start(s8[7962624]{0:T(1024)(128)(4,1)} %bitcast.8), calls=%async_computation.1 | async-start | bytes 7536640
  23.0 13.5 %copy-start.2 = (f32[384]{0:T(512)S(1)}, f32[384]{0:T(512)}, u32[]{:S(2)}) copy-start(f32[384]{0:T(512)} %param.15) | copy-start | bytes 4612
  23.1 13.5 %copy-start.3 = (f32[384]{0:T(512)S(1)}, f32[384]{0:T(512)}, u32[]{:S(2)}) copy-start(f32[384]{0:T(512)} %param.16) | copy-start | bytes 4612
  24.8 1.3 %collective-permute-start.10 = (bf16[48,1024]{1,0:T(8,128)(2,1)S(1)}, bf16[48,1024]{1,0:T(8,128)(2,1)S(1)}, u32[]{:S(2)}, u32[]{:S(2)}) collective-permute-start(bf16[48,1024]{1,0:T(8,128)(2,1)S(1)} %collective-permute-done.7.refs_2_), channel_id=1, source_target_pairs={{0,1},{1,0},{2,3},{3,2},{4,5},{5,4},{6,7},{7,6},{8,9},{9,8},{10,11... | collective-permute-start | bytes 294920 | tf_op jit(solution)/shard_map/ppermute | solution.py:22
  24.8 1.5 %collective-permute-start.9 = (bf16[48,1024]{1,0:T(8,128)(2,1)S(1)}, bf16[48,1024]{1,0:T(8,128)(2,1)S(1)}, u32[]{:S(2)}, u32[]{:S(2)}) collective-permute-start(bf16[48,1024]{1,0:T(8,128)(2,1)S(1)} %collective-permute-done.4.refs_1_), channel_id=1, source_target_pairs={{0,1},{1,0},{2,3},{3,2},{4,5},{5,4},{6,7},{7,6},{8,9},{9,8},{10,11... | collective-permute-start | bytes 294920 | tf_op jit(solution)/shard_map/ppermute | solution.py:22
  27.0 5.9 %collective-permute-start.12 = (bf16[96,128]{1,0:T(8,128)(2,1)S(1)}, bf16[96,128]{1,0:T(8,128)(2,1)S(1)}, u32[]{:S(2)}, u32[]{:S(2)}) collective-permute-start(bf16[96,128]{1,0:T(8,128)(2,1)S(1)} %attend_far.1.own), channel_id=1, source_target_pairs={{0,12},{1,13},{2,14},{3,15},{4,8},{5,9},{6,10},{7,11},{8,4},{9,5},... | collective-permute-start | bytes 73736 | tf_op jit(solution)/shard_map/ppermute | solution.py:22
  29.3 4.7 %collective-permute-start.13 = (bf16[96,128]{1,0:T(8,128)(2,1)S(1)}, bf16[96,128]{1,0:T(8,128)(2,1)S(1)}, u32[]{:S(2)}, u32[]{:S(2)}) collective-permute-start(bf16[96,128]{1,0:T(8,128)(2,1)S(1)} %attend_far.1.own), channel_id=1, source_target_pairs={{0,8},{1,9},{2,10},{3,11},{4,12},{5,13},{6,14},{7,15},{8,0},{9,1},... | collective-permute-start | bytes 73736 | tf_op jit(solution)/shard_map/ppermute | solution.py:22
  30.4 3.9 %collective-permute-start.14 = (bf16[96,128]{1,0:T(8,128)(2,1)S(1)}, bf16[96,128]{1,0:T(8,128)(2,1)S(1)}, u32[]{:S(2)}, u32[]{:S(2)}) collective-permute-start(bf16[96,128]{1,0:T(8,128)(2,1)S(1)} %attend_far.1.own), channel_id=1, source_target_pairs={{0,4},{1,5},{2,6},{3,7},{4,0},{5,1},{6,2},{7,3},{8,12},{9,13},{10,... | collective-permute-start | bytes 73736 | tf_op jit(solution)/shard_map/ppermute | solution.py:22
  34.4 3.5 %collective-permute-start.15 = (bf16[96,128]{1,0:T(8,128)(2,1)S(1)}, bf16[96,128]{1,0:T(8,128)(2,1)S(1)}, u32[]{:S(2)}, u32[]{:S(2)}) collective-permute-start(bf16[96,128]{1,0:T(8,128)(2,1)S(1)} %gather.1.refs_0_), channel_id=1, source_target_pairs={{0,3},{1,2},{2,1},{3,0},{4,7},{5,6},{6,5},{7,4},{8,11},{9,10},{10,... | collective-permute-start | bytes 73736 | tf_op jit(solution)/shard_map/ppermute | solution.py:22
  34.5 3.8 %collective-permute-start.16 = (bf16[96,128]{1,0:T(8,128)(2,1)S(1)}, bf16[96,128]{1,0:T(8,128)(2,1)S(1)}, u32[]{:S(2)}, u32[]{:S(2)}) collective-permute-start(bf16[96,128]{1,0:T(8,128)(2,1)S(1)} %gather.1.refs_0_), channel_id=1, source_target_pairs={{0,2},{1,3},{2,0},{3,1},{4,6},{5,7},{6,4},{7,5},{8,10},{9,11},{10,... | collective-permute-start | bytes 73736 | tf_op jit(solution)/shard_map/ppermute | solution.py:22
  36.0 2.3 %collective-permute-start.17 = (bf16[96,128]{1,0:T(8,128)(2,1)S(1)}, bf16[96,128]{1,0:T(8,128)(2,1)S(1)}, u32[]{:S(2)}, u32[]{:S(2)}) collective-permute-start(bf16[96,128]{1,0:T(8,128)(2,1)S(1)} %gather.1.refs_0_), channel_id=1, source_target_pairs={{0,1},{1,0},{2,3},{3,2},{4,5},{5,4},{6,7},{7,6},{8,9},{9,8},{10,11... | collective-permute-start | bytes 73736 | tf_op jit(solution)/shard_map/ppermute | solution.py:22
